TPU v7x, 512 devices: a whole 4x4x16 slice. The times are simulated.
512 devices in a mesh: orb: 64 (over x, z), comp: 8 (over y, core).
Axes of the slice: x: 4, y: 4, z: 16, core: 2. Of those that a mesh axis runs over, the one named last changes fastest.
Arguments:
- orbitals: float32 [64, 128, 128, 128], P('orb', 'comp'), may hold values from -24 to 24
- potential: float32 [128, 128, 128], P('comp'), may hold values from 0.1 to 4
- segments: int32 [2, 128, 128], P(None, 'comp'), may hold values from 0 to 128, as said below
Outputs:
- new_orbitals: float32 [64, 128, 128, 128], P('orb', 'comp')
- grad_rms: float32 [64], replicated
Inputs may be any that keep to these rules, and one draw needn't show every extreme that they name: segments[0] <= segments[1] in every column, and each region holds at least 64 cells.
All inputs are finite; a program needn't handle non-finite values.
Results may differ from a plain program's by a relative error of at most 0.00007.
Values sent between devices are 32-bit elements; how exact they have to be, the bound alone decides.
No kernel may reach another device: no remote copies, remote signals or barrier semaphores. Data moves between devices by JAX's collectives and lax.ppermute only.
A program may use at most 64 MiB of HBM per device.

v0:
```python
import math

import jax
import jax.numpy as jnp
from jax import lax
from jax.sharding import PartitionSpec as P

spacing = 0.4
descent = 0.02


def extended(array, sides, width):
    for axis, dim in sides:
        peers, length = (lax.axis_size(axis), array.shape[dim])
        up = [(i, (i + 1) % peers) for i in range(peers - 1)]
        down = [(j, i) for i, j in up]
        last = lax.slice_in_dim(array, length - width, length, axis=dim)
        first = lax.slice_in_dim(array, 0, width, axis=dim)
        before = lax.ppermute(last, axis, up)
        after = lax.ppermute(first, axis, down)
        array = jnp.concatenate([before, array, after], axis=dim)
    return array


def second_coefs_list():
    accuracy_order = 7
    coef_terms = []
    for offset in range(1, accuracy_order + 1):
        coef_terms.append(
            2.0
            * (-1) ** (offset + 1)
            * math.factorial(accuracy_order) ** 2
            / (
                offset
                * offset
                * math.factorial(accuracy_order - offset)
                * math.factorial(accuracy_order + offset)
            )
        )
    return [-2.0 * sum(coef_terms)] + coef_terms


def band_matrix(extent_len, stencil):
    positions = jnp.arange(extent_len, dtype=jnp.int32)
    distance = jnp.abs(positions[:, None] - positions[None, :])
    band_table = jnp.zeros((extent_len, extent_len), jnp.float32)
    for offset in range(len(stencil)):
        band_table = band_table + jnp.where(
            distance == offset, jnp.float32(stencil[offset]), jnp.float32(0.0)
        )
    return band_table


def region_mask(segments, depth_len):
    depth_index = jnp.arange(depth_len, dtype=jnp.int32)
    return (depth_index >= segments[0][..., None]) & (depth_index < segments[1][..., None])


def on_device(orbitals, potential, segments):
    stencil = second_coefs_list()
    halo_width = len(stencil) - 1
    padded = extended(orbitals, (("comp", 1),), halo_width)
    slab_cells = orbitals.shape[1]
    summed = stencil[0] * orbitals
    for offset in range(1, halo_width + 1):
        upper_part = padded[:, halo_width + offset : halo_width + offset + slab_cells]
        lower_part = padded[:, halo_width - offset : halo_width - offset + slab_cells]
        summed = summed + stencil[offset] * (upper_part + lower_part)
    band_y = band_matrix(orbitals.shape[2], stencil)
    band_z = band_matrix(orbitals.shape[3], stencil)
    summed = summed + jnp.einsum("oxyz,yv->oxvz", orbitals, band_y, precision=lax.Precision.HIGHEST)
    summed = summed + jnp.einsum("oxyz,zw->oxyw", orbitals, band_z, precision=lax.Precision.HIGHEST)
    images = -0.5 / spacing**2 * summed + potential[None] * orbitals
    moved_orbitals, moved_images = (
        lax.all_to_all(orbitals, "orb", split_axis=2, concat_axis=0, tiled=True),
        lax.all_to_all(images, "orb", split_axis=2, concat_axis=0, tiled=True),
    )
    orbital_count = moved_orbitals.shape[0]
    flat_orbitals = moved_orbitals.reshape(orbital_count, -1)
    flat_images = moved_images.reshape(orbital_count, -1)
    partial_correlation = jnp.dot(flat_orbitals, flat_images.T, precision=lax.Precision.HIGHEST)
    cell_count = flat_orbitals.shape[1] * lax.axis_size("orb") * lax.axis_size("comp")
    correlation = lax.psum(partial_correlation, ("orb", "comp")) / cell_count
    lagrange = 0.5 * (correlation + correlation.T)
    gradient = flat_images - jnp.dot(lagrange, flat_orbitals, precision=lax.Precision.HIGHEST)
    squares = lax.psum(jnp.sum(gradient * gradient, axis=1), ("orb", "comp"))
    mean_squares = squares / cell_count
    grad_rms = jnp.sqrt(mean_squares)
    returned = lax.all_to_all(
        gradient.reshape(moved_orbitals.shape), "orb", split_axis=0, concat_axis=2, tiled=True
    )
    inside = region_mask(segments, orbitals.shape[3])
    new_orbitals = jnp.where(inside[None], orbitals - descent * returned, jnp.float32(0.0))
    return (new_orbitals, grad_rms)


def solution(mesh):
    return jax.shard_map(
        on_device,
        mesh=mesh,
        in_specs=(P("orb", "comp", None, None), P("comp", None, None), P(None, "comp", None)),
        out_specs=(P("orb", "comp", None, None), P()),
        check_vma=False,
    )
```

profile of v0, /device:TPU:1, one launch (start us, length us, event | category | flops | bytes accessed | tf_op | source)
XLA Modules:
  0.0 379.8 jit_solution(723027397918070039)
XLA Ops:
  0.6 2.8 copy.29
  3.4 19.2 %all-to-all-start.1 = ((f32[1,16,128,128]{3,1,0,2:T(8,128)}), f32[1,16,128,128]{3,1,0,2:T(8,128)S(1)}, u32[]{:S(2)}, u32[]{:S(2)}) async-start(f32[1,16,128,128]{3,1,0,2:T(8,128)} %copy.29), calls=%async_computation.1 | async-start | bytes 2097152 | tf_op jit(solution)/shard_map/all_to_all | solution.py:75
  22.8 4.0 %collective-permute-start.1 = (f32[1,7,128,128]{3,2,1,0:T(8,128)S(1)}, f32[1,7,128,128]{3,2,1,0:T(8,128)S(1)}, u32[]{:S(2)}, u32[]{:S(2)}) collective-permute-start(f32[1,7,128,128]{3,2,1,0:T(8,128)S(1)} %get-tuple-element.3), channel_id=1, source_target_pairs={{0,1},{1,2},{2,3},{3,4},{4,5},{5,6},{6,7},{8,9},{9,10},{10,11},{11... | collective-permute-start | bytes 1376264 | tf_op jit(solution)/shard_map/ppermute | solution.py:19
  26.8 1.9 collective-permute-start
  28.7 1.1 convolution_bitcast_fusion.1
  29.8 2.4 collective-permute-done.1
  32.5 4.4 %collective-permute-done = f32[1,7,128,128]{3,2,1,0:T(8,128)S(1)} collective-permute-done((f32[1,7,128,128]{3,2,1,0:T(8,128)S(1)}, f32[1,7,128,128]{3,2,1,0:T(8,128)S(1)}, u32[]{:S(2)}, u32[]{:S(2)}) %collective-permute-start) | collective-permute-done | bytes 458784 | tf_op jit(solution)/shard_map/ppermute | solution.py:20
  37.0 2.1 fusion.2
  39.1 1.6 copy.26
  40.6 32.4 %all-to-all-done.1 = f32[1,16,128,128]{3,1,0,2:T(8,128)S(1)} async-done(((f32[1,16,128,128]{3,1,0,2:T(8,128)}), f32[1,16,128,128]{3,1,0,2:T(8,128)S(1)}, u32[]{:S(2)}, u32[]{:S(2)}) %all-to-all-start.1) | async-done | bytes 1048608 | tf_op jit(solution)/shard_map/all_to_all | solution.py:75
  73.0 10.1 %all-to-all-start = ((f32[1,16,128,128]{3,1,0,2:T(8,128)}), f32[1,16,128,128]{3,1,0,2:T(8,128)S(1)}, u32[]{:S(2)}, u32[]{:S(2)}) async-start(f32[1,16,128,128]{3,1,0,2:T(8,128)} %copy.26), calls=%async_computation | async-start | bytes 2097152 | tf_op jit(solution)/shard_map/all_to_all | solution.py:76
  83.1 1.5 copy.32
  84.6 3.1 reshape.64
  87.7 45.7 %all-to-all-done = f32[1,16,128,128]{3,1,0,2:T(8,128)S(1)} async-done(((f32[1,16,128,128]{3,1,0,2:T(8,128)}), f32[1,16,128,128]{3,1,0,2:T(8,128)S(1)}, u32[]{:S(2)}, u32[]{:S(2)}) %all-to-all-start) | async-done | bytes 1048608 | tf_op jit(solution)/shard_map/all_to_all | solution.py:76
  133.4 2.1 convolution_bitcast_fusion.2
  135.6 105.0 %psum.14 = f32[64,64]{0,1:T(8,128)S(1)} all-reduce(f32[64,64]{0,1:T(8,128)S(1)} %convolution_bitcast_fusion.2), channel_id=1, replica_groups=mesh['orb'=64,'comp'=8] {'orb','comp'}, use_global_device_ids=true, to_apply=%region_0.1 | all-reduce | flops 4096 | bytes 32768 | tf_op jit(solution)/shard_map/psum | solution.py:83
  240.7 1.5 copy.28
  242.2 2.2 reshape.61
  244.4 2.1 multiply_reduce_fusion
  246.5 3.1 reshape.65
  249.6 8.0 %all-to-all-start.2 = ((f32[64,16,2,128]{3,2,1,0:T(2,128)}), f32[64,16,2,128]{3,2,1,0:T(2,128)S(1)}, u32[]{:S(2)}, u32[]{:S(2)}) async-start(f32[64,16,2,128]{3,2,1,0:T(2,128)} %reshape.65), calls=%async_computation.2 | async-start | bytes 2097152 | tf_op jit(solution)/shard_map/all_to_all | solution.py:89
  257.7 118.9 %psum.15 = f32[64]{0:T(128)S(1)} all-reduce(f32[64]{0:T(128)S(1)} %get-tuple-element.8), channel_id=1, replica_groups=mesh['orb'=64,'comp'=8] {'orb','comp'}, use_global_device_ids=true, to_apply=%region_2.3 | all-reduce | flops 64 | bytes 512 | tf_op jit(solution)/shard_map/psum | solution.py:86
  377.1 0.6 multiply_bitcast_fusion
  378.3 1.5 subtract_select_fusion
  (18 shorter events, 1.5 us)
Async XLA Ops:
  3.4 19.3 %copy-start = (f32[1,16,128,128]{3,2,1,0:T(8,128)S(1)}, f32[1,16,128,128]{3,2,1,0:T(8,128)}, u32[]{:S(2)}) copy-start(f32[1,16,128,128]{3,2,1,0:T(8,128)} %param.3) | copy-start | bytes 3145732
  3.4 69.6 %all-to-all-start.1 = ((f32[1,16,128,128]{3,1,0,2:T(8,128)}), f32[1,16,128,128]{3,1,0,2:T(8,128)S(1)}, u32[]{:S(2)}, u32[]{:S(2)}) async-start(f32[1,16,128,128]{3,1,0,2:T(8,128)} %copy.29), calls=%async_computation.1 | async-start | bytes 2097152 | tf_op jit(solution)/shard_map/all_to_all | solution.py:75
  22.8 9.5 %collective-permute-start.1 = (f32[1,7,128,128]{3,2,1,0:T(8,128)S(1)}, f32[1,7,128,128]{3,2,1,0:T(8,128)S(1)}, u32[]{:S(2)}, u32[]{:S(2)}) collective-permute-start(f32[1,7,128,128]{3,2,1,0:T(8,128)S(1)} %get-tuple-element.3), channel_id=1, source_target_pairs={{0,1},{1,2},{2,3},{3,4},{4,5},{5,6},{6,7},{8,9},{9,10},{10,11},{11... | collective-permute-start | bytes 1376264 | tf_op jit(solution)/shard_map/ppermute | solution.py:19
  26.8 10.1 %collective-permute-start = (f32[1,7,128,128]{3,2,1,0:T(8,128)S(1)}, f32[1,7,128,128]{3,2,1,0:T(8,128)S(1)}, u32[]{:S(2)}, u32[]{:S(2)}) collective-permute-start(f32[1,7,128,128]{3,2,1,0:T(8,128)S(1)} %get-tuple-element.2), channel_id=1, source_target_pairs={{1,0},{2,1},{3,2},{4,3},{5,4},{6,5},{7,6},{9,8},{10,9},{11,10},{12... | collective-permute-start | bytes 1376264 | tf_op jit(solution)/shard_map/ppermute | solution.py:20
  32.3 4.7 %copy-start.3 = (f32[16,128,128]{2,1,0:T(8,128)S(1)}, f32[16,128,128]{2,1,0:T(8,128)}, u32[]{:S(2)}) copy-start(f32[16,128,128]{2,1,0:T(8,128)} %param.4) | copy-start | bytes 3145732
  73.0 60.4 %all-to-all-start = ((f32[1,16,128,128]{3,1,0,2:T(8,128)}), f32[1,16,128,128]{3,1,0,2:T(8,128)S(1)}, u32[]{:S(2)}, u32[]{:S(2)}) async-start(f32[1,16,128,128]{3,1,0,2:T(8,128)} %copy.26), calls=%async_computation | async-start | bytes 2097152 | tf_op jit(solution)/shard_map/all_to_all | solution.py:76
  242.2 2.2 copy-start.1
  249.6 8.0 %copy-start.2 = (s32[2,16,128]{2,1,0:T(8,128)S(1)}, s32[2,16,128]{2,1,0:T(8,128)}, u32[]{:S(2)}) copy-start(s32[2,16,128]{2,1,0:T(8,128)} %param.5) | copy-start | bytes 49156
  249.6 127.5 %all-to-all-start.2 = ((f32[64,16,2,128]{3,2,1,0:T(2,128)}), f32[64,16,2,128]{3,2,1,0:T(2,128)S(1)}, u32[]{:S(2)}, u32[]{:S(2)}) async-start(f32[64,16,2,128]{3,2,1,0:T(2,128)} %reshape.65), calls=%async_computation.2 | async-start | bytes 2097152 | tf_op jit(solution)/shard_map/all_to_all | solution.py:89
where the time goes:
time: 381 us; the launch traced here: 380 us
  blocking collectives  224 us (59%)
  waiting for transfers between devices  84.9 us (22%)
  starting transfers between devices  43.3 us (11%)
  local copies, waits for them, and re-layouts  16.7 us (4%)
  matrix products  7.45 us (2%)
    psum x1, blocking collectives, on_device(): squares = lax.psum(jnp.sum(gradient * gradient, axis=1), ('orb', 'comp'))  119 us
    psum x1, blocking collectives, on_device(): correlation = lax.psum(partial_correlation, ('orb', 'comp')) / cell_count  105 us
    all_to_all x1, waiting for transfers between devices, on_device(): lax.all_to_all(images, 'orb', split_axis=2, concat_axis=0, tiled=True)  45.7 us
    all_to_all x1, waiting for transfers between devices, on_device(): lax.all_to_all(orbitals, 'orb', split_axis=2, concat_axis=0, tiled=True)  32.4 us
    all_to_all x1, starting transfers between devices, on_device(): lax.all_to_all(orbitals, 'orb', split_axis=2, concat_axis=0, tiled=True)  19.2 us
    all_to_all x1, starting transfers between devices, on_device(): lax.all_to_all(images, 'orb', split_axis=2, concat_axis=0, tiled=True)  10.1 us
    all_to_all x1, starting transfers between devices, on_device(): lax.all_to_all(gradient.reshape(moved_orbitals.shape), 'orb', split_axis=...  8.01 us
  transfers between devices with their start and end apart: 5, of which 4 were waited for; matrix products, arithmetic and copies ran while one was open for 3% of the time, Pallas kernels for 0%

commit v1 on v0

v1 whole, which is shorter than its diff:
```python
import functools
import math

import jax
import jax.numpy as jnp
import numpy as np
from jax import lax
from jax.experimental import pallas as pl
from jax.experimental.pallas import tpu as pltpu
from jax.sharding import Mesh
from jax.sharding import PartitionSpec as P

spacing = 0.4
descent = 0.02
NX, NY, NZ, NORB = 128, 128, 128, 64
CELLS = NX * NY * NZ
KINETIC = -0.5 / spacing**2
REACH = 7
XG, YB, XL, ZB = 4, 8, 4, 32
ROWS, LANES = XG * YB, XL * ZB
HIGH = lax.Precision.HIGHEST
PARAMS = pltpu.CompilerParams(vmem_limit_bytes=48 * 1024 * 1024)
ORB, COMP = ("x", "z"), ("y", "core")


def second_coefs_list():
    terms = []
    for k in range(1, REACH + 1):
        terms.append(
            2.0
            * (-1) ** (k + 1)
            * math.factorial(REACH) ** 2
            / (k * k * math.factorial(REACH - k) * math.factorial(REACH + k))
        )
    return [-2.0 * sum(terms)] + terms


COEFS = [KINETIC * c for c in second_coefs_list()]


def lane_matrices(forward):
    own, near, far = (np.zeros((LANES, LANES)) for _ in range(3))
    halo = np.zeros((XG, LANES, LANES))

    def coef(k):
        return COEFS[k] if 1 <= k <= REACH else 0.0

    for x in range(XL):
        for z in range(ZB):
            out = x * ZB + z
            for zi in range(ZB):
                own[x * ZB + zi, out] += coef(zi - z if forward else z - zi)
            for xi in range(XL):
                step = xi - x if forward else x - xi
                own[xi * ZB + z, out] += coef(step)
                near[xi * ZB + z, out] += coef(step + XL)
                far[xi * ZB + z, out] += coef(step + 2 * XL)
            for xg in range(XG):
                for t in range(8):
                    k = ZB + t - z if forward else z + 8 - t
                    halo[xg, x * ZB + xg * 8 + t, out] += coef(k)
    first = np.concatenate([own, near], axis=0)
    second = np.stack([np.concatenate([far, halo[xg]], axis=0) for xg in range(XG)])
    return first.astype(np.float32), second.astype(np.float32)


def pack_kernel(src, dst):
    group = lax.broadcasted_iota(jnp.int32, (32, LANES), 1) // ZB
    for xg in range(XG):
        for part in range(4):
            rows = slice(part * 32, part * 32 + 32)
            layers = [src[xg * XL + x, rows, :] for x in range(XL)]
            for q in range(4):
                piece = layers[q]
                for x in range(XL):
                    if x != q:
                        moved = pltpu.roll(layers[x], ((x - q) * ZB) % LANES, 1)
                        piece = jnp.where(group == x, moved, piece)
                first = q * 16 + part * 4
                dst[first : first + 4, xg * YB : (xg + 1) * YB, :] = piece.reshape(4, YB, LANES)


def unpack_kernel(src, dst):
    group = lax.broadcasted_iota(jnp.int32, (YB, LANES), 1) // ZB
    for yb in range(16):
        for xg in range(XG):
            pieces = [src[pl.ds((q * 16 + yb) * (ROWS + 1) + xg * YB, YB), :] for q in range(4)]
            for x in range(XL):
                layer = pieces[x]
                for q in range(4):
                    if q != x:
                        moved = pltpu.roll(pieces[q], ((q - x) * ZB) % LANES, 1)
                        layer = jnp.where(group == q, moved, layer)
                dst[xg * XL + x, yb * YB : (yb + 1) * YB, :] = layer


def spread_kernel(src, phi, y_up_a, y_down_b, x_up, z_up, y_down_a, y_up_b, x_down, z_down):
    slot = (lax.broadcasted_iota(jnp.int32, (NORB, LANES), 1) % ZB) // 8
    for y in range(YB):
        up = down = jnp.zeros((NORB, LANES), jnp.float32)
        for xg in range(XG):
            r = xg * YB + y
            row = src[pl.ds(r, NORB, stride=ROWS), :]
            phi[r] = row
            g = xg % 2
            if xg < 2:
                x_up[r] = row
                if y < REACH:
                    y_up_a[g * REACH + y] = row
                if y >= 1:
                    y_down_a[g * REACH + y - 1] = row
            else:
                x_down[r - 2 * YB] = row
                if y < REACH:
                    y_up_b[g * REACH + y] = row
                if y >= 1:
                    y_down_b[g * REACH + y - 1] = row
            up = jnp.where(slot == xg, pltpu.roll(row, xg * 8, 1) if xg else row, up)
            down = jnp.where(slot == xg, pltpu.roll(row, (xg * 8 - 24) % LANES, 1) if xg != 3 else row, down)
        z_up[y] = up
        z_down[y] = down


def one_side(forward, xg, phi, y_halo, y_forward, x_halo, z_halo, half, first, second):
    def group(i):
        if 0 <= i < XG:
            return phi[i * YB : (i + 1) * YB].reshape(YB * NORB, LANES)
        j = i - XG if forward else i + 2
        return x_halo[j * YB : (j + 1) * YB].reshape(YB * NORB, LANES)

    step = 1 if forward else -1
    lhs = jnp.concatenate([group(xg), group(xg + step)], axis=1)
    total = jnp.dot(lhs, first[...], precision=HIGH, preferred_element_type=jnp.float32)
    lhs = jnp.concatenate([group(xg + 2 * step), z_halo[...].reshape(YB * NORB, LANES)], axis=1)
    total = total + jnp.dot(lhs, second[xg], precision=HIGH, preferred_element_type=jnp.float32)
    g = xg % 2
    result = []
    for y in range(YB):
        r = xg * YB + y
        value = total[y * NORB : (y + 1) * NORB] + half[r : r + 1, :] * phi[r]
        for k in range(1, REACH + 1):
            if y_forward:
                row = phi[r + k] if y + k < YB else y_halo[g * REACH + y + k - YB]
            else:
                row = phi[r - k] if y - k >= 0 else y_halo[g * REACH + REACH + y - k]
            value = value + COEFS[k] * row
        result.append(value)
    return result


def first_side_kernel(phi, y_a, y_b, x_halo, z_halo, half, first, second, out, partial):
    total = jnp.zeros((NORB, NORB), jnp.float32)
    for xg in range(XG):
        y_halo = y_a if xg < 2 else y_b
        values = one_side(True, xg, phi, y_halo, xg < 2, x_halo, z_halo, half, first, second)
        for y in range(YB):
            out[xg * YB + y] = values[y]
        left = jnp.concatenate([phi[xg * YB + y] for y in range(YB)], axis=1)
        right = jnp.concatenate(values, axis=1)
        total = total + lax.dot_general(
            left, right, (((1,), (1,)), ((), ())), precision=HIGH, preferred_element_type=jnp.float32
        )
    partial[...] = jnp.concatenate([total[: NORB // 2], total[NORB // 2 :]], axis=1)


def second_side_kernel(phi, y_a, y_b, x_halo, z_halo, half, first, second, before, out):
    for xg in range(XG):
        y_halo = y_a if xg < 2 else y_b
        values = one_side(False, xg, phi, y_halo, xg >= 2, x_halo, z_halo, half, first, second)
        for y in range(YB):
            r = xg * YB + y
            out[r] = before[r] + values[y]


def update_kernel(phi, images, lagrange, inside, out):
    lag = lagrange[...]
    squares = jnp.zeros((NORB, LANES), jnp.float32)
    for xg in range(XG):
        rows = [phi[xg * YB + y] for y in range(YB)]
        mixed = jnp.dot(lag, jnp.concatenate(rows, axis=1), precision=HIGH, preferred_element_type=jnp.float32)
        for y in range(YB):
            r = xg * YB + y
            gradient = images[r] - mixed[:, y * LANES : (y + 1) * LANES]
            squares = squares + gradient * gradient
            moved = rows[y] - descent * gradient
            out[pl.ds(r, NORB, stride=ROWS + 1), :] = jnp.where(inside[r : r + 1, :] > 0.0, moved, 0.0)
    ones = jnp.ones((8, LANES), jnp.float32)
    sums = lax.dot_general(ones, squares, (((1,), (1,)), ((), ())), precision=HIGH, preferred_element_type=jnp.float32)
    sums = jnp.concatenate([sums, jnp.zeros((8, LANES - NORB), jnp.float32)], axis=1)
    out[pl.ds(ROWS, NORB, stride=ROWS + 1), :] = jnp.broadcast_to(sums[0:1, :], (NORB, LANES))


def f32(*shape):
    return jax.ShapeDtypeStruct(shape, jnp.float32)


def call(kernel, out_shape, name, flops, nbytes):
    return pl.pallas_call(
        kernel,
        out_shape=out_shape,
        compiler_params=PARAMS,
        name=name,
        cost_estimate=pl.CostEstimate(flops=flops, bytes_accessed=nbytes, transcendentals=0),
    )


def copies_sum(value, axes):
    peers = math.prod(lax.axis_size(a) for a in axes)
    sent = jnp.broadcast_to(value[None], (peers,) + value.shape)
    return jnp.sum(lax.all_to_all(sent, axes, 0, 0, tiled=True), axis=0)


def shift(value, axes, count, up):
    pairs = [(i + 1, i) if up else (i, i + 1) for i in range(count - 1)]
    return lax.ppermute(value, axes, pairs)


def on_device(orbitals, potential, segments):
    mib = 1 << 20
    with jax.named_scope("pack"):
        pieces = call(pack_kernel, f32(NORB, ROWS, LANES), "pack", 1 << 20, 2 * mib)(orbitals[0])
    with jax.named_scope("transpose"):
        arrived = lax.all_to_all(pieces, ORB, 0, 0, tiled=True).reshape(NORB * ROWS, LANES)

    x_pos, z_pos = lax.axis_index("x"), lax.axis_index("z")
    with jax.named_scope("block_constants"):
        block = lax.dynamic_slice(potential, (0, z_pos * YB, x_pos * ZB), (16, YB, ZB))
        block = block.reshape(XG, XL, YB, ZB).transpose(0, 2, 1, 3).reshape(ROWS, LANES)
        half = 0.5 * (jnp.float32(3.0 * COEFS[0]) + block)
        ends = lax.dynamic_slice(segments, (0, 0, z_pos * YB), (2, 16, YB))
        ends = ends.reshape(2, XG, XL, YB).transpose(0, 1, 3, 2)
        ends = jnp.broadcast_to(ends[..., None], (2, XG, YB, XL, ZB)).reshape(2, ROWS, LANES)
        depth = x_pos * ZB + lax.broadcasted_iota(jnp.int32, (ROWS, LANES), 1) % ZB
        inside = ((depth >= ends[0]) & (depth < ends[1])).astype(jnp.float32)
    up_first, up_second = (jnp.asarray(m) for m in lane_matrices(True))
    down_first, down_second = (jnp.asarray(m) for m in lane_matrices(False))

    with jax.named_scope("spread"):
        y_shape, x_shape, z_shape = (f32(2 * REACH, NORB, LANES), f32(2 * YB, NORB, LANES), f32(YB, NORB, LANES))
        side = [y_shape, y_shape, x_shape, z_shape]
        phi, *sides = call(spread_kernel, [f32(ROWS, NORB, LANES)] + side + side, "spread", 1 << 20, 6 * mib)(arrived)
    y_up_a, y_down_b, x_up, z_up, y_down_a, y_up_b, x_down, z_down = sides
    with jax.named_scope("first_halo"):
        y_up_a = shift(y_up_a, "z", 16, True)
        y_down_b = shift(y_down_b, "z", 16, False)
        x_up = shift(x_up, COMP, 8, True)
        z_up = shift(z_up, "x", 4, True)
    with jax.named_scope("first_side"):
        one, partial = call(
            first_side_kernel, [f32(ROWS, NORB, LANES), f32(NORB // 2, 2 * NORB)], "first_side", 1 << 30, 5 * mib
        )(phi, y_up_a, y_down_b, x_up, z_up, half, up_first, up_second)
    with jax.named_scope("correlation_sum"):
        partial = copies_sum(partial, ("x", "y"))
        partial = copies_sum(partial, ("core",))
        partial = copies_sum(partial, ("z",))
        partial = jnp.concatenate([partial[:, :NORB], partial[:, NORB:]], axis=0)
        lagrange = (partial + partial.T) * jnp.float32(1.0 / CELLS)
    with jax.named_scope("second_halo"):
        y_down_a = shift(y_down_a, "z", 16, False)
        y_up_b = shift(y_up_b, "z", 16, True)
        x_down = shift(x_down, COMP, 8, False)
        z_down = shift(z_down, "x", 4, False)
    with jax.named_scope("second_side"):
        images = call(second_side_kernel, f32(ROWS, NORB, LANES), "second_side", 1 << 30, 6 * mib)(
            phi, y_down_a, y_up_b, x_down, z_down, half, down_first, down_second, one
        )
    with jax.named_scope("update"):
        sent = call(update_kernel, f32(NORB * (ROWS + 1), LANES), "update", 1 << 28, 3 * mib)(
            phi, images, lagrange, inside
        )
    with jax.named_scope("transpose_back"):
        back = lax.all_to_all(sent.reshape(NORB, ROWS + 1, 1, LANES), ORB, 0, 0, tiled=True)
    with jax.named_scope("rms"):
        slab = jnp.sum(back[:, ROWS, :, :], axis=0)
        squares = copies_sum(slab, COMP)[0, :NORB]
        grad_rms = jnp.sqrt(squares / CELLS)
    with jax.named_scope("unpack"):
        new = call(unpack_kernel, f32(16, NY, NZ), "unpack", 1 << 20, 2 * mib)(back.reshape(NORB * (ROWS + 1), LANES))
    return new[None], grad_rms


def solution(mesh):
    fine = Mesh(mesh.devices.reshape(4, 16, 4, 2), ("x", "z", "y", "core"))
    return jax.shard_map(
        on_device,
        mesh=fine,
        in_specs=(P(ORB, COMP, None, None), P(COMP, None, None), P(None, COMP, None)),
        out_specs=(P(ORB, COMP, None, None), P()),
        check_vma=False,
    )
```

time: 381 us -> 251 us (0.66)
  waiting for transfers between devices: 84.9 us -> 13.4 us
  blocking collectives: 224 us -> 154 us
  Pallas kernels: 0 us -> 16.9 us
  matrix products: 7.45 us -> 0 us
  starting transfers between devices: 43.3 us -> 36.8 us
  local copies, waits for them, and re-layouts: 16.7 us -> 22.8 us
    psum x2 -> x0, blocking collectives: 224 us -> none  [the longest x1 119 us: on_device(): squares = lax.psum(jnp.sum(gradient * gradient, axis=1), ('orb', 'comp'))]
    all_to_all x0 -> x4, blocking collectives: none -> 154 us  [the longest x1 69.2 us: on_device(): lax.all_to_all(pieces, ORB, 0, 0, tiled=True).reshape(NORB * ROWS, LANES)]
    all_to_all x3 -> x2, waiting for transfers between devices: 78.1 us -> 2.75 us  [copies_sum(): return jnp.sum(lax.all_to_all(sent, axes, 0, 0, tiled=True), axis=0)]
    all_to_all x3 -> x2, starting transfers between devices: 37.4 us -> 13.4 us  [copies_sum(): return jnp.sum(lax.all_to_all(sent, axes, 0, 0, tiled=True), axis=0)]
    ppermute x2 -> x8, starting transfers between devices: 5.97 us -> 23.4 us  [shift(): return lax.ppermute(value, axes, pairs)]
    pallas_call x0 -> x6, Pallas kernels: none -> 16.9 us  [the longest x1 6.26 us: on_device(): call(first_side_kernel, [f32(ROWS, NORB, LANES), f32(NORB // 2, 2 * NORB)...]
    unnamed x11 -> x40, local copies, waits for them, and re-layouts: 3.08 us -> 13.9 us
    reshape x3 -> x0, local copies, waits for them, and re-layouts: 8.33 us -> none  [the longest x1 3.09 us: on_device(): flat_orbitals = moved_orbitals.reshape(orbital_count, -1)]
  transfers between devices with their start and end apart: 5 -> 10, of which waited for: 4 -> 4; matrix products, arithmetic and copies ran while one was open for 3% -> 4% of each run, Pallas kernels for 0% -> 3%
where the time goes in v1:
time: 251 us; the launch traced here: 250 us
  blocking collectives  154 us (61%)
  starting transfers between devices  36.8 us (15%)
  local copies, waits for them, and re-layouts  22.8 us (9%)
  Pallas kernels  16.9 us (7%)
  waiting for transfers between devices  13.4 us (5%)
  other arithmetic  5.13 us (2%)
    all_to_all x1, blocking collectives, on_device(): lax.all_to_all(pieces, ORB, 0, 0, tiled=True).reshape(NORB * ROWS, LANES)  69.2 us
    all_to_all x1, blocking collectives, on_device(): lax.all_to_all(sent.reshape(NORB, ROWS + 1, 1, LANES), ORB, 0, 0, tiled=T...  65 us
    ppermute x8, starting transfers between devices, shift(): return lax.ppermute(value, axes, pairs)  23.4 us
    all_to_all x2, blocking collectives, copies_sum(): return jnp.sum(lax.all_to_all(sent, axes, 0, 0, tiled=True), axis=0)  19.6 us
    unnamed x40, local copies, waits for them, and re-layouts  13.9 us
    all_to_all x2, starting transfers between devices, copies_sum(): return jnp.sum(lax.all_to_all(sent, axes, 0, 0, tiled=True), axis=0)  13.4 us
    ppermute x8, waiting for transfers between devices, shift(): return lax.ppermute(value, axes, pairs)  10.7 us
    pallas_call x1, Pallas kernels, on_device(): call(first_side_kernel, [f32(ROWS, NORB, LANES), f32(NORB // 2, 2 * NORB)...  6.26 us
  transfers between devices with their start and end apart: 10, of which 4 were waited for; matrix products, arithmetic and copies ran while one was open for 4% of the time, Pallas kernels for 3%

profile of v1, /device:TPU:1, one launch (start us, length us, event | category | flops | bytes accessed | tf_op | source)
XLA Modules:
  0.0 249.7 jit_solution(15033516825523975189)
XLA Ops:
  0.7 1.2 copy-done.1
  2.8 69.2 %all_to_all.30 = f32[64,32,128]{2,1,0:T(8,128)S(1)} all-to-all(f32[64,32,128]{2,1,0:T(8,128)S(1)} %pack.1), channel_id=1, replica_groups=mesh['x'=4,'z'=16,'y'=4,'core'=2] {'x','z'}, dimensions={0} | all-to-all | bytes 2097152 | tf_op jit(solution)/shard_map/transpose/all_to_all | solution.py:223
  72.0 1.9 spread.1
  74.6 6.4 %collective-permute-start.6 = (f32[16,64,128]{2,1,0:T(8,128)S(1)}, f32[16,64,128]{2,1,0:T(8,128)S(1)}, u32[]{:S(2)}, u32[]{:S(2)}) collective-permute-start(f32[16,64,128]{2,1,0:T(8,128)S(1)} %get-tuple-element.20), channel_id=1, source_target_pairs={{1,0},{2,1},{3,2},{4,3},{5,4},{6,5},{7,6},{9,8},{10,9},{11,10},{12... | collective-permute-start | bytes 1572872 | tf_op jit(solution)/shard_map/first_halo/ppermute | solution.py:215
  81.0 1.3 collective-permute-start.4
  82.3 4.8 %collective-permute-start.5 = (f32[14,64,128]{2,1,0:T(8,128)S(1)}, f32[14,64,128]{2,1,0:T(8,128)}, u32[]{:S(2)}, u32[]{:S(2)}) collective-permute-start(f32[14,64,128]{2,1,0:T(8,128)S(1)} %get-tuple-element.19), channel_id=1, source_target_pairs={{0,8},{8,16},{16,24},{24,32},{32,40},{40,48},{48,56},{56,64},{64,7... | collective-permute-start | bytes 1376264 | tf_op jit(solution)/shard_map/first_halo/ppermute | solution.py:215
  87.1 1.3 collective-permute-start.7
  90.9 6.4 %collective-permute-done.7.z_halo = f32[8,64,128]{2,1,0:T(8,128)} collective-permute-done((f32[8,64,128]{2,1,0:T(8,128)}, f32[8,64,128]{2,1,0:T(8,128)}, u32[]{:S(2)}, u32[]{:S(2)}) %collective-permute-start.7) | collective-permute-done | bytes 262176 | tf_op jit(solution)/shard_map/first_halo/ppermute | solution.py:215
  102.9 6.3 %first_side.1 = (f32[32,64,128]{2,1,0:T(8,128)S(1)}, f32[32,128]{1,0:T(8,128)S(1)}) custom-call(f32[32,64,128]{2,1,0:T(8,128)S(1)} %get-tuple-element.13.phi, f32[14,64,128]{2,1,0:T(8,128)S(1)} %copy-done.15, f32[14,64,128]{2,1,0:T(8,128)} %collective-permute-done.5.y_b, f32[16,64,128]{2,1,0:T(8,128)S(1)} %copy-done.13, ...), custom_call_target="tpu_custom_call" | custom-call | flops 1073741824 | bytes 5242880 | tf_op jit(solution)/shard_map/first_side/first_side/pallas_call | solution.py:249
  109.2 13.4 %all_to_all.31 = f32[16,32,128]{2,1,0:T(8,128)S(1)} all-to-all(f32[16,32,128]{2,1,0:T(8,128)S(1)} %broadcast_in_dim.18), channel_id=1, replica_groups=mesh['x'=4,'z'=16,'y'=4,'core'=2] {'x','y'}, dimensions={0} | all-to-all | bytes 524288 | tf_op jit(solution)/shard_map/correlation_sum/all_to_all | solution.py:210
  122.6 6.3 %all_to_all.32 = f32[2,32,128]{2,1,0:T(8,128)S(1)} all-to-all(f32[2,32,128]{2,1,0:T(8,128)S(1)} %broadcast_in_dim.19), channel_id=1, replica_groups=mesh['x'=4,'z'=16,'y'=4,'core'=2] {'core'}, dimensions={0} | all-to-all | bytes 65536 | tf_op jit(solution)/shard_map/correlation_sum/all_to_all | solution.py:210
  129.6 5.5 %all-to-all-start.3 = ((f32[16,32,128]{2,1,0:T(8,128)}), f32[16,32,128]{2,1,0:T(8,128)}, u32[]{:S(2)}, u32[]{:S(2)}) async-start(f32[16,32,128]{2,1,0:T(8,128)} %broadcast_in_dim.20), calls=%async_computation.3 | async-start | bytes 524288 | tf_op jit(solution)/shard_map/correlation_sum/all_to_all | solution.py:210
  135.2 3.2 %collective-permute-start = (f32[14,64,128]{2,1,0:T(8,128)}, f32[14,64,128]{2,1,0:T(8,128)S(1)}, u32[]{:S(2)}, u32[]{:S(2)}) collective-permute-start(f32[14,64,128]{2,1,0:T(8,128)} %get-tuple-element.14), channel_id=1, source_target_pairs={{0,8},{8,16},{16,24},{24,32},{32,40},{40,48},{48,56},{56,64},{64,7... | collective-permute-start | bytes 1376264 | tf_op jit(solution)/shard_map/second_halo/ppermute | solution.py:215
  138.4 1.3 collective-permute-start.1
  139.7 3.1 %collective-permute-start.2 = (f32[16,64,128]{2,1,0:T(8,128)}, f32[16,64,128]{2,1,0:T(8,128)S(1)}, u32[]{:S(2)}, u32[]{:S(2)}) collective-permute-start(f32[16,64,128]{2,1,0:T(8,128)} %copy-done.11), channel_id=1, source_target_pairs={{0,1},{1,2},{2,3},{3,4},{4,5},{5,6},{6,7},{8,9},{9,10},{10,11},{11... | collective-permute-start | bytes 1572872 | tf_op jit(solution)/shard_map/second_halo/ppermute | solution.py:215
  144.0 2.0 collective-permute-start.3
  148.7 1.4 copy.34
  151.6 1.3 fusion.4.inside
  153.0 3.7 %collective-permute-done.y_a = f32[14,64,128]{2,1,0:T(8,128)S(1)} collective-permute-done((f32[14,64,128]{2,1,0:T(8,128)}, f32[14,64,128]{2,1,0:T(8,128)S(1)}, u32[]{:S(2)}, u32[]{:S(2)}) %collective-permute-start) | collective-permute-done | bytes 458784 | tf_op jit(solution)/shard_map/second_halo/ppermute | solution.py:215
  162.7 4.9 %second_side.1.images = f32[32,64,128]{2,1,0:T(8,128)S(1)} custom-call(f32[32,64,128]{2,1,0:T(8,128)S(1)} %get-tuple-element.13.phi, f32[14,64,128]{2,1,0:T(8,128)S(1)} %copy-done.6, f32[14,64,128]{2,1,0:T(8,128)} %collective-permute-done.1.y_b, f32[16,64,128]{2,1,0:T(8,128)S(1)} %copy-done.4, f32[8,64,128]{2,1,0:T(8,128)S(1)} %collective-permute-done.3.z_halo, ...), custom_call_target="tpu_custom_call" | custom-call | flops 1073741824 | bytes 6291456 | tf_op jit(solution)/shard_map/second_side/second_side/pallas_call | solution.py:264
  170.9 65.0 %all_to_all.33 = f32[64,33,1,128]{3,2,1,0:T(1,128)S(1)} all-to-all(f32[64,33,1,128]{3,2,1,0:T(1,128)S(1)} %bitcast.25), channel_id=1, replica_groups=mesh['x'=4,'z'=16,'y'=4,'core'=2] {'x','z'}, dimensions={0} | all-to-all | bytes 2162688 | tf_op jit(solution)/shard_map/transpose_back/all_to_all | solution.py:272
  236.6 7.9 %all-to-all-start.5 = ((f32[8,1,128]{2,1,0:T(1,128)}), f32[8,1,128]{2,1,0:T(1,128)S(1)}, u32[]{:S(2)}, u32[]{:S(2)}) async-start(f32[8,1,128]{2,1,0:T(1,128)} %broadcast_in_dim.47), calls=%async_computation.5 | async-start | bytes 8192 | tf_op jit(solution)/shard_map/rms/all_to_all | solution.py:210
  244.6 1.8 unpack.1
  246.4 2.7 %all-to-all-done.5 = f32[8,1,128]{2,1,0:T(1,128)S(1)} async-done(((f32[8,1,128]{2,1,0:T(1,128)}), f32[8,1,128]{2,1,0:T(1,128)S(1)}, u32[]{:S(2)}, u32[]{:S(2)}) %all-to-all-start.5) | async-done | bytes 4128 | tf_op jit(solution)/shard_map/rms/all_to_all | solution.py:210
  (74 shorter events, 26.6 us)
Async XLA Ops:
  0.6 134.5 %copy-start = (s32[2,16,128]{2,1,0:T(8,128)S(1)}, s32[2,16,128]{2,1,0:T(8,128)}, u32[]{:S(2)}) copy-start(s32[2,16,128]{2,1,0:T(8,128)} %param.9) | copy-start | bytes 49156
  0.6 1.2 copy-start.1
  74.6 6.4 %copy-start.16 = (f32[8,64,128]{2,1,0:T(8,128)}, f32[8,64,128]{2,1,0:T(8,128)S(1)}, u32[]{:S(2)}) copy-start(f32[8,64,128]{2,1,0:T(8,128)S(1)} %get-tuple-element.17) | copy-start | bytes 786436
  74.6 23.5 %collective-permute-start.6 = (f32[16,64,128]{2,1,0:T(8,128)S(1)}, f32[16,64,128]{2,1,0:T(8,128)S(1)}, u32[]{:S(2)}, u32[]{:S(2)}) collective-permute-start(f32[16,64,128]{2,1,0:T(8,128)S(1)} %get-tuple-element.20), channel_id=1, source_target_pairs={{1,0},{2,1},{3,2},{4,3},{5,4},{6,5},{7,6},{9,8},{10,9},{11,10},{12... | collective-permute-start | bytes 1572872 | tf_op jit(solution)/shard_map/first_halo/ppermute | solution.py:215
  81.0 16.3 %collective-permute-start.4 = (f32[14,64,128]{2,1,0:T(8,128)S(1)}, f32[14,64,128]{2,1,0:T(8,128)S(1)}, u32[]{:S(2)}, u32[]{:S(2)}) collective-permute-start(f32[14,64,128]{2,1,0:T(8,128)S(1)} %get-tuple-element.18), channel_id=1, source_target_pairs={{8,0},{16,8},{24,16},{32,24},{40,32},{48,40},{56,48},{64,56},{72,6... | collective-permute-start | bytes 1376264 | tf_op jit(solution)/shard_map/first_halo/ppermute | solution.py:215
  82.3 15.7 %collective-permute-start.5 = (f32[14,64,128]{2,1,0:T(8,128)S(1)}, f32[14,64,128]{2,1,0:T(8,128)}, u32[]{:S(2)}, u32[]{:S(2)}) collective-permute-start(f32[14,64,128]{2,1,0:T(8,128)S(1)} %get-tuple-element.19), channel_id=1, source_target_pairs={{0,8},{8,16},{16,24},{24,32},{32,40},{40,48},{48,56},{56,64},{64,7... | collective-permute-start | bytes 1376264 | tf_op jit(solution)/shard_map/first_halo/ppermute | solution.py:215
  87.1 10.2 %collective-permute-start.7 = (f32[8,64,128]{2,1,0:T(8,128)}, f32[8,64,128]{2,1,0:T(8,128)}, u32[]{:S(2)}, u32[]{:S(2)}) collective-permute-start(f32[8,64,128]{2,1,0:T(8,128)} %get-tuple-element.21), channel_id=1, source_target_pairs={{128,0},{256,128},{384,256},{129,1},{257,129},{385,257},{130,2},{2... | collective-permute-start | bytes 786440 | tf_op jit(solution)/shard_map/first_halo/ppermute | solution.py:215
  90.9 18.3 %copy-start.8 = (f32[32,128]{1,0:T(8,128)}, f32[32,128]{1,0:T(8,128)S(1)}, u32[]{:S(2)}) copy-start(f32[32,128]{1,0:T(8,128)S(1)} %mul.32.half) | copy-start | bytes 49156
  98.1 0.8 copy-start.12
  98.9 1.0 copy-start.13
  99.9 1.0 copy-start.15
  101.0 1.0 copy-start.17
  102.0 0.9 copy-start.18
  109.2 49.7 %copy-start.7 = (f32[256,128]{1,0:T(8,128)S(1)}, f32[256,128]{1,0:T(8,128)}, u32[]{:S(2)}) copy-start(f32[256,128]{1,0:T(8,128)} %constant.52.clone.first) | copy-start | bytes 393220
  129.6 37.9 %all-to-all-start.3 = ((f32[16,32,128]{2,1,0:T(8,128)}), f32[16,32,128]{2,1,0:T(8,128)}, u32[]{:S(2)}, u32[]{:S(2)}) async-start(f32[16,32,128]{2,1,0:T(8,128)} %broadcast_in_dim.20), calls=%async_computation.3 | async-start | bytes 524288 | tf_op jit(solution)/shard_map/correlation_sum/all_to_all | solution.py:210
  135.2 21.5 %collective-permute-start = (f32[14,64,128]{2,1,0:T(8,128)}, f32[14,64,128]{2,1,0:T(8,128)S(1)}, u32[]{:S(2)}, u32[]{:S(2)}) collective-permute-start(f32[14,64,128]{2,1,0:T(8,128)} %get-tuple-element.14), channel_id=1, source_target_pairs={{0,8},{8,16},{16,24},{24,32},{32,40},{40,48},{48,56},{56,64},{64,7... | collective-permute-start | bytes 1376264 | tf_op jit(solution)/shard_map/second_halo/ppermute | solution.py:215
  138.4 19.6 %collective-permute-start.1 = (f32[14,64,128]{2,1,0:T(8,128)}, f32[14,64,128]{2,1,0:T(8,128)}, u32[]{:S(2)}, u32[]{:S(2)}) collective-permute-start(f32[14,64,128]{2,1,0:T(8,128)} %get-tuple-element.15), channel_id=1, source_target_pairs={{8,0},{16,8},{24,16},{32,24},{40,32},{48,40},{56,48},{64,56},{72,6... | collective-permute-start | bytes 1376264 | tf_op jit(solution)/shard_map/second_halo/ppermute | solution.py:215
  139.7 18.3 %collective-permute-start.2 = (f32[16,64,128]{2,1,0:T(8,128)}, f32[16,64,128]{2,1,0:T(8,128)S(1)}, u32[]{:S(2)}, u32[]{:S(2)}) collective-permute-start(f32[16,64,128]{2,1,0:T(8,128)} %copy-done.11), channel_id=1, source_target_pairs={{0,1},{1,2},{2,3},{3,4},{4,5},{5,6},{6,7},{8,9},{9,10},{10,11},{11... | collective-permute-start | bytes 1572872 | tf_op jit(solution)/shard_map/second_halo/ppermute | solution.py:215
  144.0 9.0 %collective-permute-start.3 = (f32[8,64,128]{2,1,0:T(8,128)}, f32[8,64,128]{2,1,0:T(8,128)S(1)}, u32[]{:S(2)}, u32[]{:S(2)}) collective-permute-start(f32[8,64,128]{2,1,0:T(8,128)} %copy-done.16), channel_id=1, source_target_pairs={{0,128},{128,256},{256,384},{1,129},{129,257},{257,385},{2,130},{1... | collective-permute-start | bytes 786440 | tf_op jit(solution)/shard_map/second_halo/ppermute | solution.py:215
  156.7 0.8 copy-start.5
  158.9 1.0 copy-start.2
  159.9 1.0 copy-start.4
  160.9 1.0 copy-start.6
  236.6 12.5 %all-to-all-start.5 = ((f32[8,1,128]{2,1,0:T(1,128)}), f32[8,1,128]{2,1,0:T(1,128)S(1)}, u32[]{:S(2)}, u32[]{:S(2)}) async-start(f32[8,1,128]{2,1,0:T(1,128)} %broadcast_in_dim.47), calls=%async_computation.5 | async-start | bytes 8192 | tf_op jit(solution)/shard_map/rms/all_to_all | solution.py:210
  (5 other events, 3.8 us)

commit v2 on v1

v2 whole, which is shorter than its diff:
```python
import math

import jax
import jax.numpy as jnp
import numpy as np
from jax import lax
from jax.experimental import pallas as pl
from jax.experimental.pallas import tpu as pltpu
from jax.sharding import Mesh
from jax.sharding import PartitionSpec as P

spacing = 0.4
descent = 0.02
NX, NY, NZ, NORB = 128, 128, 128, 64
CELLS = NX * NY * NZ
KINETIC = -0.5 / spacing**2
REACH = 7
XG, YB, XL, ZB = 4, 8, 4, 32
ROWS, LANES = XG * YB, XL * ZB
HIGH = lax.Precision.HIGHEST
PARAMS = pltpu.CompilerParams(vmem_limit_bytes=12 * 1024 * 1024)
ORB, COMP = ("x", "z"), ("y", "core")


def second_coefs_list():
    terms = []
    for k in range(1, REACH + 1):
        terms.append(
            2.0
            * (-1) ** (k + 1)
            * math.factorial(REACH) ** 2
            / (k * k * math.factorial(REACH - k) * math.factorial(REACH + k))
        )
    return [-2.0 * sum(terms)] + terms


COEFS = [KINETIC * c for c in second_coefs_list()]


def coef(k):
    return COEFS[k] if 1 <= k <= REACH else 0.0


def inner_matrix():
    x, z = 16, ZB
    line_x = np.array([[coef(abs(i - j)) for j in range(x)] for i in range(x)])
    line_z = np.array([[coef(abs(i - j)) for j in range(z)] for i in range(z)])
    return (np.kron(line_x, np.eye(z)) + np.kron(np.eye(x), line_z)).astype(np.float32)


def edge_matrix(forward):
    table = np.zeros((3 * LANES, XG * LANES))
    for x in range(16):
        for z in range(ZB):
            out = x * ZB + z
            for layer in range(8):
                table[layer * ZB + z, out] += coef(16 + layer - x if forward else x + 8 - layer)
            for t in range(8):
                row = 2 * LANES + (x % XL) * ZB + (x // XL) * 8 + t
                table[row, out] += coef(ZB + t - z if forward else z + 8 - t)
    return table.astype(np.float32)


def pack_kernel(src, dst):
    group = lax.broadcasted_iota(jnp.int32, (32, LANES), 1) // ZB
    for xg in range(XG):
        for part in range(4):
            rows = slice(part * 32, part * 32 + 32)
            layers = [src[xg * XL + x, rows, :] for x in range(XL)]
            for q in range(4):
                piece = layers[q]
                for x in range(XL):
                    if x != q:
                        moved = pltpu.roll(layers[x], ((x - q) * ZB) % LANES, 1)
                        piece = jnp.where(group == x, moved, piece)
                first = q * 16 + part * 4
                dst[first : first + 4, xg * YB : (xg + 1) * YB, :] = piece.reshape(4, YB, LANES)


def unpack_kernel(src, dst):
    group = lax.broadcasted_iota(jnp.int32, (YB, LANES), 1) // ZB
    for yb in range(16):
        for xg in range(XG):
            pieces = [src[pl.ds((q * 16 + yb) * (ROWS + 1) + xg * YB, YB), :] for q in range(4)]
            for x in range(XL):
                layer = pieces[x]
                for q in range(4):
                    if q != x:
                        moved = pltpu.roll(pieces[q], ((q - x) * ZB) % LANES, 1)
                        layer = jnp.where(group == q, moved, layer)
                dst[xg * XL + x, yb * YB : (yb + 1) * YB, :] = layer


def spread_kernel(src, phi, y_up_a, y_down_b, x_up, z_up, y_down_a, y_up_b, x_down, z_down):
    slot = (lax.broadcasted_iota(jnp.int32, (NORB, LANES), 1) % ZB) // 8
    for y in range(YB):
        up = down = jnp.zeros((NORB, LANES), jnp.float32)
        for xg in range(XG):
            r = xg * YB + y
            row = src[pl.ds(r, NORB, stride=ROWS), :]
            phi[r] = row
            g = xg % 2
            if xg < 2:
                x_up[r] = row
                if y < REACH:
                    y_up_a[g * REACH + y] = row
                if y >= 1:
                    y_down_a[g * REACH + y - 1] = row
            else:
                x_down[r - 2 * YB] = row
                if y < REACH:
                    y_up_b[g * REACH + y] = row
                if y >= 1:
                    y_down_b[g * REACH + y - 1] = row
            up = jnp.where(slot == xg, pltpu.roll(row, xg * 8, 1) if xg else row, up)
            down = jnp.where(slot == xg, pltpu.roll(row, (xg * 8 - 24) % LANES, 1) if xg != 3 else row, down)
        z_up[y] = up
        z_down[y] = down


def constants_kernel(place, potential, segments, diagonal, inside):
    x_pos, z_pos = place[0], place[1]
    lane = lax.broadcasted_iota(jnp.int32, (YB, LANES), 1)
    first_row = pl.multiple_of(z_pos * YB, YB)
    pick = lax.broadcasted_iota(jnp.int32, (YB, NY), 1) == z_pos * YB + lax.broadcasted_iota(jnp.int32, (YB, NY), 0)
    ends = []
    for side in range(2):
        table = segments[side].astype(jnp.float32)
        ends.append(
            lax.dot_general(
                pick.astype(jnp.float32), table, (((1,), (1,)), ((), ())), precision=HIGH, preferred_element_type=jnp.float32
            )
        )
    depth = (x_pos * ZB + lane % ZB).astype(jnp.float32)
    layer = lax.broadcasted_iota(jnp.int32, (16, LANES), 0)
    for xg in range(XG):
        block = jnp.zeros((YB, LANES), jnp.float32)
        for x in range(XL):
            rows = potential[xg * XL + x, pl.ds(first_row, YB), :]
            moved = pltpu.roll(rows, lax.rem(x * ZB + LANES - x_pos * ZB, LANES), 1)
            block = jnp.where(lane // ZB == x, moved, block)
        diagonal[xg * YB : (xg + 1) * YB, :] = block + jnp.float32(3.0 * COEFS[0])
        widen = layer == xg * XL + lax.broadcasted_iota(jnp.int32, (16, LANES), 1) // ZB
        low, high = (
            jnp.dot(e, widen.astype(jnp.float32), precision=HIGH, preferred_element_type=jnp.float32) for e in ends
        )
        held = jnp.where(depth >= low, 1.0, 0.0) * jnp.where(depth < high, 1.0, 0.0)
        inside[xg * YB : (xg + 1) * YB, :] = held


def tall(ref, xg):
    return ref[xg * YB : (xg + 1) * YB].reshape(YB * NORB, LANES)


def pair_sums(left, right):
    left, right = jnp.concatenate(left, axis=1), jnp.concatenate(right, axis=1)
    return lax.dot_general(
        left, right, (((1,), (1,)), ((), ())), precision=HIGH, preferred_element_type=jnp.float32
    )


def inner_kernel(phi, diagonal, matrix, images, half_sums):
    total = jnp.zeros((NORB, NORB), jnp.float32)
    for pair in range(2):
        cells = jnp.concatenate([tall(phi, xg) for xg in range(XG)], axis=1)
        columns = slice(pair * 2 * LANES, (pair + 1) * 2 * LANES)
        both = jnp.dot(cells, matrix[:, columns], precision=HIGH, preferred_element_type=jnp.float32)
        for xg in (2 * pair, 2 * pair + 1):
            own = slice((xg % 2) * LANES, (xg % 2 + 1) * LANES)
            rows = [phi[xg * YB + y] for y in range(YB)]
            values = []
            for y in range(YB):
                r = xg * YB + y
                value = both[y * NORB : (y + 1) * NORB, own] + diagonal[r : r + 1, :] * rows[y]
                for other in range(YB):
                    if other != y:
                        value = value + COEFS[abs(other - y)] * rows[other]
                images[r] = value
                values.append(value)
            total = total + pair_sums(rows, values)
    half_sums[...] = 0.5 * total


def edge_terms(forward, x_halo, z_halo, y_a, y_b, matrix):
    halo = jnp.concatenate([tall(x_halo, 0), tall(x_halo, 1), z_halo[...].reshape(YB * NORB, LANES)], axis=1)
    for pair in range(2):
        columns = slice(pair * 2 * LANES, (pair + 1) * 2 * LANES)
        both = jnp.dot(halo, matrix[:, columns], precision=HIGH, preferred_element_type=jnp.float32)
        y_halo = y_b if pair else y_a
        for xg in (2 * pair, 2 * pair + 1):
            own = slice((xg % 2) * LANES, (xg % 2 + 1) * LANES)
            rows = [y_halo[(xg % 2) * REACH + i] for i in range(REACH)]
            values = []
            for y in range(YB):
                value = both[y * NORB : (y + 1) * NORB, own]
                for i in range(REACH):
                    k = YB + i - y if forward != bool(pair) else y + REACH - i
                    if 1 <= k <= REACH:
                        value = value + COEFS[k] * rows[i]
                values.append(value)
            yield xg, values


def first_edge_kernel(phi, y_a, y_b, x_halo, z_halo, matrix, inner, half_sums, images, partial):
    total = half_sums[...]
    for xg, values in edge_terms(True, x_halo, z_halo, y_a, y_b, matrix):
        for y in range(YB):
            images[xg * YB + y] = inner[xg * YB + y] + values[y]
        total = total + pair_sums([phi[xg * YB + y] for y in range(YB)], values)
    partial[...] = jnp.concatenate([total[: NORB // 2], total[NORB // 2 :]], axis=1)


def second_edge_kernel(y_a, y_b, x_halo, z_halo, matrix, before, images):
    for xg, values in edge_terms(False, x_halo, z_halo, y_a, y_b, matrix):
        for y in range(YB):
            images[xg * YB + y] = before[xg * YB + y] + values[y]


def update_kernel(phi, images, sums, inside, out):
    packed = jnp.sum(sums[...], axis=0)
    half = jnp.concatenate([packed[:, :NORB], packed[:, NORB:]], axis=0)
    lag = (half + half.T) * jnp.float32(1.0 / CELLS)
    squares = jnp.zeros((NORB, LANES), jnp.float32)
    for xg in range(XG):
        rows = [phi[xg * YB + y] for y in range(YB)]
        mixed = jnp.dot(lag, jnp.concatenate(rows, axis=1), precision=HIGH, preferred_element_type=jnp.float32)
        for y in range(YB):
            r = xg * YB + y
            gradient = images[r] - mixed[:, y * LANES : (y + 1) * LANES]
            squares = squares + gradient * gradient
            moved = rows[y] - descent * gradient
            out[pl.ds(r, NORB, stride=ROWS + 1), :] = jnp.where(inside[r : r + 1, :] > 0.0, moved, 0.0)
    ones = jnp.ones((8, LANES), jnp.float32)
    sums = lax.dot_general(ones, squares, (((1,), (1,)), ((), ())), precision=HIGH, preferred_element_type=jnp.float32)
    sums = jnp.concatenate([sums, jnp.zeros((8, LANES - NORB), jnp.float32)], axis=1)
    out[pl.ds(ROWS, NORB, stride=ROWS + 1), :] = jnp.broadcast_to(sums[0:1, :], (NORB, LANES))


def f32(*shape):
    return jax.ShapeDtypeStruct(shape, jnp.float32)


def call(kernel, out_shape, name, flops, nbytes, **more):
    return pl.pallas_call(
        kernel,
        out_shape=out_shape,
        compiler_params=PARAMS,
        name=name,
        cost_estimate=pl.CostEstimate(flops=flops, bytes_accessed=nbytes, transcendentals=0),
        **more,
    )


def copies(value, axes):
    peers = math.prod(lax.axis_size(a) for a in axes)
    sent = jnp.broadcast_to(value[None], (peers,) + value.shape)
    return lax.all_to_all(sent, axes, 0, 0, tiled=True)


def shift(value, axes, count, up):
    pairs = [(i + 1, i) if up else (i, i + 1) for i in range(count - 1)]
    return lax.ppermute(value, axes, pairs)


def on_device(orbitals, potential, segments):
    mib = 1 << 20
    with jax.named_scope("pack"):
        pieces = call(pack_kernel, f32(NORB, ROWS, LANES), "pack", 1 << 20, 2 * mib)(orbitals[0])
    with jax.named_scope("transpose"):
        arrived = lax.all_to_all(pieces, ORB, 0, 0, tiled=True).reshape(NORB * ROWS, LANES)

    with jax.named_scope("block_constants"):
        place = jnp.stack([lax.axis_index("x"), lax.axis_index("z")]).astype(jnp.int32)
        vmem = pl.BlockSpec(memory_space=pltpu.VMEM)
        diagonal, inside = call(
            constants_kernel,
            [f32(ROWS, LANES)] * 2,
            "constants",
            1 << 20,
            mib,
            in_specs=[pl.BlockSpec(memory_space=pltpu.SMEM), vmem, vmem],
        )(place, potential, segments)
    inner, ahead, behind = (jnp.asarray(m) for m in (inner_matrix(), edge_matrix(True), edge_matrix(False)))

    with jax.named_scope("spread"):
        side = [f32(2 * REACH, NORB, LANES)] * 2 + [f32(2 * YB, NORB, LANES), f32(YB, NORB, LANES)]
        whole = f32(ROWS, NORB, LANES)
        phi, *sides = call(spread_kernel, [whole] + side + side, "spread", 1 << 20, 6 * mib)(arrived)
    y_up_a, y_down_b, x_up, z_up, *second = sides
    with jax.named_scope("first_halo"):
        y_up_a = shift(y_up_a, "z", 16, True)
        y_down_b = shift(y_down_b, "z", 16, False)
        x_up = shift(x_up, COMP, 8, True)
        z_up = shift(z_up, "x", 4, True)
    with jax.named_scope("inner"):
        images, sums = call(inner_kernel, [whole, f32(NORB, NORB)], "inner", 1 << 32, 2 * mib)(phi, diagonal, inner)
    with jax.named_scope("first_edge"):
        images, partial = call(first_edge_kernel, [whole, f32(NORB // 2, 2 * NORB)], "first_edge", 1 << 31, 4 * mib)(
            phi, y_up_a, y_down_b, x_up, z_up, ahead, images, sums
        )
    partial, second = lax.optimization_barrier((partial, second))
    y_down_a, y_up_b, x_down, z_down = second
    with jax.named_scope("correlation_sum"):
        partial = jnp.sum(copies(partial, ("x", "y")), axis=0)
        partial = jnp.sum(copies(partial, ("core",)), axis=0)
    with jax.named_scope("second_halo"):
        y_down_a = shift(y_down_a, "z", 16, False)
        y_up_b = shift(y_up_b, "z", 16, True)
        x_down = shift(x_down, COMP, 8, False)
        z_down = shift(z_down, "x", 4, False)
    partial, y_down_a, y_up_b, x_down, z_down = lax.optimization_barrier((partial, y_down_a, y_up_b, x_down, z_down))
    with jax.named_scope("correlation_sum"):
        partial = copies(partial, ("z",))
    with jax.named_scope("second_edge"):
        images = call(second_edge_kernel, whole, "second_edge", 1 << 31, 4 * mib)(
            y_down_a, y_up_b, x_down, z_down, behind, images
        )
    with jax.named_scope("update"):
        sent = call(update_kernel, f32(NORB * (ROWS + 1), LANES), "update", 1 << 28, 3 * mib)(
            phi, images, partial, inside
        )
    with jax.named_scope("transpose_back"):
        back = lax.all_to_all(sent.reshape(NORB, ROWS + 1, 1, LANES), ORB, 0, 0, tiled=True)
    with jax.named_scope("rms"):
        slab = jnp.sum(back[:, ROWS, 0, :], axis=0)
        squares = jnp.sum(copies(slab, COMP), axis=0)[:NORB]
        grad_rms = jnp.sqrt(squares / CELLS)
    with jax.named_scope("unpack"):
        new = call(unpack_kernel, f32(16, NY, NZ), "unpack", 1 << 20, 2 * mib)(back.reshape(NORB * (ROWS + 1), LANES))
    return new[None], grad_rms


def solution(mesh):
    fine = Mesh(mesh.devices.reshape(4, 16, 4, 2), ("x", "z", "y", "core"))
    return jax.shard_map(
        on_device,
        mesh=fine,
        in_specs=(P(ORB, COMP, None, None), P(COMP, None, None), P(None, COMP, None)),
        out_specs=(P(ORB, COMP, None, None), P()),
        check_vma=False,
    )
```

time: 251 us -> 241 us (0.960)
  local copies, waits for them, and re-layouts: 22.8 us -> 11.3 us
  starting transfers between devices: 36.8 us -> 41.4 us
  other arithmetic: 5.13 us -> 1.68 us
  Pallas kernels: 16.9 us -> 19.9 us
    ppermute x8, waiting for transfers between devices: 10.7 us -> 2.71 us  [shift(): return lax.ppermute(value, axes, pairs)]
    all_to_all x2, waiting for transfers between devices: 2.75 us -> 10.3 us  [copies(): return lax.all_to_all(sent, axes, 0, 0, tiled=True)]
    unnamed x40 -> x32, local copies, waits for them, and re-layouts: 13.9 us -> 9.92 us
    broadcast_in_dim x8 -> x4, local copies, waits for them, and re-layouts: 4.37 us -> 1.42 us  [copies(): sent = jnp.broadcast_to(value[None], (peers,) + value.shape)]
    pallas_call x3 -> x5, Pallas kernels: 13 us -> 15.9 us  [the longest x1 5.63 us: on_device(): call(first_edge_kernel, [whole, f32(NORB // 2, 2 * NORB)], 'first_edge',...]
    slice x4 -> x0, local copies, waits for them, and re-layouts: 2.74 us -> none  [the longest x3 2.67 us: on_device(): inside = ((depth >= ends[0]) & (depth < ends[1])).astype(jnp.float32)]
    all_to_all x2, starting transfers between devices: 13.4 us -> 16 us  [copies(): return lax.all_to_all(sent, axes, 0, 0, tiled=True)]
  transfers between devices with their start and end apart: 10 -> 10, of which waited for: 4 -> 3; matrix products, arithmetic and copies ran while one was open for 4% -> 0% of each run, Pallas kernels for 3% -> 4%
where the time goes in v2:
time: 241 us; the launch traced here: 240 us
  blocking collectives  152 us (63%)
  starting transfers between devices  41.4 us (17%)
  Pallas kernels  19.9 us (8%)
  waiting for transfers between devices  13 us (5%)
  local copies, waits for them, and re-layouts  11.3 us (5%)
    all_to_all x1, blocking collectives, on_device(): lax.all_to_all(pieces, ORB, 0, 0, tiled=True).reshape(NORB * ROWS, LANES)  69.4 us
    all_to_all x1, blocking collectives, on_device(): lax.all_to_all(sent.reshape(NORB, ROWS + 1, 1, LANES), ORB, 0, 0, tiled=T...  63.3 us
    ppermute x8, starting transfers between devices, shift(): return lax.ppermute(value, axes, pairs)  25.4 us
    all_to_all x2, blocking collectives, copies(): return lax.all_to_all(sent, axes, 0, 0, tiled=True)  19 us
    all_to_all x2, starting transfers between devices, copies(): return lax.all_to_all(sent, axes, 0, 0, tiled=True)  16 us
    all_to_all x2, waiting for transfers between devices, copies(): return lax.all_to_all(sent, axes, 0, 0, tiled=True)  10.3 us
    unnamed x32, local copies, waits for them, and re-layouts  9.92 us
    pallas_call x1, Pallas kernels, on_device(): call(first_edge_kernel, [whole, f32(NORB // 2, 2 * NORB)], 'first_edge',...  5.63 us
  transfers between devices with their start and end apart: 10, of which 3 were waited for; matrix products, arithmetic and copies ran while one was open for 0% of the time, Pallas kernels for 4%

profile of v2, /device:TPU:1, one launch (start us, length us, event | category | flops | bytes accessed | tf_op | source)
XLA Modules:
  0.0 239.9 jit_solution(256095974700671674)
XLA Ops:
  2.8 69.4 %all_to_all.31 = f32[64,32,128]{2,1,0:T(8,128)S(1)} all-to-all(f32[64,32,128]{2,1,0:T(8,128)S(1)} %pack.1), channel_id=1, replica_groups=mesh['x'=4,'z'=16,'y'=4,'core'=2] {'x','z'}, dimensions={0} | all-to-all | bytes 2097152 | tf_op jit(solution)/shard_map/transpose/all_to_all | solution.py:270
  72.1 1.6 spread.1
  76.8 6.4 %collective-permute-start.2 = (f32[16,64,128]{2,1,0:T(8,128)S(1)}, f32[16,64,128]{2,1,0:T(8,128)}, u32[]{:S(2)}, u32[]{:S(2)}) collective-permute-start(f32[16,64,128]{2,1,0:T(8,128)S(1)} %get-tuple-element.30), channel_id=1, source_target_pairs={{1,0},{2,1},{3,2},{4,3},{5,4},{6,5},{7,6},{9,8},{10,9},{11,10},{12... | collective-permute-start | bytes 1572872 | tf_op jit(solution)/shard_map/first_halo/ppermute | solution.py:262
  83.2 1.3 collective-permute-start
  84.5 4.0 %collective-permute-start.1 = (f32[14,64,128]{2,1,0:T(8,128)}, f32[14,64,128]{2,1,0:T(8,128)S(1)}, u32[]{:S(2)}, u32[]{:S(2)}) collective-permute-start(f32[14,64,128]{2,1,0:T(8,128)} %copy-done.7), channel_id=1, source_target_pairs={{0,8},{8,16},{16,24},{24,32},{32,40},{40,48},{48,56},{56,64},{64,7... | collective-permute-start | bytes 1376264 | tf_op jit(solution)/shard_map/first_halo/ppermute | solution.py:262
  89.5 1.3 collective-permute-start.3
  92.0 4.7 %inner.1 = (f32[32,64,128]{2,1,0:T(8,128)S(1)}, f32[64,64]{1,0:T(8,128)S(1)}) custom-call(f32[32,64,128]{2,1,0:T(8,128)S(1)} %get-tuple-element.27.phi, f32[32,128]{1,0:T(8,128)S(1)} %get-tuple-element.32.diagonal, f32[512,512]{1,0:T(8,128)S(1)} %copy-done.11), custom_call_target="tpu_custom_call" | custom-call | flops 4294967296 | bytes 2097152 | tf_op jit(solution)/shard_map/inner/inner/pallas_call | solution.py:296
  96.7 2.7 %collective-permute-done.3.z_halo = f32[8,64,128]{2,1,0:T(8,128)S(1)} collective-permute-done((f32[8,64,128]{2,1,0:T(8,128)S(1)}, f32[8,64,128]{2,1,0:T(8,128)S(1)}, u32[]{:S(2)}, u32[]{:S(2)}) %collective-permute-start.3) | collective-permute-done | bytes 262176 | tf_op jit(solution)/shard_map/first_halo/ppermute | solution.py:262
  99.4 5.6 %first_edge.1 = (f32[32,64,128]{2,1,0:T(8,128)S(1)}, f32[32,128]{1,0:T(8,128)S(1)}) custom-call(f32[32,64,128]{2,1,0:T(8,128)S(1)} %get-tuple-element.27.phi, f32[14,64,128]{2,1,0:T(8,128)S(1)} %collective-permute-done.y_a, f32[14,64,128]{2,1,0:T(8,128)S(1)} %collective-permute-done.1.y_b, f32[16,64,128]{2,1,0:T(8,128)} %collective-permute-done.2.x_halo, ...), custom_call_target="tpu_custom_call" | custom-call | flops 2147483648 | bytes 4194304 | tf_op jit(solution)/shard_map/first_edge/first_edge/pallas_call | solution.py:298
  106.1 3.8 %collective-permute-start.6 = (f32[16,64,128]{2,1,0:T(8,128)S(1)}, f32[16,64,128]{2,1,0:T(8,128)S(1)}, u32[]{:S(2)}, u32[]{:S(2)}) collective-permute-start(f32[16,64,128]{2,1,0:T(8,128)S(1)} %get-tuple-element.43), channel_id=1, source_target_pairs={{0,1},{1,2},{2,3},{3,4},{4,5},{5,6},{6,7},{8,9},{9,10},{10,11},{11... | collective-permute-start | bytes 1572872 | tf_op jit(solution)/shard_map/second_halo/ppermute | solution.py:262
  109.9 3.4 %collective-permute-start.4 = (f32[14,64,128]{2,1,0:T(8,128)S(1)}, f32[14,64,128]{2,1,0:T(8,128)S(1)}, u32[]{:S(2)}, u32[]{:S(2)}) collective-permute-start(f32[14,64,128]{2,1,0:T(8,128)S(1)} %copy-done.6), channel_id=1, source_target_pairs={{0,8},{8,16},{16,24},{24,32},{32,40},{40,48},{48,56},{56,64},{64,7... | collective-permute-start | bytes 1376264 | tf_op jit(solution)/shard_map/second_halo/ppermute | solution.py:262
  113.3 1.3 collective-permute-start.5
  114.6 3.9 %collective-permute-start.7 = (f32[8,64,128]{2,1,0:T(8,128)}, f32[8,64,128]{2,1,0:T(8,128)}, u32[]{:S(2)}, u32[]{:S(2)}) collective-permute-start(f32[8,64,128]{2,1,0:T(8,128)} %get-tuple-element.44), channel_id=1, source_target_pairs={{0,128},{128,256},{256,384},{1,129},{129,257},{257,385},{2,130},{1... | collective-permute-start | bytes 786440 | tf_op jit(solution)/shard_map/second_halo/ppermute | solution.py:262
  118.5 14.2 %all_to_all.32 = f32[16,32,128]{2,1,0:T(8,128)} all-to-all(f32[16,32,128]{2,1,0:T(8,128)S(1)} %broadcast_in_dim.10), channel_id=1, replica_groups=mesh['x'=4,'z'=16,'y'=4,'core'=2] {'x','y'}, dimensions={0} | all-to-all | bytes 524288 | tf_op jit(solution)/shard_map/correlation_sum/all_to_all | solution.py:257
  133.7 4.8 %all_to_all.33 = f32[2,32,128]{2,1,0:T(8,128)S(1)} all-to-all(f32[2,32,128]{2,1,0:T(8,128)S(1)} %broadcast_in_dim.11), channel_id=1, replica_groups=mesh['x'=4,'z'=16,'y'=4,'core'=2] {'core'}, dimensions={0} | all-to-all | bytes 65536 | tf_op jit(solution)/shard_map/correlation_sum/all_to_all | solution.py:257
  139.4 8.1 %all-to-all-start.3 = ((f32[16,32,128]{2,1,0:T(8,128)}), f32[16,32,128]{2,1,0:T(8,128)S(1)}, u32[]{:S(2)}, u32[]{:S(2)}) async-start(f32[16,32,128]{2,1,0:T(8,128)} %broadcast_in_dim.12), calls=%async_computation.3 | async-start | bytes 524288 | tf_op jit(solution)/shard_map/correlation_sum/all_to_all | solution.py:257
  149.7 1.2 copy-done.15
  150.9 3.1 %second_edge.1.images = f32[32,64,128]{2,1,0:T(8,128)S(1)} custom-call(f32[14,64,128]{2,1,0:T(8,128)S(1)} %copy-done.10, f32[14,64,128]{2,1,0:T(8,128)} %collective-permute-done.5.y_b, f32[16,64,128]{2,1,0:T(8,128)S(1)} %collective-permute-done.6.x_halo, f32[8,64,128]{2,1,0:T(8,128)} %collective-permute-done.7.z_halo, f32[384,512]{1,0:T(8,128)S(1)} %copy-done.12, ...), custom_call_target="tpu_custom_call" | custom-call | flops 2147483648 | bytes 4194304 | tf_op jit(solution)/shard_map/second_edge/second_edge/pallas_call | solution.py:315
  154.0 7.5 %all-to-all-done.3.sums = f32[16,32,128]{2,1,0:T(8,128)S(1)} async-done(((f32[16,32,128]{2,1,0:T(8,128)}), f32[16,32,128]{2,1,0:T(8,128)S(1)}, u32[]{:S(2)}, u32[]{:S(2)}) %all-to-all-start.3) | async-done | bytes 262176 | tf_op jit(solution)/shard_map/correlation_sum/all_to_all | solution.py:257
  161.5 1.3 update.1
  162.8 63.3 %all_to_all.34 = f32[64,33,1,128]{3,2,1,0:T(1,128)S(1)} all-to-all(f32[64,33,1,128]{3,2,1,0:T(1,128)S(1)} %bitcast.9), channel_id=1, replica_groups=mesh['x'=4,'z'=16,'y'=4,'core'=2] {'x','z'}, dimensions={0} | all-to-all | bytes 2162688 | tf_op jit(solution)/shard_map/transpose_back/all_to_all | solution.py:323
  226.8 7.9 %all-to-all-start.5 = ((f32[8,1,128]{2,1,0:T(1,128)}), f32[8,1,128]{2,1,0:T(1,128)S(1)}, u32[]{:S(2)}, u32[]{:S(2)}) async-start(f32[8,1,128]{2,1,0:T(1,128)} %broadcast_in_dim.14), calls=%async_computation.5 | async-start | bytes 8192 | tf_op jit(solution)/shard_map/rms/all_to_all | solution.py:257
  234.7 1.8 unpack.1
  236.6 2.7 %all-to-all-done.5 = f32[8,1,128]{2,1,0:T(1,128)S(1)} async-done(((f32[8,1,128]{2,1,0:T(1,128)}), f32[8,1,128]{2,1,0:T(1,128)S(1)}, u32[]{:S(2)}, u32[]{:S(2)}) %all-to-all-start.5) | async-done | bytes 4128 | tf_op jit(solution)/shard_map/rms/all_to_all | solution.py:257
  (50 shorter events, 13.6 us)
Async XLA Ops:
  0.6 1.2 copy-start
  2.7 85.9 %copy-start.1 = (f32[16,128,128]{2,1,0:T(8,128)S(1)}, f32[16,128,128]{2,1,0:T(8,128)}, u32[]{:S(2)}) copy-start(f32[16,128,128]{2,1,0:T(8,128)} %potential.1) | copy-start | bytes 3145732
  2.7 85.9 %copy-start.2 = (s32[2,16,128]{2,1,0:T(8,128)S(1)}, s32[2,16,128]{2,1,0:T(8,128)}, u32[]{:S(2)}) copy-start(s32[2,16,128]{2,1,0:T(8,128)} %segments.1) | copy-start | bytes 49156
  73.7 0.8 copy-start.3
  74.5 0.8 copy-start.5
  76.8 22.6 %collective-permute-start.2 = (f32[16,64,128]{2,1,0:T(8,128)S(1)}, f32[16,64,128]{2,1,0:T(8,128)}, u32[]{:S(2)}, u32[]{:S(2)}) collective-permute-start(f32[16,64,128]{2,1,0:T(8,128)S(1)} %get-tuple-element.30), channel_id=1, source_target_pairs={{1,0},{2,1},{3,2},{4,3},{5,4},{6,5},{7,6},{9,8},{10,9},{11,10},{12... | collective-permute-start | bytes 1572872 | tf_op jit(solution)/shard_map/first_halo/ppermute | solution.py:262
  83.2 16.2 %collective-permute-start = (f32[14,64,128]{2,1,0:T(8,128)}, f32[14,64,128]{2,1,0:T(8,128)S(1)}, u32[]{:S(2)}, u32[]{:S(2)}) collective-permute-start(f32[14,64,128]{2,1,0:T(8,128)} %copy-done.8), channel_id=1, source_target_pairs={{8,0},{16,8},{24,16},{32,24},{40,32},{48,40},{56,48},{64,56},{72,6... | collective-permute-start | bytes 1376264 | tf_op jit(solution)/shard_map/first_halo/ppermute | solution.py:262
  84.5 14.9 %collective-permute-start.1 = (f32[14,64,128]{2,1,0:T(8,128)}, f32[14,64,128]{2,1,0:T(8,128)S(1)}, u32[]{:S(2)}, u32[]{:S(2)}) collective-permute-start(f32[14,64,128]{2,1,0:T(8,128)} %copy-done.7), channel_id=1, source_target_pairs={{0,8},{8,16},{16,24},{24,32},{32,40},{40,48},{48,56},{56,64},{64,7... | collective-permute-start | bytes 1376264 | tf_op jit(solution)/shard_map/first_halo/ppermute | solution.py:262
  89.5 9.9 %collective-permute-start.3 = (f32[8,64,128]{2,1,0:T(8,128)S(1)}, f32[8,64,128]{2,1,0:T(8,128)S(1)}, u32[]{:S(2)}, u32[]{:S(2)}) collective-permute-start(f32[8,64,128]{2,1,0:T(8,128)S(1)} %get-tuple-element.31), channel_id=1, source_target_pairs={{128,0},{256,128},{384,256},{129,1},{257,129},{385,257},{130,2},{2... | collective-permute-start | bytes 786440 | tf_op jit(solution)/shard_map/first_halo/ppermute | solution.py:262
  90.8 1.2 copy-start.11
  92.0 7.4 %copy-start.13 = (f32[384,512]{1,0:T(8,128)S(1)}, f32[384,512]{1,0:T(8,128)}, u32[]{:S(2)}) copy-start(f32[384,512]{1,0:T(8,128)} %constant.23.clone.matrix) | copy-start | bytes 2359300
  99.4 10.4 %copy-start.6 = (f32[14,64,128]{2,1,0:T(8,128)S(1)}, f32[14,64,128]{2,1,0:T(8,128)}, u32[]{:S(2)}) copy-start(f32[14,64,128]{2,1,0:T(8,128)} %copy-done.5) | copy-start | bytes 1376260
  99.4 13.9 %copy-start.4 = (f32[14,64,128]{2,1,0:T(8,128)S(1)}, f32[14,64,128]{2,1,0:T(8,128)}, u32[]{:S(2)}) copy-start(f32[14,64,128]{2,1,0:T(8,128)} %copy-done.3) | copy-start | bytes 1376260
  105.1 1.0 copy-start.14
  106.1 32.5 %collective-permute-start.6 = (f32[16,64,128]{2,1,0:T(8,128)S(1)}, f32[16,64,128]{2,1,0:T(8,128)S(1)}, u32[]{:S(2)}, u32[]{:S(2)}) collective-permute-start(f32[16,64,128]{2,1,0:T(8,128)S(1)} %get-tuple-element.43), channel_id=1, source_target_pairs={{0,1},{1,2},{2,3},{3,4},{4,5},{5,6},{6,7},{8,9},{9,10},{10,11},{11... | collective-permute-start | bytes 1572872 | tf_op jit(solution)/shard_map/second_halo/ppermute | solution.py:262
  109.9 28.7 %collective-permute-start.4 = (f32[14,64,128]{2,1,0:T(8,128)S(1)}, f32[14,64,128]{2,1,0:T(8,128)S(1)}, u32[]{:S(2)}, u32[]{:S(2)}) collective-permute-start(f32[14,64,128]{2,1,0:T(8,128)S(1)} %copy-done.6), channel_id=1, source_target_pairs={{0,8},{8,16},{16,24},{24,32},{32,40},{40,48},{48,56},{56,64},{64,7... | collective-permute-start | bytes 1376264 | tf_op jit(solution)/shard_map/second_halo/ppermute | solution.py:262
  113.3 25.3 %collective-permute-start.5 = (f32[14,64,128]{2,1,0:T(8,128)S(1)}, f32[14,64,128]{2,1,0:T(8,128)}, u32[]{:S(2)}, u32[]{:S(2)}) collective-permute-start(f32[14,64,128]{2,1,0:T(8,128)S(1)} %copy-done.4), channel_id=1, source_target_pairs={{8,0},{16,8},{24,16},{32,24},{40,32},{48,40},{56,48},{64,56},{72,6... | collective-permute-start | bytes 1376264 | tf_op jit(solution)/shard_map/second_halo/ppermute | solution.py:262
  114.6 23.9 %collective-permute-start.7 = (f32[8,64,128]{2,1,0:T(8,128)}, f32[8,64,128]{2,1,0:T(8,128)}, u32[]{:S(2)}, u32[]{:S(2)}) collective-permute-start(f32[8,64,128]{2,1,0:T(8,128)} %get-tuple-element.44), channel_id=1, source_target_pairs={{0,128},{128,256},{256,384},{1,129},{129,257},{257,385},{2,130},{1... | collective-permute-start | bytes 786440 | tf_op jit(solution)/shard_map/second_halo/ppermute | solution.py:262
  138.5 9.0 %copy-start.9 = (f32[14,64,128]{2,1,0:T(8,128)}, f32[14,64,128]{2,1,0:T(8,128)S(1)}, u32[]{:S(2)}) copy-start(f32[14,64,128]{2,1,0:T(8,128)S(1)} %collective-permute-done.4.y_a) | copy-start | bytes 1376260
  139.4 22.1 %all-to-all-start.3 = ((f32[16,32,128]{2,1,0:T(8,128)}), f32[16,32,128]{2,1,0:T(8,128)S(1)}, u32[]{:S(2)}, u32[]{:S(2)}) async-start(f32[16,32,128]{2,1,0:T(8,128)} %broadcast_in_dim.12), calls=%async_computation.3 | async-start | bytes 524288 | tf_op jit(solution)/shard_map/correlation_sum/all_to_all | solution.py:257
  147.5 1.0 copy-start.10
  148.5 1.1 copy-start.12
  149.7 1.2 copy-start.15
  226.8 12.5 %all-to-all-start.5 = ((f32[8,1,128]{2,1,0:T(1,128)}), f32[8,1,128]{2,1,0:T(1,128)S(1)}, u32[]{:S(2)}, u32[]{:S(2)}) async-start(f32[8,1,128]{2,1,0:T(1,128)} %broadcast_in_dim.14), calls=%async_computation.5 | async-start | bytes 8192 | tf_op jit(solution)/shard_map/rms/all_to_all | solution.py:257
  (2 other events, 1.5 us)

commit v3 on v2

--- a/solution.py
+++ b/solution.py
@@ -48,17 +48,31 @@
     return (np.kron(line_x, np.eye(z)) + np.kron(np.eye(x), line_z)).astype(np.float32)
 
 
-def edge_matrix(forward):
-    table = np.zeros((3 * LANES, XG * LANES))
+def edge_matrix():
+    table = np.zeros((2, 4 * LANES, 4 * LANES))
     for x in range(16):
         for z in range(ZB):
             out = x * ZB + z
             for layer in range(8):
-                table[layer * ZB + z, out] += coef(16 + layer - x if forward else x + 8 - layer)
+                table[0, layer * ZB + z, out] += coef(x + 8 - layer)
+                table[1, layer * ZB + z, out] += coef(16 + layer - x)
             for t in range(8):
                 row = 2 * LANES + (x % XL) * ZB + (x // XL) * 8 + t
-                table[row, out] += coef(ZB + t - z if forward else z + 8 - t)
-    return table.astype(np.float32)
+                table[:, row, out] += coef(ZB + t - z)
+                table[:, row + LANES, out] += coef(z + 8 - t)
+    return np.concatenate([table[0, :, : 2 * LANES], table[1, :, 2 * LANES :]], axis=1)
+
+
+def split(value):
+    high = value.astype(jnp.bfloat16)
+    return high, (value - high.astype(jnp.float32)).astype(jnp.bfloat16)
+
+
+def three_products(left, right, dims=(((1,), (0,)), ((), ()))):
+    def product(a, b):
+        return lax.dot_general(a, b, dims, preferred_element_type=jnp.float32)
+
+    return product(left[0], right[0]) + (product(left[1], right[0]) + product(left[0], right[1]))
 
 
 def pack_kernel(src, dst):
@@ -91,7 +105,10 @@
                 dst[xg * XL + x, yb * YB : (yb + 1) * YB, :] = layer
 
 
-def spread_kernel(src, phi, y_up_a, y_down_b, x_up, z_up, y_down_a, y_up_b, x_down, z_down):
+def spread_kernel(src, phi, *refs):
+    sent, kept, sems = refs[:6], refs[6:12], refs[12]
+    y_up, y_down, x_up, x_down, z_up, z_down = kept
+    moves = [pltpu.make_async_copy(kept[i], sent[i], sems.at[i]) for i in range(6)]
     slot = (lax.broadcasted_iota(jnp.int32, (NORB, LANES), 1) % ZB) // 8
     for y in range(YB):
         up = down = jnp.zeros((NORB, LANES), jnp.float32)
@@ -99,23 +116,24 @@
             r = xg * YB + y
             row = src[pl.ds(r, NORB, stride=ROWS), :]
             phi[r] = row
-            g = xg % 2
+            if y < REACH:
+                y_up[xg * REACH + y] = row
+            if y >= 1:
+                y_down[xg * REACH + y - 1] = row
             if xg < 2:
                 x_up[r] = row
-                if y < REACH:
-                    y_up_a[g * REACH + y] = row
-                if y >= 1:
-                    y_down_a[g * REACH + y - 1] = row
             else:
                 x_down[r - 2 * YB] = row
-                if y < REACH:
-                    y_up_b[g * REACH + y] = row
-                if y >= 1:
-                    y_down_b[g * REACH + y - 1] = row
             up = jnp.where(slot == xg, pltpu.roll(row, xg * 8, 1) if xg else row, up)
             down = jnp.where(slot == xg, pltpu.roll(row, (xg * 8 - 24) % LANES, 1) if xg != 3 else row, down)
         z_up[y] = up
         z_down[y] = down
+        if y == REACH - 1:
+            moves[0].start()
+    for i in range(1, 6):
+        moves[i].start()
+    for move in moves:
+        move.wait()
 
 
 def constants_kernel(place, potential, segments, diagonal, inside):
@@ -159,7 +177,7 @@
     )
 
 
-def inner_kernel(phi, diagonal, matrix, images, half_sums):
+def inner_kernel(phi, diagonal, matrix, images, sums):
     total = jnp.zeros((NORB, NORB), jnp.float32)
     for pair in range(2):
         cells = jnp.concatenate([tall(phi, xg) for xg in range(XG)], axis=1)
@@ -178,48 +196,53 @@
                 images[r] = value
                 values.append(value)
             total = total + pair_sums(rows, values)
-    half_sums[...] = 0.5 * total
-
-
-def edge_terms(forward, x_halo, z_halo, y_a, y_b, matrix):
-    halo = jnp.concatenate([tall(x_halo, 0), tall(x_halo, 1), z_halo[...].reshape(YB * NORB, LANES)], axis=1)
+    sums[...] = total
+
+
+def edge_kernel(phi, inner, sums, high, low, *refs):
+    came, images, partial, kept, sems = refs[:6], refs[6], refs[7], refs[8:14], refs[14]
+    y_up, y_down, x_up, x_down, z_up, z_down = kept
+    moves = [pltpu.make_async_copy(came[i], kept[i], sems.at[i]) for i in range(6)]
+    for move in moves:
+        move.start()
+    for move in moves:
+        move.wait()
+    total = sums[...]
+    z_halo = [z_up[...].reshape(YB * NORB, LANES), z_down[...].reshape(YB * NORB, LANES)]
     for pair in range(2):
+        x_halo = x_up if pair else x_down
+        halo = split(jnp.concatenate([tall(x_halo, 0), tall(x_halo, 1)] + z_halo, axis=1))
         columns = slice(pair * 2 * LANES, (pair + 1) * 2 * LANES)
-        both = jnp.dot(halo, matrix[:, columns], precision=HIGH, preferred_element_type=jnp.float32)
-        y_halo = y_b if pair else y_a
+        both = three_products(halo, (high[:, columns], low[:, columns]))
         for xg in (2 * pair, 2 * pair + 1):
             own = slice((xg % 2) * LANES, (xg % 2 + 1) * LANES)
-            rows = [y_halo[(xg % 2) * REACH + i] for i in range(REACH)]
+            above = [y_up[xg * REACH + i] for i in range(REACH)]
+            below = [y_down[xg * REACH + i] for i in range(REACH)]
             values = []
             for y in range(YB):
                 value = both[y * NORB : (y + 1) * NORB, own]
                 for i in range(REACH):
-                    k = YB + i - y if forward != bool(pair) else y + REACH - i
-                    if 1 <= k <= REACH:
-                        value = value + COEFS[k] * rows[i]
+                    if YB + i - y <= REACH:
+                        value = value + COEFS[YB + i - y] * above[i]
+                    if 1 <= y + REACH - i <= REACH:
+                        value = value + COEFS[y + REACH - i] * below[i]
+                images[xg * YB + y] = inner[xg * YB + y] + value
                 values.append(value)
-            yield xg, values
-
-
-def first_edge_kernel(phi, y_a, y_b, x_halo, z_halo, matrix, inner, half_sums, images, partial):
-    total = half_sums[...]
-    for xg, values in edge_terms(True, x_halo, z_halo, y_a, y_b, matrix):
-        for y in range(YB):
-            images[xg * YB + y] = inner[xg * YB + y] + values[y]
-        total = total + pair_sums([phi[xg * YB + y] for y in range(YB)], values)
-    partial[...] = jnp.concatenate([total[: NORB // 2], total[NORB // 2 :]], axis=1)
-
-
-def second_edge_kernel(y_a, y_b, x_halo, z_halo, matrix, before, images):
-    for xg, values in edge_terms(False, x_halo, z_halo, y_a, y_b, matrix):
-        for y in range(YB):
-            images[xg * YB + y] = before[xg * YB + y] + values[y]
+            left = split(jnp.concatenate([phi[xg * YB + y] for y in range(YB)], axis=1))
+            right = split(jnp.concatenate(values, axis=1))
+            total = total + three_products(left, right, (((1,), (1,)), ((), ())))
+    packed = jnp.concatenate([total[: NORB // 2], total[NORB // 2 :]], axis=1)
+    partial[...] = jnp.broadcast_to(packed[None], partial.shape)
+
+
+def sum_kernel(came, sent):
+    sent[...] = jnp.broadcast_to(jnp.sum(came[...], axis=0)[None], sent.shape)
 
 
 def update_kernel(phi, images, sums, inside, out):
     packed = jnp.sum(sums[...], axis=0)
     half = jnp.concatenate([packed[:, :NORB], packed[:, NORB:]], axis=0)
-    lag = (half + half.T) * jnp.float32(1.0 / CELLS)
+    lag = (half + half.T) * jnp.float32(0.5 / CELLS)
     squares = jnp.zeros((NORB, LANES), jnp.float32)
     for xg in range(XG):
         rows = [phi[xg * YB + y] for y in range(YB)]
@@ -251,10 +274,8 @@
     )
 
 
-def copies(value, axes):
-    peers = math.prod(lax.axis_size(a) for a in axes)
-    sent = jnp.broadcast_to(value[None], (peers,) + value.shape)
-    return lax.all_to_all(sent, axes, 0, 0, tiled=True)
+def exchange(value, axes):
+    return lax.all_to_all(value, axes, 0, 0, tiled=True)
 
 
 def shift(value, axes, count, up):
@@ -280,41 +301,53 @@
             mib,
             in_specs=[pl.BlockSpec(memory_space=pltpu.SMEM), vmem, vmem],
         )(place, potential, segments)
-    inner, ahead, behind = (jnp.asarray(m) for m in (inner_matrix(), edge_matrix(True), edge_matrix(False)))
-
+    inner, edge = inner_matrix(), edge_matrix()
+    edge_high = edge.astype(jnp.bfloat16)
+    edge_low = (edge - edge_high.astype(np.float64)).astype(jnp.bfloat16)
+
+    whole = f32(ROWS, NORB, LANES)
+    y_side, x_side, z_side = (f32(n, NORB, LANES) for n in (XG * REACH, 2 * YB, YB))
+    sides = [y_side, y_side, x_side, x_side, z_side, z_side]
+    far = pl.BlockSpec(memory_space=pltpu.HBM)
+    slots = [pltpu.VMEM(side.shape, jnp.float32) for side in sides] + [pltpu.SemaphoreType.DMA((6,))]
     with jax.named_scope("spread"):
-        side = [f32(2 * REACH, NORB, LANES)] * 2 + [f32(2 * YB, NORB, LANES), f32(YB, NORB, LANES)]
-        whole = f32(ROWS, NORB, LANES)
-        phi, *sides = call(spread_kernel, [whole] + side + side, "spread", 1 << 20, 6 * mib)(arrived)
-    y_up_a, y_down_b, x_up, z_up, *second = sides
-    with jax.named_scope("first_halo"):
-        y_up_a = shift(y_up_a, "z", 16, True)
-        y_down_b = shift(y_down_b, "z", 16, False)
+        phi, *sides = call(
+            spread_kernel,
+            [whole] + sides,
+            "spread",
+            1 << 20,
+            8 * mib,
+            out_specs=[vmem] + [far] * 6,
+            scratch_shapes=slots,
+        )(arrived)
+    y_up, y_down, x_up, x_down, z_up, z_down = sides
+    with jax.named_scope("halo"):
+        y_up = shift(y_up, "z", 16, True)
+        y_down = shift(y_down, "z", 16, False)
         x_up = shift(x_up, COMP, 8, True)
+        x_down = shift(x_down, COMP, 8, False)
         z_up = shift(z_up, "x", 4, True)
+        z_down = shift(z_down, "x", 4, False)
     with jax.named_scope("inner"):
-        images, sums = call(inner_kernel, [whole, f32(NORB, NORB)], "inner", 1 << 32, 2 * mib)(phi, diagonal, inner)
-    with jax.named_scope("first_edge"):
-        images, partial = call(first_edge_kernel, [whole, f32(NORB // 2, 2 * NORB)], "first_edge", 1 << 31, 4 * mib)(
-            phi, y_up_a, y_down_b, x_up, z_up, ahead, images, sums
-        )
-    partial, second = lax.optimization_barrier((partial, second))
-    y_down_a, y_up_b, x_down, z_down = second
+        images, sums = call(inner_kernel, [whole, f32(NORB, NORB)], "inner", 1 << 32, 2 * mib)(
+            phi, diagonal, jnp.asarray(inner)
+        )
+    with jax.named_scope("edge"):
+        images, partial = call(
+            edge_kernel,
+            [whole, f32(16, NORB // 2, 2 * NORB)],
+            "edge",
+            1 << 31,
+            6 * mib,
+            in_specs=[vmem] * 5 + [far] * 6,
+            scratch_shapes=slots,
+        )(phi, images, sums, jnp.asarray(edge_high), jnp.asarray(edge_low), y_up, y_down, x_up, x_down, z_up, z_down)
     with jax.named_scope("correlation_sum"):
-        partial = jnp.sum(copies(partial, ("x", "y")), axis=0)
-        partial = jnp.sum(copies(partial, ("core",)), axis=0)
-    with jax.named_scope("second_halo"):
-        y_down_a = shift(y_down_a, "z", 16, False)
-        y_up_b = shift(y_up_b, "z", 16, True)
-        x_down = shift(x_down, COMP, 8, False)
-        z_down = shift(z_down, "x", 4, False)
-    partial, y_down_a, y_up_b, x_down, z_down = lax.optimization_barrier((partial, y_down_a, y_up_b, x_down, z_down))
-    with jax.named_scope("correlation_sum"):
-        partial = copies(partial, ("z",))
-    with jax.named_scope("second_edge"):
-        images = call(second_edge_kernel, whole, "second_edge", 1 << 31, 4 * mib)(
-            y_down_a, y_up_b, x_down, z_down, behind, images
-        )
+        partial = exchange(partial, ("x", "y"))
+        partial = call(sum_kernel, f32(2, NORB // 2, 2 * NORB), "sum_plane", 1 << 16, mib)(partial)
+        partial = exchange(partial, ("core",))
+        partial = call(sum_kernel, f32(16, NORB // 2, 2 * NORB), "sum_chip", 1 << 16, mib)(partial)
+        partial = exchange(partial, ("z",))
     with jax.named_scope("update"):
         sent = call(update_kernel, f32(NORB * (ROWS + 1), LANES), "update", 1 << 28, 3 * mib)(
             phi, images, partial, inside
@@ -323,7 +356,8 @@
         back = lax.all_to_all(sent.reshape(NORB, ROWS + 1, 1, LANES), ORB, 0, 0, tiled=True)
     with jax.named_scope("rms"):
         slab = jnp.sum(back[:, ROWS, 0, :], axis=0)
-        squares = jnp.sum(copies(slab, COMP), axis=0)[:NORB]
+        sent = jnp.broadcast_to(slab, (8, 1, LANES))
+        squares = jnp.sum(exchange(sent, COMP), axis=(0, 1))[:NORB]
         grad_rms = jnp.sqrt(squares / CELLS)
     with jax.named_scope("unpack"):
         new = call(unpack_kernel, f32(16, NY, NZ), "unpack", 1 << 20, 2 * mib)(back.reshape(NORB * (ROWS + 1), LANES))

time: 241 us -> 227 us (0.942)
  blocking collectives: 152 us -> 172 us
  starting transfers between devices: 41.4 us -> 29.8 us
  waiting for transfers between devices: 13 us -> 2.62 us
  local copies, waits for them, and re-layouts: 11.3 us -> 3.73 us
  Pallas kernels: 19.9 us -> 16.5 us
    all_to_all x2 -> x3, blocking collectives: 19 us -> 39.4 us  [exchange(): return lax.all_to_all(value, axes, 0, 0, tiled=True)]
    all_to_all x2 -> x1, starting transfers between devices: 16 us -> 7.92 us  [exchange(): return lax.all_to_all(value, axes, 0, 0, tiled=True)]
    all_to_all x2 -> x1, waiting for transfers between devices: 10.3 us -> 2.6 us  [exchange(): return lax.all_to_all(value, axes, 0, 0, tiled=True)]
    unnamed x32 -> x14, local copies, waits for them, and re-layouts: 9.92 us -> 3.13 us
    ppermute x8 -> x6, starting transfers between devices: 25.4 us -> 21.9 us  [shift(): return lax.ppermute(value, axes, pairs)]
    pallas_call x3 -> x4, Pallas kernels: 10.3 us -> 6.95 us  [the longest x1 4.4 us: on_device(): call(edge_kernel, [whole, f32(16, NORB // 2, 2 * NORB)], 'edge', 1 << 31,...]
    ppermute x8 -> x6, waiting for transfers between devices: 2.71 us -> 0.02 us  [shift(): return lax.ppermute(value, axes, pairs)]
  transfers between devices with their start and end apart: 10 -> 7, of which waited for: 3 -> 1; matrix products, arithmetic and copies ran while one was open for 0% -> 0% of each run, Pallas kernels for 4% -> 3%
where the time goes in v3:
time: 227 us; the launch traced here: 226 us
  blocking collectives  172 us (76%)
  starting transfers between devices  29.8 us (13%)
  Pallas kernels  16.5 us (7%)
  local copies, waits for them, and re-layouts  3.73 us (2%)
  waiting for transfers between devices  2.62 us (1%)
    all_to_all x1, blocking collectives, on_device(): lax.all_to_all(pieces, ORB, 0, 0, tiled=True).reshape(NORB * ROWS, LANES)  69.4 us
    all_to_all x1, blocking collectives, on_device(): lax.all_to_all(sent.reshape(NORB, ROWS + 1, 1, LANES), ORB, 0, 0, tiled=T...  63.4 us
    all_to_all x3, blocking collectives, exchange(): return lax.all_to_all(value, axes, 0, 0, tiled=True)  39.4 us
    ppermute x6, starting transfers between devices, shift(): return lax.ppermute(value, axes, pairs)  21.9 us
    all_to_all x1, starting transfers between devices, exchange(): return lax.all_to_all(value, axes, 0, 0, tiled=True)  7.92 us
    pallas_call x1, Pallas kernels, on_device(): call(inner_kernel, [whole, f32(NORB, NORB)], 'inner', 1 << 32, 2 * mib)  4.65 us
  transfers between devices with their start and end apart: 7, of which 1 were waited for; matrix products, arithmetic and copies ran while one was open for 0% of the time, Pallas kernels for 3%

profile of v3, /device:TPU:1, one launch (start us, length us, event | category | flops | bytes accessed | tf_op | source)
XLA Modules:
  0.0 226.3 jit_solution(13021770986041930797)
XLA Ops:
  0.6 1.2 copy-done
  1.9 0.9 pack.1
  2.8 69.4 %all_to_all.30 = f32[64,32,128]{2,1,0:T(8,128)S(1)} all-to-all(f32[64,32,128]{2,1,0:T(8,128)S(1)} %pack.1), channel_id=1, replica_groups=mesh['x'=4,'z'=16,'y'=4,'core'=2] {'x','z'}, dimensions={0} | all-to-all | bytes 2097152 | tf_op jit(solution)/shard_map/transpose/all_to_all | solution.py:291
  72.1 2.5 %spread.1 = (f32[32,64,128]{2,1,0:T(8,128)S(1)}, f32[28,64,128]{2,1,0:T(8,128)}, f32[28,64,128]{2,1,0:T(8,128)}, f32[16,64,128]{2,1,0:T(8,128)}, f32[16,64,128]{...) custom-call(f32[2048,128]{1,0:T(8,128)S(1)} %bitcast.10), custom_call_target="tpu_custom_call" | custom-call | flops 1048576 | bytes 8388608 | tf_op jit(solution)/shard_map/spread/spread/pallas_call | solution.py:314
  74.6 0.7 copy-done.3
  75.3 1.3 collective-permute-start
  76.6 6.5 %collective-permute-start.1 = (f32[28,64,128]{2,1,0:T(8,128)}, f32[28,64,128]{2,1,0:T(8,128)}, u32[]{:S(2)}, u32[]{:S(2)}) collective-permute-start(f32[28,64,128]{2,1,0:T(8,128)} %get-tuple-element.20), channel_id=1, source_target_pairs={{0,8},{8,16},{16,24},{24,32},{32,40},{40,48},{48,56},{56,64},{64,7... | collective-permute-start | bytes 2752520 | tf_op jit(solution)/shard_map/halo/ppermute | solution.py:283
  83.1 1.3 collective-permute-start.4
  84.4 5.4 %collective-permute-start.2 = (f32[16,64,128]{2,1,0:T(8,128)}, f32[16,64,128]{2,1,0:T(8,128)S(1)}, u32[]{:S(2)}, u32[]{:S(2)}) collective-permute-start(f32[16,64,128]{2,1,0:T(8,128)} %get-tuple-element.21), channel_id=1, source_target_pairs={{1,0},{2,1},{3,2},{4,3},{5,4},{6,5},{7,6},{9,8},{10,9},{11,10},{12... | collective-permute-start | bytes 1572872 | tf_op jit(solution)/shard_map/halo/ppermute | solution.py:283
  89.8 3.1 %collective-permute-start.3 = (f32[16,64,128]{2,1,0:T(8,128)}, f32[16,64,128]{2,1,0:T(8,128)}, u32[]{:S(2)}, u32[]{:S(2)}) collective-permute-start(f32[16,64,128]{2,1,0:T(8,128)} %get-tuple-element.22), channel_id=1, source_target_pairs={{0,1},{1,2},{2,3},{3,4},{4,5},{5,6},{6,7},{8,9},{9,10},{10,11},{11... | collective-permute-start | bytes 1572872 | tf_op jit(solution)/shard_map/halo/ppermute | solution.py:283
  93.0 0.9 constants.1
  93.9 4.3 %collective-permute-start.5 = (f32[8,64,128]{2,1,0:T(8,128)}, f32[8,64,128]{2,1,0:T(8,128)S(1)}, u32[]{:S(2)}, u32[]{:S(2)}) collective-permute-start(f32[8,64,128]{2,1,0:T(8,128)} %copy-done.3), channel_id=1, source_target_pairs={{0,128},{128,256},{256,384},{1,129},{129,257},{257,385},{2,130},{1... | collective-permute-start | bytes 786440 | tf_op jit(solution)/shard_map/halo/ppermute | solution.py:283
  98.2 1.2 copy-done.4
  99.5 4.7 %inner.1 = (f32[32,64,128]{2,1,0:T(8,128)S(1)}, f32[64,64]{1,0:T(8,128)S(1)}) custom-call(f32[32,64,128]{2,1,0:T(8,128)S(1)} %get-tuple-element.15.phi, f32[32,128]{1,0:T(8,128)S(1)} %get-tuple-element.16.diagonal, f32[512,512]{1,0:T(8,128)S(1)} %copy-done.4), custom_call_target="tpu_custom_call" | custom-call | flops 4294967296 | bytes 2097152 | tf_op jit(solution)/shard_map/inner/inner/pallas_call | solution.py:332
  104.2 4.4 %edge.1 = (f32[32,64,128]{2,1,0:T(8,128)S(1)}, f32[16,32,128]{2,1,0:T(8,128)S(1)}) custom-call(f32[32,64,128]{2,1,0:T(8,128)S(1)} %get-tuple-element.15.phi, f32[32,64,128]{2,1,0:T(8,128)S(1)} %get-tuple-element.17.inner, f32[64,64]{1,0:T(8,128)S(1)} %get-tuple-element.18.sums, bf16[512,512]{1,0:T(8,128)(2,1)S(1)} %copy-done.6, ...), custom_call_target="tpu_custom_call" | custom-call | flops 2147483648 | bytes 6291456 | tf_op jit(solution)/shard_map/edge/edge/pallas_call | solution.py:336
  108.6 15.8 %all_to_all.31.came = f32[16,32,128]{2,1,0:T(8,128)S(1)} all-to-all(f32[16,32,128]{2,1,0:T(8,128)S(1)} %get-tuple-element.26), channel_id=1, replica_groups=mesh['x'=4,'z'=16,'y'=4,'core'=2] {'x','y'}, dimensions={0} | all-to-all | bytes 524288 | tf_op jit(solution)/shard_map/correlation_sum/all_to_all | solution.py:278
  124.5 5.4 %all_to_all.32.came = f32[2,32,128]{2,1,0:T(8,128)S(1)} all-to-all(f32[2,32,128]{2,1,0:T(8,128)S(1)} %sum_plane.1), channel_id=1, replica_groups=mesh['x'=4,'z'=16,'y'=4,'core'=2] {'core'}, dimensions={0} | all-to-all | bytes 65536 | tf_op jit(solution)/shard_map/correlation_sum/all_to_all | solution.py:278
  129.9 18.2 %all_to_all.33.sums = f32[16,32,128]{2,1,0:T(8,128)S(1)} all-to-all(f32[16,32,128]{2,1,0:T(8,128)S(1)} %sum_chip.1), channel_id=1, replica_groups=mesh['x'=4,'z'=16,'y'=4,'core'=2] {'z'}, dimensions={0} | all-to-all | bytes 524288 | tf_op jit(solution)/shard_map/correlation_sum/all_to_all | solution.py:278
  148.1 1.3 update.1
  149.3 63.4 %all_to_all.34 = f32[64,33,1,128]{3,2,1,0:T(1,128)S(1)} all-to-all(f32[64,33,1,128]{3,2,1,0:T(1,128)S(1)} %bitcast.9), channel_id=1, replica_groups=mesh['x'=4,'z'=16,'y'=4,'core'=2] {'x','z'}, dimensions={0} | all-to-all | bytes 2162688 | tf_op jit(solution)/shard_map/transpose_back/all_to_all | solution.py:356
  212.8 0.6 broadcast_in_dim.7
  213.4 7.9 %all-to-all-start.5 = ((f32[8,1,128]{2,1,0:T(1,128)}), f32[8,1,128]{2,1,0:T(1,128)S(1)}, u32[]{:S(2)}, u32[]{:S(2)}) async-start(f32[8,1,128]{2,1,0:T(1,128)} %broadcast_in_dim.7), calls=%async_computation.5 | async-start | bytes 8192 | tf_op jit(solution)/shard_map/rms/all_to_all | solution.py:278
  221.3 1.8 unpack.1
  223.2 2.6 %all-to-all-done.5 = f32[8,1,128]{2,1,0:T(1,128)S(1)} async-done(((f32[8,1,128]{2,1,0:T(1,128)}), f32[8,1,128]{2,1,0:T(1,128)S(1)}, u32[]{:S(2)}, u32[]{:S(2)}) %all-to-all-start.5) | async-done | bytes 4128 | tf_op jit(solution)/shard_map/rms/all_to_all | solution.py:278
  (23 shorter events, 0.8 us)
Async XLA Ops:
  0.6 1.2 copy-start
  2.7 90.3 %copy-start.1 = (f32[16,128,128]{2,1,0:T(8,128)S(1)}, f32[16,128,128]{2,1,0:T(8,128)}, u32[]{:S(2)}) copy-start(f32[16,128,128]{2,1,0:T(8,128)} %potential.1) | copy-start | bytes 3145732
  2.7 90.3 %copy-start.2 = (s32[2,16,128]{2,1,0:T(8,128)S(1)}, s32[2,16,128]{2,1,0:T(8,128)}, u32[]{:S(2)}) copy-start(s32[2,16,128]{2,1,0:T(8,128)} %segments.1) | copy-start | bytes 49156
  74.6 0.7 copy-start.3
  75.3 28.8 %collective-permute-start = (f32[28,64,128]{2,1,0:T(8,128)}, f32[28,64,128]{2,1,0:T(8,128)S(1)}, u32[]{:S(2)}, u32[]{:S(2)}) collective-permute-start(f32[28,64,128]{2,1,0:T(8,128)} %get-tuple-element.19), channel_id=1, source_target_pairs={{8,0},{16,8},{24,16},{32,24},{40,32},{48,40},{56,48},{64,56},{72,6... | collective-permute-start | bytes 2752520 | tf_op jit(solution)/shard_map/halo/ppermute | solution.py:283
  76.6 27.6 %collective-permute-start.1 = (f32[28,64,128]{2,1,0:T(8,128)}, f32[28,64,128]{2,1,0:T(8,128)}, u32[]{:S(2)}, u32[]{:S(2)}) collective-permute-start(f32[28,64,128]{2,1,0:T(8,128)} %get-tuple-element.20), channel_id=1, source_target_pairs={{0,8},{8,16},{16,24},{24,32},{32,40},{40,48},{48,56},{56,64},{64,7... | collective-permute-start | bytes 2752520 | tf_op jit(solution)/shard_map/halo/ppermute | solution.py:283
  83.1 10.8 %collective-permute-start.4 = (f32[8,64,128]{2,1,0:T(8,128)}, f32[8,64,128]{2,1,0:T(8,128)}, u32[]{:S(2)}, u32[]{:S(2)}) collective-permute-start(f32[8,64,128]{2,1,0:T(8,128)} %get-tuple-element.23), channel_id=1, source_target_pairs={{128,0},{256,128},{384,256},{129,1},{257,129},{385,257},{130,2},{2... | collective-permute-start | bytes 786440 | tf_op jit(solution)/shard_map/halo/ppermute | solution.py:283
  84.4 19.7 %collective-permute-start.2 = (f32[16,64,128]{2,1,0:T(8,128)}, f32[16,64,128]{2,1,0:T(8,128)S(1)}, u32[]{:S(2)}, u32[]{:S(2)}) collective-permute-start(f32[16,64,128]{2,1,0:T(8,128)} %get-tuple-element.21), channel_id=1, source_target_pairs={{1,0},{2,1},{3,2},{4,3},{5,4},{6,5},{7,6},{9,8},{10,9},{11,10},{12... | collective-permute-start | bytes 1572872 | tf_op jit(solution)/shard_map/halo/ppermute | solution.py:283
  89.8 14.3 %collective-permute-start.3 = (f32[16,64,128]{2,1,0:T(8,128)}, f32[16,64,128]{2,1,0:T(8,128)}, u32[]{:S(2)}, u32[]{:S(2)}) collective-permute-start(f32[16,64,128]{2,1,0:T(8,128)} %get-tuple-element.22), channel_id=1, source_target_pairs={{0,1},{1,2},{2,3},{3,4},{4,5},{5,6},{6,7},{8,9},{9,10},{10,11},{11... | collective-permute-start | bytes 1572872 | tf_op jit(solution)/shard_map/halo/ppermute | solution.py:283
  93.9 10.2 %collective-permute-start.5 = (f32[8,64,128]{2,1,0:T(8,128)}, f32[8,64,128]{2,1,0:T(8,128)S(1)}, u32[]{:S(2)}, u32[]{:S(2)}) collective-permute-start(f32[8,64,128]{2,1,0:T(8,128)} %copy-done.3), channel_id=1, source_target_pairs={{0,128},{128,256},{256,384},{1,129},{129,257},{257,385},{2,130},{1... | collective-permute-start | bytes 786440 | tf_op jit(solution)/shard_map/halo/ppermute | solution.py:283
  98.2 1.2 copy-start.4
  99.5 4.7 %copy-start.5 = (bf16[512,512]{1,0:T(8,128)(2,1)S(1)}, bf16[512,512]{1,0:T(8,128)(2,1)}, u32[]{:S(2)}) copy-start(bf16[512,512]{1,0:T(8,128)(2,1)} %constant.24.clone.low) | copy-start | bytes 1572868
  99.5 4.7 %copy-start.6 = (bf16[512,512]{1,0:T(8,128)(2,1)S(1)}, bf16[512,512]{1,0:T(8,128)(2,1)}, u32[]{:S(2)}) copy-start(bf16[512,512]{1,0:T(8,128)(2,1)} %constant.23.clone.high) | copy-start | bytes 1572868
  213.4 12.4 %all-to-all-start.5 = ((f32[8,1,128]{2,1,0:T(1,128)}), f32[8,1,128]{2,1,0:T(1,128)S(1)}, u32[]{:S(2)}, u32[]{:S(2)}) async-start(f32[8,1,128]{2,1,0:T(1,128)} %broadcast_in_dim.7), calls=%async_computation.5 | async-start | bytes 8192 | tf_op jit(solution)/shard_map/rms/all_to_all | solution.py:278

commit v4 on v3

--- a/solution.py
+++ b/solution.py
@@ -1,3 +1,4 @@
+import functools
 import math
 
 import jax
@@ -17,6 +18,7 @@
 REACH = 7
 XG, YB, XL, ZB = 4, 8, 4, 32
 ROWS, LANES = XG * YB, XL * ZB
+FOLD, SLOT = 17, 24
 HIGH = lax.Precision.HIGHEST
 PARAMS = pltpu.CompilerParams(vmem_limit_bytes=12 * 1024 * 1024)
 ORB, COMP = ("x", "z"), ("y", "core")
@@ -110,27 +112,24 @@
     y_up, y_down, x_up, x_down, z_up, z_down = kept
     moves = [pltpu.make_async_copy(kept[i], sent[i], sems.at[i]) for i in range(6)]
     slot = (lax.broadcasted_iota(jnp.int32, (NORB, LANES), 1) % ZB) // 8
-    for y in range(YB):
-        up = down = jnp.zeros((NORB, LANES), jnp.float32)
-        for xg in range(XG):
+    for xg in range(XG):
+        x_side = x_up if xg < 2 else x_down
+        for y in range(YB):
             r = xg * YB + y
             row = src[pl.ds(r, NORB, stride=ROWS), :]
             phi[r] = row
+            x_side[xg % 2 * YB + y] = row
             if y < REACH:
                 y_up[xg * REACH + y] = row
             if y >= 1:
                 y_down[xg * REACH + y - 1] = row
-            if xg < 2:
-                x_up[r] = row
-            else:
-                x_down[r - 2 * YB] = row
-            up = jnp.where(slot == xg, pltpu.roll(row, xg * 8, 1) if xg else row, up)
-            down = jnp.where(slot == xg, pltpu.roll(row, (xg * 8 - 24) % LANES, 1) if xg != 3 else row, down)
-        z_up[y] = up
-        z_down[y] = down
-        if y == REACH - 1:
-            moves[0].start()
-    for i in range(1, 6):
+            up = pltpu.roll(row, xg * 8, 1) if xg else row
+            down = pltpu.roll(row, (xg * 8 - 24) % LANES, 1) if xg != 3 else row
+            z_up[y] = jnp.where(slot == xg, up, z_up[y]) if xg else up
+            z_down[y] = jnp.where(slot == xg, down, z_down[y]) if xg else down
+        if xg == 1:
+            moves[2].start()
+    for i in (0, 1, 3, 4, 5):
         moves[i].start()
     for move in moves:
         move.wait()
@@ -199,14 +198,44 @@
     sums[...] = total
 
 
+def fold(table):
+    n = NORB // 2
+    above = lax.broadcasted_iota(jnp.int32, (n, n), 0) - lax.broadcasted_iota(jnp.int32, (n, n), 1)
+    last = table[n:, n:]
+    corner = table[:n, n:]
+    mixed = jnp.where(above <= 0, table[:n, :n], last)
+    diagonal = jnp.sum(jnp.where(above == 0, last, 0.0), axis=0, keepdims=True)
+    top = jnp.concatenate([corner[: n // 2], corner[n // 2 :], mixed[: n // 2], mixed[n // 2 :]], axis=1)
+    bottom = jnp.concatenate([diagonal, jnp.zeros((1, LANES - n), jnp.float32)], axis=1)
+    return top, bottom
+
+
+def unfold(top, bottom):
+    n = NORB // 2
+    above = lax.broadcasted_iota(jnp.int32, (n, n), 0) - lax.broadcasted_iota(jnp.int32, (n, n), 1)
+    corner = jnp.concatenate([top[:, :n], top[:, n : 2 * n]], axis=0)
+    mixed = jnp.concatenate([top[:, 2 * n : 3 * n], top[:, 3 * n :]], axis=0)
+    turned = mixed.T
+    first = jnp.where(above <= 0, mixed, turned)
+    last = jnp.where(above > 0, mixed, jnp.where(above == 0, bottom[:, :n], turned))
+    left = jnp.concatenate([first, corner.T], axis=0)
+    right = jnp.concatenate([corner, last], axis=0)
+    return jnp.concatenate([left, right], axis=1)
+
+
+def arrive(came, kept, sems):
+    moves = [pltpu.make_async_copy(came[i], kept[i], sems.at[i]) for i in range(len(came))]
+    for move in moves:
+        move.start()
+    return moves
+
+
 def edge_kernel(phi, inner, sums, high, low, *refs):
     came, images, partial, kept, sems = refs[:6], refs[6], refs[7], refs[8:14], refs[14]
     y_up, y_down, x_up, x_down, z_up, z_down = kept
-    moves = [pltpu.make_async_copy(came[i], kept[i], sems.at[i]) for i in range(6)]
-    for move in moves:
-        move.start()
-    for move in moves:
-        move.wait()
+    moves = arrive(came, kept, sems)
+    for i in (2, 3, 4, 5, 0, 1):
+        moves[i].wait()
     total = sums[...]
     z_halo = [z_up[...].reshape(YB * NORB, LANES), z_down[...].reshape(YB * NORB, LANES)]
     for pair in range(2):
@@ -231,18 +260,31 @@
             left = split(jnp.concatenate([phi[xg * YB + y] for y in range(YB)], axis=1))
             right = split(jnp.concatenate(values, axis=1))
             total = total + three_products(left, right, (((1,), (1,)), ((), ())))
-    packed = jnp.concatenate([total[: NORB // 2], total[NORB // 2 :]], axis=1)
-    partial[...] = jnp.broadcast_to(packed[None], partial.shape)
-
-
-def sum_kernel(came, sent):
-    sent[...] = jnp.broadcast_to(jnp.sum(came[...], axis=0)[None], sent.shape)
+    top, bottom = fold(total + total.T)
+    rest = jnp.zeros((SLOT - FOLD, LANES), jnp.float32)
+    for i in range(2):
+        partial[i * SLOT : (i + 1) * SLOT, :] = jnp.concatenate([top, bottom, rest], axis=0)
+
+
+def added(came, count):
+    size = came.shape[0] // count
+    top = came[0 : FOLD - 1, :]
+    bottom = came[FOLD - 1 : FOLD, :]
+    for i in range(1, count):
+        top = top + came[i * size : i * size + FOLD - 1, :]
+        bottom = bottom + came[i * size + FOLD - 1 : i * size + FOLD, :]
+    return top, bottom
+
+
+def sum_kernel(count, came, sent):
+    top, bottom = added(came, count)
+    for i in range(sent.shape[0] // FOLD):
+        sent[i * FOLD : i * FOLD + FOLD - 1, :] = top
+        sent[i * FOLD + FOLD - 1 : (i + 1) * FOLD, :] = bottom
 
 
 def update_kernel(phi, images, sums, inside, out):
-    packed = jnp.sum(sums[...], axis=0)
-    half = jnp.concatenate([packed[:, :NORB], packed[:, NORB:]], axis=0)
-    lag = (half + half.T) * jnp.float32(0.5 / CELLS)
+    lag = unfold(*added(sums, 16)) * jnp.float32(0.5 / CELLS)
     squares = jnp.zeros((NORB, LANES), jnp.float32)
     for xg in range(XG):
         rows = [phi[xg * YB + y] for y in range(YB)]
@@ -278,6 +320,11 @@
     return lax.all_to_all(value, axes, 0, 0, tiled=True)
 
 
+def exchange_folded(value, axes):
+    shape = value.shape
+    return exchange(value.reshape(shape[0] // FOLD, FOLD, 1, LANES), axes).reshape(shape)
+
+
 def shift(value, axes, count, up):
     pairs = [(i + 1, i) if up else (i, i + 1) for i in range(count - 1)]
     return lax.ppermute(value, axes, pairs)
@@ -309,18 +356,21 @@
     y_side, x_side, z_side = (f32(n, NORB, LANES) for n in (XG * REACH, 2 * YB, YB))
     sides = [y_side, y_side, x_side, x_side, z_side, z_side]
     far = pl.BlockSpec(memory_space=pltpu.HBM)
-    slots = [pltpu.VMEM(side.shape, jnp.float32) for side in sides] + [pltpu.SemaphoreType.DMA((6,))]
+
+    def slots(shapes):
+        return [pltpu.VMEM(one.shape, jnp.float32) for one in shapes] + [pltpu.SemaphoreType.DMA((len(shapes),))]
+
     with jax.named_scope("spread"):
-        phi, *sides = call(
+        phi, *sides_out = call(
             spread_kernel,
-            [whole] + sides,
+            [whole] + [pltpu.HBM(side.shape, jnp.float32) for side in sides],
             "spread",
             1 << 20,
             8 * mib,
             out_specs=[vmem] + [far] * 6,
-            scratch_shapes=slots,
+            scratch_shapes=slots(sides),
         )(arrived)
-    y_up, y_down, x_up, x_down, z_up, z_down = sides
+    y_up, y_down, x_up, x_down, z_up, z_down = sides_out
     with jax.named_scope("halo"):
         y_up = shift(y_up, "z", 16, True)
         y_down = shift(y_down, "z", 16, False)
@@ -335,19 +385,19 @@
     with jax.named_scope("edge"):
         images, partial = call(
             edge_kernel,
-            [whole, f32(16, NORB // 2, 2 * NORB)],
+            [whole, f32(2 * SLOT, LANES)],
             "edge",
             1 << 31,
             6 * mib,
             in_specs=[vmem] * 5 + [far] * 6,
-            scratch_shapes=slots,
+            scratch_shapes=slots(sides),
         )(phi, images, sums, jnp.asarray(edge_high), jnp.asarray(edge_low), y_up, y_down, x_up, x_down, z_up, z_down)
     with jax.named_scope("correlation_sum"):
-        partial = exchange(partial, ("x", "y"))
-        partial = call(sum_kernel, f32(2, NORB // 2, 2 * NORB), "sum_plane", 1 << 16, mib)(partial)
-        partial = exchange(partial, ("core",))
-        partial = call(sum_kernel, f32(16, NORB // 2, 2 * NORB), "sum_chip", 1 << 16, mib)(partial)
-        partial = exchange(partial, ("z",))
+        partial = exchange(partial.reshape(2, SLOT, LANES), ("core",)).reshape(2 * SLOT, LANES)
+        partial = call(functools.partial(sum_kernel, 2), f32(16 * FOLD, LANES), "sum_chip", 1 << 16, mib)(partial)
+        partial = exchange_folded(partial, ("x", "y"))
+        partial = call(functools.partial(sum_kernel, 16), f32(16 * FOLD, LANES), "sum_plane", 1 << 16, mib)(partial)
+        partial = exchange_folded(partial, ("z",))
     with jax.named_scope("update"):
         sent = call(update_kernel, f32(NORB * (ROWS + 1), LANES), "update", 1 << 28, 3 * mib)(
             phi, images, partial, inside

time: 227 us -> 218 us (0.960)
  blocking collectives: 172 us -> 162 us
    all_to_all x1, blocking collectives: 63.4 us -> 56.9 us  [on_device(): lax.all_to_all(sent.reshape(NORB, ROWS + 1, 1, LANES), ORB, 0, 0, tiled=T...]
    all_to_all x3, blocking collectives: 39.4 us -> 35.4 us  [exchange(): return lax.all_to_all(value, axes, 0, 0, tiled=True)]
where the time goes in v4:
time: 218 us; the launch traced here: 217 us
  blocking collectives  162 us (74%)
  starting transfers between devices  31.7 us (15%)
  Pallas kernels  16.7 us (8%)
  local copies, waits for them, and re-layouts  3.05 us (1%)
  waiting for transfers between devices  2.77 us (1%)
    all_to_all x1, blocking collectives, on_device(): lax.all_to_all(pieces, ORB, 0, 0, tiled=True).reshape(NORB * ROWS, LANES)  69.4 us
    all_to_all x1, blocking collectives, on_device(): lax.all_to_all(sent.reshape(NORB, ROWS + 1, 1, LANES), ORB, 0, 0, tiled=T...  56.9 us
    all_to_all x3, blocking collectives, exchange(): return lax.all_to_all(value, axes, 0, 0, tiled=True)  35.4 us
    ppermute x6, starting transfers between devices, shift(): return lax.ppermute(value, axes, pairs)  21.9 us
    all_to_all x1, starting transfers between devices, exchange(): return lax.all_to_all(value, axes, 0, 0, tiled=True)  9.78 us
    pallas_call x1, Pallas kernels, on_device(): call(inner_kernel, [whole, f32(NORB, NORB)], 'inner', 1 << 32, 2 * mib)  4.65 us
    pallas_call x1, Pallas kernels, on_device(): call(edge_kernel, [whole, f32(2 * SLOT, LANES)], 'edge', 1 << 31, 6 * mib...  4.52 us
  transfers between devices with their start and end apart: 7, of which 1 were waited for; matrix products, arithmetic and copies ran while one was open for 0% of the time, Pallas kernels for 3%

profile of v4, /device:TPU:1, one launch (start us, length us, event | category | flops | bytes accessed | tf_op | source)
XLA Modules:
  0.0 217.4 jit_solution(16434905683921551360)
XLA Ops:
  0.6 1.2 copy-done
  1.9 0.9 pack.1
  2.8 69.4 %all_to_all.30 = f32[64,32,128]{2,1,0:T(8,128)S(1)} all-to-all(f32[64,32,128]{2,1,0:T(8,128)S(1)} %pack.1), channel_id=1, replica_groups=mesh['x'=4,'z'=16,'y'=4,'core'=2] {'x','z'}, dimensions={0} | all-to-all | bytes 2097152 | tf_op jit(solution)/shard_map/transpose/all_to_all | solution.py:338
  72.1 2.5 %spread.1 = (f32[32,64,128]{2,1,0:T(8,128)S(1)}, f32[28,64,128]{2,1,0:T(8,128)}, f32[28,64,128]{2,1,0:T(8,128)}, f32[16,64,128]{2,1,0:T(8,128)}, f32[16,64,128]{...) custom-call(f32[2048,128]{1,0:T(8,128)S(1)} %bitcast.16), custom_call_target="tpu_custom_call" | custom-call | flops 1048576 | bytes 8388608 | tf_op jit(solution)/shard_map/spread/spread/pallas_call | solution.py:364
  74.6 1.3 collective-permute-start
  75.9 6.5 %collective-permute-start.1 = (f32[28,64,128]{2,1,0:T(8,128)}, f32[28,64,128]{2,1,0:T(8,128)}, u32[]{:S(2)}, u32[]{:S(2)}) collective-permute-start(f32[28,64,128]{2,1,0:T(8,128)} %get-tuple-element.20), channel_id=1, source_target_pairs={{0,8},{8,16},{16,24},{24,32},{32,40},{40,48},{48,56},{56,64},{64,7... | collective-permute-start | bytes 2752520 | tf_op jit(solution)/shard_map/halo/ppermute | solution.py:330
  82.4 1.3 collective-permute-start.4
  83.7 5.4 %collective-permute-start.2 = (f32[16,64,128]{2,1,0:T(8,128)}, f32[16,64,128]{2,1,0:T(8,128)S(1)}, u32[]{:S(2)}, u32[]{:S(2)}) collective-permute-start(f32[16,64,128]{2,1,0:T(8,128)} %get-tuple-element.21), channel_id=1, source_target_pairs={{1,0},{2,1},{3,2},{4,3},{5,4},{6,5},{7,6},{9,8},{10,9},{11,10},{12... | collective-permute-start | bytes 1572872 | tf_op jit(solution)/shard_map/halo/ppermute | solution.py:330
  89.1 3.1 %collective-permute-start.3 = (f32[16,64,128]{2,1,0:T(8,128)}, f32[16,64,128]{2,1,0:T(8,128)}, u32[]{:S(2)}, u32[]{:S(2)}) collective-permute-start(f32[16,64,128]{2,1,0:T(8,128)} %get-tuple-element.22), channel_id=1, source_target_pairs={{0,1},{1,2},{2,3},{3,4},{4,5},{5,6},{6,7},{8,9},{9,10},{10,11},{11... | collective-permute-start | bytes 1572872 | tf_op jit(solution)/shard_map/halo/ppermute | solution.py:330
  92.3 0.9 constants.1
  93.2 4.3 %collective-permute-start.5 = (f32[8,64,128]{2,1,0:T(8,128)}, f32[8,64,128]{2,1,0:T(8,128)S(1)}, u32[]{:S(2)}, u32[]{:S(2)}) collective-permute-start(f32[8,64,128]{2,1,0:T(8,128)} %get-tuple-element.24), channel_id=1, source_target_pairs={{0,128},{128,256},{256,384},{1,129},{129,257},{257,385},{2,130},{1... | collective-permute-start | bytes 786440 | tf_op jit(solution)/shard_map/halo/ppermute | solution.py:330
  97.5 1.2 copy-done.3
  98.7 4.7 %inner.1 = (f32[32,64,128]{2,1,0:T(8,128)S(1)}, f32[64,64]{1,0:T(8,128)S(1)}) custom-call(f32[32,64,128]{2,1,0:T(8,128)S(1)} %get-tuple-element.15.phi, f32[32,128]{1,0:T(8,128)S(1)} %get-tuple-element.16.diagonal, f32[512,512]{1,0:T(8,128)S(1)} %copy-done.3), custom_call_target="tpu_custom_call" | custom-call | flops 4294967296 | bytes 2097152 | tf_op jit(solution)/shard_map/inner/inner/pallas_call | solution.py:382
  103.5 4.5 %edge.1 = (f32[32,64,128]{2,1,0:T(8,128)S(1)}, f32[48,128]{1,0:T(8,128)S(1)}) custom-call(f32[32,64,128]{2,1,0:T(8,128)S(1)} %get-tuple-element.15.phi, f32[32,64,128]{2,1,0:T(8,128)S(1)} %get-tuple-element.17.inner, f32[64,64]{1,0:T(8,128)S(1)} %get-tuple-element.18.sums, bf16[512,512]{1,0:T(8,128)(2,1)S(1)} %copy-done.5, bf16[512,512]{1,0:T(8,128)(2,1)S(1)} %copy-done.4, ...), custom_call_target="tpu_custom_call" | custom-call | flops 2147483648 | bytes 6291456 | tf_op jit(solution)/shard_map/edge/edge/pallas_call | solution.py:386
  108.0 4.3 %all_to_all.31 = f32[2,24,128]{2,1,0:T(8,128)S(1)} all-to-all(f32[2,24,128]{2,1,0:T(8,128)S(1)} %bitcast.23), channel_id=1, replica_groups=mesh['x'=4,'z'=16,'y'=4,'core'=2] {'core'}, dimensions={0} | all-to-all | bytes 49152 | tf_op jit(solution)/shard_map/correlation_sum/all_to_all | solution.py:320
  112.3 14.6 %all_to_all.32 = f32[16,17,1,128]{3,2,1,0:T(1,128)S(1)} all-to-all(f32[16,17,1,128]{3,2,1,0:T(1,128)S(1)} %bitcast.19), channel_id=1, replica_groups=mesh['x'=4,'z'=16,'y'=4,'core'=2] {'x','y'}, dimensions={0} | all-to-all | bytes 278528 | tf_op jit(solution)/shard_map/correlation_sum/all_to_all | solution.py:320
  126.9 16.5 %all_to_all.33 = f32[16,17,1,128]{3,2,1,0:T(1,128)S(1)} all-to-all(f32[16,17,1,128]{3,2,1,0:T(1,128)S(1)} %bitcast.21), channel_id=1, replica_groups=mesh['x'=4,'z'=16,'y'=4,'core'=2] {'z'}, dimensions={0} | all-to-all | bytes 278528 | tf_op jit(solution)/shard_map/correlation_sum/all_to_all | solution.py:320
  143.4 1.4 update.1
  144.8 56.9 %all_to_all.34 = f32[64,33,1,128]{3,2,1,0:T(1,128)S(1)} all-to-all(f32[64,33,1,128]{3,2,1,0:T(1,128)S(1)} %bitcast.15), channel_id=1, replica_groups=mesh['x'=4,'z'=16,'y'=4,'core'=2] {'x','z'}, dimensions={0} | all-to-all | bytes 2162688 | tf_op jit(solution)/shard_map/transpose_back/all_to_all | solution.py:406
  201.9 0.6 broadcast_in_dim.7
  202.5 9.8 %all-to-all-start.5 = ((f32[8,1,128]{2,1,0:T(1,128)}), f32[8,1,128]{2,1,0:T(1,128)S(1)}, u32[]{:S(2)}, u32[]{:S(2)}) async-start(f32[8,1,128]{2,1,0:T(1,128)} %broadcast_in_dim.7), calls=%async_computation.5 | async-start | bytes 8192 | tf_op jit(solution)/shard_map/rms/all_to_all | solution.py:320
  212.2 1.8 unpack.1
  214.1 2.7 %all-to-all-done.5 = f32[8,1,128]{2,1,0:T(1,128)S(1)} async-done(((f32[8,1,128]{2,1,0:T(1,128)}), f32[8,1,128]{2,1,0:T(1,128)S(1)}, u32[]{:S(2)}, u32[]{:S(2)}) %all-to-all-start.5) | async-done | bytes 4128 | tf_op jit(solution)/shard_map/rms/all_to_all | solution.py:320
  216.8 0.5 multiply_sqrt_fusion
  (21 shorter events, 0.3 us)
Async XLA Ops:
  0.6 1.2 copy-start
  2.7 89.6 %copy-start.1 = (f32[16,128,128]{2,1,0:T(8,128)S(1)}, f32[16,128,128]{2,1,0:T(8,128)}, u32[]{:S(2)}) copy-start(f32[16,128,128]{2,1,0:T(8,128)} %potential.1) | copy-start | bytes 3145732
  2.7 89.6 %copy-start.2 = (s32[2,16,128]{2,1,0:T(8,128)S(1)}, s32[2,16,128]{2,1,0:T(8,128)}, u32[]{:S(2)}) copy-start(s32[2,16,128]{2,1,0:T(8,128)} %segments.1) | copy-start | bytes 49156
  74.6 28.8 %collective-permute-start = (f32[28,64,128]{2,1,0:T(8,128)}, f32[28,64,128]{2,1,0:T(8,128)S(1)}, u32[]{:S(2)}, u32[]{:S(2)}) collective-permute-start(f32[28,64,128]{2,1,0:T(8,128)} %get-tuple-element.19), channel_id=1, source_target_pairs={{8,0},{16,8},{24,16},{32,24},{40,32},{48,40},{56,48},{64,56},{72,6... | collective-permute-start | bytes 2752520 | tf_op jit(solution)/shard_map/halo/ppermute | solution.py:330
  75.9 27.6 %collective-permute-start.1 = (f32[28,64,128]{2,1,0:T(8,128)}, f32[28,64,128]{2,1,0:T(8,128)}, u32[]{:S(2)}, u32[]{:S(2)}) collective-permute-start(f32[28,64,128]{2,1,0:T(8,128)} %get-tuple-element.20), channel_id=1, source_target_pairs={{0,8},{8,16},{16,24},{24,32},{32,40},{40,48},{48,56},{56,64},{64,7... | collective-permute-start | bytes 2752520 | tf_op jit(solution)/shard_map/halo/ppermute | solution.py:330
  82.4 10.8 %collective-permute-start.4 = (f32[8,64,128]{2,1,0:T(8,128)}, f32[8,64,128]{2,1,0:T(8,128)}, u32[]{:S(2)}, u32[]{:S(2)}) collective-permute-start(f32[8,64,128]{2,1,0:T(8,128)} %get-tuple-element.23), channel_id=1, source_target_pairs={{128,0},{256,128},{384,256},{129,1},{257,129},{385,257},{130,2},{2... | collective-permute-start | bytes 786440 | tf_op jit(solution)/shard_map/halo/ppermute | solution.py:330
  83.7 19.7 %collective-permute-start.2 = (f32[16,64,128]{2,1,0:T(8,128)}, f32[16,64,128]{2,1,0:T(8,128)S(1)}, u32[]{:S(2)}, u32[]{:S(2)}) collective-permute-start(f32[16,64,128]{2,1,0:T(8,128)} %get-tuple-element.21), channel_id=1, source_target_pairs={{1,0},{2,1},{3,2},{4,3},{5,4},{6,5},{7,6},{9,8},{10,9},{11,10},{12... | collective-permute-start | bytes 1572872 | tf_op jit(solution)/shard_map/halo/ppermute | solution.py:330
  89.1 14.3 %collective-permute-start.3 = (f32[16,64,128]{2,1,0:T(8,128)}, f32[16,64,128]{2,1,0:T(8,128)}, u32[]{:S(2)}, u32[]{:S(2)}) collective-permute-start(f32[16,64,128]{2,1,0:T(8,128)} %get-tuple-element.22), channel_id=1, source_target_pairs={{0,1},{1,2},{2,3},{3,4},{4,5},{5,6},{6,7},{8,9},{9,10},{10,11},{11... | collective-permute-start | bytes 1572872 | tf_op jit(solution)/shard_map/halo/ppermute | solution.py:330
  93.2 10.2 %collective-permute-start.5 = (f32[8,64,128]{2,1,0:T(8,128)}, f32[8,64,128]{2,1,0:T(8,128)S(1)}, u32[]{:S(2)}, u32[]{:S(2)}) collective-permute-start(f32[8,64,128]{2,1,0:T(8,128)} %get-tuple-element.24), channel_id=1, source_target_pairs={{0,128},{128,256},{256,384},{1,129},{129,257},{257,385},{2,130},{1... | collective-permute-start | bytes 786440 | tf_op jit(solution)/shard_map/halo/ppermute | solution.py:330
  97.5 1.2 copy-start.3
  98.7 4.7 %copy-start.4 = (bf16[512,512]{1,0:T(8,128)(2,1)S(1)}, bf16[512,512]{1,0:T(8,128)(2,1)}, u32[]{:S(2)}) copy-start(bf16[512,512]{1,0:T(8,128)(2,1)} %constant.24.clone.low) | copy-start | bytes 1572868
  98.7 4.7 %copy-start.5 = (bf16[512,512]{1,0:T(8,128)(2,1)S(1)}, bf16[512,512]{1,0:T(8,128)(2,1)}, u32[]{:S(2)}) copy-start(bf16[512,512]{1,0:T(8,128)(2,1)} %constant.23.clone.high) | copy-start | bytes 1572868
  202.5 14.4 %all-to-all-start.5 = ((f32[8,1,128]{2,1,0:T(1,128)}), f32[8,1,128]{2,1,0:T(1,128)S(1)}, u32[]{:S(2)}, u32[]{:S(2)}) async-start(f32[8,1,128]{2,1,0:T(1,128)} %broadcast_in_dim.7), calls=%async_computation.5 | async-start | bytes 8192 | tf_op jit(solution)/shard_map/rms/all_to_all | solution.py:320

commit v5 on v4

--- a/solution.py
+++ b/solution.py
@@ -18,7 +18,7 @@
 REACH = 7
 XG, YB, XL, ZB = 4, 8, 4, 32
 ROWS, LANES = XG * YB, XL * ZB
-FOLD, SLOT = 17, 24
+FOLD = 17
 HIGH = lax.Precision.HIGHEST
 PARAMS = pltpu.CompilerParams(vmem_limit_bytes=12 * 1024 * 1024)
 ORB, COMP = ("x", "z"), ("y", "core")
@@ -43,11 +43,14 @@
     return COEFS[k] if 1 <= k <= REACH else 0.0
 
 
-def inner_matrix():
-    x, z = 16, ZB
-    line_x = np.array([[coef(abs(i - j)) for j in range(x)] for i in range(x)])
-    line_z = np.array([[coef(abs(i - j)) for j in range(z)] for i in range(z)])
-    return (np.kron(line_x, np.eye(z)) + np.kron(np.eye(x), line_z)).astype(np.float32)
+def inner_blocks():
+    steps = np.arange(XL)[:, None] - np.arange(XL)[None, :]
+    line_z = np.array([[coef(abs(i - j)) for j in range(ZB)] for i in range(ZB)])
+    blocks = []
+    for shift_by in range(-2, 3):
+        line_x = np.array([[coef(abs(int(s) - shift_by * XL)) for s in row] for row in steps])
+        blocks.append(np.kron(line_x, np.eye(ZB)) + (np.kron(np.eye(XL), line_z) if shift_by == 0 else 0.0))
+    return np.stack(blocks).astype(np.float32)
 
 
 def edge_matrix():
@@ -77,9 +80,16 @@
     return product(left[0], right[0]) + (product(left[1], right[0]) + product(left[0], right[1]))
 
 
-def pack_kernel(src, dst):
+def pack_kernel(slab, dst, src, out, sems):
     group = lax.broadcasted_iota(jnp.int32, (32, LANES), 1) // ZB
-    for xg in range(XG):
+    comes, goes = [], []
+    for xg in range(XG):
+        layers, rows = pl.ds(xg * XL, XL), pl.ds(xg * YB, YB)
+        comes.append(pltpu.make_async_copy(slab.at[layers], src.at[layers], sems.at[0, xg]))
+        goes.append(pltpu.make_async_copy(out.at[:, rows], dst.at[:, rows], sems.at[1, xg]))
+        comes[xg].start()
+    for xg in range(XG):
+        comes[xg].wait()
         for part in range(4):
             rows = slice(part * 32, part * 32 + 32)
             layers = [src[xg * XL + x, rows, :] for x in range(XL)]
@@ -90,7 +100,10 @@
                         moved = pltpu.roll(layers[x], ((x - q) * ZB) % LANES, 1)
                         piece = jnp.where(group == x, moved, piece)
                 first = q * 16 + part * 4
-                dst[first : first + 4, xg * YB : (xg + 1) * YB, :] = piece.reshape(4, YB, LANES)
+                out[first : first + 4, xg * YB : (xg + 1) * YB, :] = piece.reshape(4, YB, LANES)
+        goes[xg].start()
+    for move in goes:
+        move.wait()
 
 
 def unpack_kernel(src, dst):
@@ -107,10 +120,28 @@
                 dst[xg * XL + x, yb * YB : (yb + 1) * YB, :] = layer
 
 
+def spread_y_kernel(src, *refs):
+    sent, kept, sems = refs[:2], refs[2:4], refs[4]
+    moves = []
+    for xg in range(XG):
+        rows = pl.ds(xg * REACH, REACH)
+        for y in range(YB):
+            row = src[pl.ds(xg * YB + y, NORB, stride=ROWS), :]
+            if y < REACH:
+                kept[0][xg * REACH + y] = row
+            if y >= 1:
+                kept[1][xg * REACH + y - 1] = row
+        for side in range(2):
+            moves.append(pltpu.make_async_copy(kept[side].at[rows], sent[side].at[rows], sems.at[xg, side]))
+            moves[-1].start()
+    for move in moves:
+        move.wait()
+
+
 def spread_kernel(src, phi, *refs):
-    sent, kept, sems = refs[:6], refs[6:12], refs[12]
-    y_up, y_down, x_up, x_down, z_up, z_down = kept
-    moves = [pltpu.make_async_copy(kept[i], sent[i], sems.at[i]) for i in range(6)]
+    sent, kept, sems = refs[:4], refs[4:8], refs[8]
+    x_up, x_down, z_up, z_down = kept
+    moves = [pltpu.make_async_copy(kept[i], sent[i], sems.at[i]) for i in range(4)]
     slot = (lax.broadcasted_iota(jnp.int32, (NORB, LANES), 1) % ZB) // 8
     for xg in range(XG):
         x_side = x_up if xg < 2 else x_down
@@ -119,18 +150,14 @@
             row = src[pl.ds(r, NORB, stride=ROWS), :]
             phi[r] = row
             x_side[xg % 2 * YB + y] = row
-            if y < REACH:
-                y_up[xg * REACH + y] = row
-            if y >= 1:
-                y_down[xg * REACH + y - 1] = row
             up = pltpu.roll(row, xg * 8, 1) if xg else row
             down = pltpu.roll(row, (xg * 8 - 24) % LANES, 1) if xg != 3 else row
             z_up[y] = jnp.where(slot == xg, up, z_up[y]) if xg else up
             z_down[y] = jnp.where(slot == xg, down, z_down[y]) if xg else down
         if xg == 1:
-            moves[2].start()
-    for i in (0, 1, 3, 4, 5):
-        moves[i].start()
+            moves[0].start()
+    for move in moves[1:]:
+        move.start()
     for move in moves:
         move.wait()
 
@@ -169,19 +196,19 @@
     return ref[xg * YB : (xg + 1) * YB].reshape(YB * NORB, LANES)
 
 
-def pair_sums(left, right):
-    left, right = jnp.concatenate(left, axis=1), jnp.concatenate(right, axis=1)
-    return lax.dot_general(
-        left, right, (((1,), (1,)), ((), ())), precision=HIGH, preferred_element_type=jnp.float32
-    )
-
-
-def inner_kernel(phi, diagonal, matrix, images, sums):
+def inner_kernel(phi, diagonal, blocks, images, sums):
     total = jnp.zeros((NORB, NORB), jnp.float32)
+    nothing = jnp.zeros((LANES, LANES), jnp.float32)
     for pair in range(2):
+        matrix = jnp.concatenate(
+            [
+                jnp.concatenate([blocks[to - xg + 2] if abs(to - xg) <= 2 else nothing for xg in range(XG)], axis=0)
+                for to in (2 * pair, 2 * pair + 1)
+            ],
+            axis=1,
+        )
         cells = jnp.concatenate([tall(phi, xg) for xg in range(XG)], axis=1)
-        columns = slice(pair * 2 * LANES, (pair + 1) * 2 * LANES)
-        both = jnp.dot(cells, matrix[:, columns], precision=HIGH, preferred_element_type=jnp.float32)
+        both = jnp.dot(cells, matrix, precision=HIGH, preferred_element_type=jnp.float32)
         for xg in (2 * pair, 2 * pair + 1):
             own = slice((xg % 2) * LANES, (xg % 2 + 1) * LANES)
             rows = [phi[xg * YB + y] for y in range(YB)]
@@ -194,7 +221,8 @@
                         value = value + COEFS[abs(other - y)] * rows[other]
                 images[r] = value
                 values.append(value)
-            total = total + pair_sums(rows, values)
+            left, right = split(jnp.concatenate(rows, axis=1)), split(jnp.concatenate(values, axis=1))
+            total = total + three_products(left, right, (((1,), (1,)), ((), ())))
     sums[...] = total
 
 
@@ -223,19 +251,8 @@
     return jnp.concatenate([left, right], axis=1)
 
 
-def arrive(came, kept, sems):
-    moves = [pltpu.make_async_copy(came[i], kept[i], sems.at[i]) for i in range(len(came))]
-    for move in moves:
-        move.start()
-    return moves
-
-
 def edge_kernel(phi, inner, sums, high, low, *refs):
-    came, images, partial, kept, sems = refs[:6], refs[6], refs[7], refs[8:14], refs[14]
-    y_up, y_down, x_up, x_down, z_up, z_down = kept
-    moves = arrive(came, kept, sems)
-    for i in (2, 3, 4, 5, 0, 1):
-        moves[i].wait()
+    y_up, y_down, x_up, x_down, z_up, z_down, images, partial = refs
     total = sums[...]
     z_halo = [z_up[...].reshape(YB * NORB, LANES), z_down[...].reshape(YB * NORB, LANES)]
     for pair in range(2):
@@ -261,9 +278,13 @@
             right = split(jnp.concatenate(values, axis=1))
             total = total + three_products(left, right, (((1,), (1,)), ((), ())))
     top, bottom = fold(total + total.T)
-    rest = jnp.zeros((SLOT - FOLD, LANES), jnp.float32)
-    for i in range(2):
-        partial[i * SLOT : (i + 1) * SLOT, :] = jnp.concatenate([top, bottom, rest], axis=0)
+    store_copies(partial, top, bottom)
+
+
+def store_copies(sent, top, bottom):
+    for i in range(sent.shape[0] // FOLD):
+        sent[i * FOLD : i * FOLD + FOLD - 1, :] = top
+        sent[i * FOLD + FOLD - 1 : (i + 1) * FOLD, :] = bottom
 
 
 def added(came, count):
@@ -277,14 +298,11 @@
 
 
 def sum_kernel(count, came, sent):
-    top, bottom = added(came, count)
-    for i in range(sent.shape[0] // FOLD):
-        sent[i * FOLD : i * FOLD + FOLD - 1, :] = top
-        sent[i * FOLD + FOLD - 1 : (i + 1) * FOLD, :] = bottom
+    store_copies(sent, *added(came, count))
 
 
 def update_kernel(phi, images, sums, inside, out):
-    lag = unfold(*added(sums, 16)) * jnp.float32(0.5 / CELLS)
+    lag = unfold(*added(sums, 32)) * jnp.float32(0.5 / CELLS)
     squares = jnp.zeros((NORB, LANES), jnp.float32)
     for xg in range(XG):
         rows = [phi[xg * YB + y] for y in range(YB)]
@@ -301,6 +319,11 @@
     out[pl.ds(ROWS, NORB, stride=ROWS + 1), :] = jnp.broadcast_to(sums[0:1, :], (NORB, LANES))
 
 
+def squares_kernel(src, sent):
+    rows = src[pl.ds(ROWS, NORB, stride=ROWS + 1), :]
+    sent[...] = jnp.broadcast_to(jnp.sum(rows, axis=0, keepdims=True), sent.shape)
+
+
 def f32(*shape):
     return jax.ShapeDtypeStruct(shape, jnp.float32)
 
@@ -332,14 +355,27 @@
 
 def on_device(orbitals, potential, segments):
     mib = 1 << 20
+    far, vmem = pl.BlockSpec(memory_space=pltpu.HBM), pl.BlockSpec(memory_space=pltpu.VMEM)
     with jax.named_scope("pack"):
-        pieces = call(pack_kernel, f32(NORB, ROWS, LANES), "pack", 1 << 20, 2 * mib)(orbitals[0])
+        pieces = call(
+            pack_kernel,
+            pltpu.HBM((NORB, ROWS, LANES), jnp.float32),
+            "pack",
+            1 << 20,
+            2 * mib,
+            in_specs=[far],
+            out_specs=far,
+            scratch_shapes=[
+                pltpu.VMEM((16, NY, NZ), jnp.float32),
+                pltpu.VMEM((NORB, ROWS, LANES), jnp.float32),
+                pltpu.SemaphoreType.DMA((2, XG)),
+            ],
+        )(pltpu.with_memory_space_constraint(orbitals[0], pltpu.HBM))
     with jax.named_scope("transpose"):
         arrived = lax.all_to_all(pieces, ORB, 0, 0, tiled=True).reshape(NORB * ROWS, LANES)
 
     with jax.named_scope("block_constants"):
         place = jnp.stack([lax.axis_index("x"), lax.axis_index("z")]).astype(jnp.int32)
-        vmem = pl.BlockSpec(memory_space=pltpu.VMEM)
         diagonal, inside = call(
             constants_kernel,
             [f32(ROWS, LANES)] * 2,
@@ -348,29 +384,37 @@
             mib,
             in_specs=[pl.BlockSpec(memory_space=pltpu.SMEM), vmem, vmem],
         )(place, potential, segments)
-    inner, edge = inner_matrix(), edge_matrix()
+        arrived, diagonal, inside = lax.optimization_barrier((arrived, diagonal, inside))
+    inner, edge = inner_blocks(), edge_matrix()
     edge_high = edge.astype(jnp.bfloat16)
     edge_low = (edge - edge_high.astype(np.float64)).astype(jnp.bfloat16)
 
     whole = f32(ROWS, NORB, LANES)
     y_side, x_side, z_side = (f32(n, NORB, LANES) for n in (XG * REACH, 2 * YB, YB))
     sides = [y_side, y_side, x_side, x_side, z_side, z_side]
-    far = pl.BlockSpec(memory_space=pltpu.HBM)
 
     def slots(shapes):
         return [pltpu.VMEM(one.shape, jnp.float32) for one in shapes] + [pltpu.SemaphoreType.DMA((len(shapes),))]
 
     with jax.named_scope("spread"):
-        phi, *sides_out = call(
+        y_up, y_down = call(
+            spread_y_kernel,
+            [pltpu.HBM(y_side.shape, jnp.float32)] * 2,
+            "spread_y",
+            1 << 20,
+            3 * mib,
+            out_specs=[far] * 2,
+            scratch_shapes=[pltpu.VMEM(y_side.shape, jnp.float32)] * 2 + [pltpu.SemaphoreType.DMA((XG, 2))],
+        )(arrived)
+        phi, x_up, x_down, z_up, z_down = call(
             spread_kernel,
-            [whole] + [pltpu.HBM(side.shape, jnp.float32) for side in sides],
+            [whole] + [pltpu.HBM(side.shape, jnp.float32) for side in sides[2:]],
             "spread",
             1 << 20,
-            8 * mib,
-            out_specs=[vmem] + [far] * 6,
-            scratch_shapes=slots(sides),
+            6 * mib,
+            out_specs=[vmem] + [far] * 4,
+            scratch_shapes=slots(sides[2:]),
         )(arrived)
-    y_up, y_down, x_up, x_down, z_up, z_down = sides_out
     with jax.named_scope("halo"):
         y_up = shift(y_up, "z", 16, True)
         y_down = shift(y_down, "z", 16, False)
@@ -385,32 +429,27 @@
     with jax.named_scope("edge"):
         images, partial = call(
             edge_kernel,
-            [whole, f32(2 * SLOT, LANES)],
+            [whole, f32(16 * FOLD, LANES)],
             "edge",
             1 << 31,
             6 * mib,
-            in_specs=[vmem] * 5 + [far] * 6,
-            scratch_shapes=slots(sides),
         )(phi, images, sums, jnp.asarray(edge_high), jnp.asarray(edge_low), y_up, y_down, x_up, x_down, z_up, z_down)
     with jax.named_scope("correlation_sum"):
-        partial = exchange(partial.reshape(2, SLOT, LANES), ("core",)).reshape(2 * SLOT, LANES)
-        partial = call(functools.partial(sum_kernel, 2), f32(16 * FOLD, LANES), "sum_chip", 1 << 16, mib)(partial)
-        partial = exchange_folded(partial, ("x", "y"))
-        partial = call(functools.partial(sum_kernel, 16), f32(16 * FOLD, LANES), "sum_plane", 1 << 16, mib)(partial)
         partial = exchange_folded(partial, ("z",))
+        partial = call(functools.partial(sum_kernel, 16), f32(32 * FOLD, LANES), "sum_column", 1 << 16, mib)(partial)
+        partial = exchange_folded(partial, ("core", "x", "y"))
     with jax.named_scope("update"):
         sent = call(update_kernel, f32(NORB * (ROWS + 1), LANES), "update", 1 << 28, 3 * mib)(
             phi, images, partial, inside
         )
     with jax.named_scope("transpose_back"):
-        back = lax.all_to_all(sent.reshape(NORB, ROWS + 1, 1, LANES), ORB, 0, 0, tiled=True)
+        back = exchange(sent.reshape(NORB, ROWS + 1, 1, LANES), ORB).reshape(NORB * (ROWS + 1), LANES)
     with jax.named_scope("rms"):
-        slab = jnp.sum(back[:, ROWS, 0, :], axis=0)
-        sent = jnp.broadcast_to(slab, (8, 1, LANES))
-        squares = jnp.sum(exchange(sent, COMP), axis=(0, 1))[:NORB]
+        sent = call(squares_kernel, f32(8, LANES), "squares", 1 << 14, 1 << 15)(back)
+        squares = jnp.sum(exchange(sent.reshape(8, 1, LANES), COMP), axis=(0, 1))[:NORB]
         grad_rms = jnp.sqrt(squares / CELLS)
     with jax.named_scope("unpack"):
-        new = call(unpack_kernel, f32(16, NY, NZ), "unpack", 1 << 20, 2 * mib)(back.reshape(NORB * (ROWS + 1), LANES))
+        new = call(unpack_kernel, f32(16, NY, NZ), "unpack", 1 << 20, 2 * mib)(back)
     return new[None], grad_rms
 
 

time: 218 us -> 216 us (level)
  blocking collectives: 162 us -> 94.7 us
  waiting for transfers between devices: 2.77 us -> 52.7 us
  starting transfers between devices: 31.7 us -> 48.2 us
  local copies, waits for them, and re-layouts: 3.05 us -> 0.03 us
    all_to_all x2 -> x0, blocking collectives: 126 us -> none  [the longest x1 69.4 us: on_device(): lax.all_to_all(pieces, ORB, 0, 0, tiled=True).reshape(NORB * ROWS, LANES)]
    all_to_all x3, blocking collectives: 35.4 us -> 94.7 us  [exchange(): return lax.all_to_all(value, axes, 0, 0, tiled=True)]
    all_to_all x0 -> x1, waiting for transfers between devices: none -> 49.3 us  [on_device(): lax.all_to_all(pieces, ORB, 0, 0, tiled=True).reshape(NORB * ROWS, LANES)]
    all_to_all x0 -> x1, starting transfers between devices: none -> 19.3 us  [on_device(): lax.all_to_all(pieces, ORB, 0, 0, tiled=True).reshape(NORB * ROWS, LANES)]
    unnamed x12 -> x10, local copies, waits for them, and re-layouts: 2.46 us -> 0.03 us
    pallas_call x5 -> x6, Pallas kernels: 7.28 us -> 9.62 us  [the longest x1 2.89 us: on_device(): call(edge_kernel, [whole, f32(16 * FOLD, LANES)], 'edge', 1 << 31, 6 * mib)]
  transfers between devices with their start and end apart: 7 -> 8, of which waited for: 1 -> 3; matrix products, arithmetic and copies ran while one was open for 0% -> 0% of each run, Pallas kernels for 3% -> 4%
where the time goes in v5:
time: 216 us; the launch traced here: 215 us
  blocking collectives  94.7 us (44%)
  waiting for transfers between devices  52.7 us (24%)
  starting transfers between devices  48.2 us (22%)
  Pallas kernels  18 us (8%)
    all_to_all x3, blocking collectives, exchange(): return lax.all_to_all(value, axes, 0, 0, tiled=True)  94.7 us
    all_to_all x1, waiting for transfers between devices, on_device(): lax.all_to_all(pieces, ORB, 0, 0, tiled=True).reshape(NORB * ROWS, LANES)  49.3 us
    ppermute x6, starting transfers between devices, shift(): return lax.ppermute(value, axes, pairs)  21 us
    all_to_all x1, starting transfers between devices, on_device(): lax.all_to_all(pieces, ORB, 0, 0, tiled=True).reshape(NORB * ROWS, LANES)  19.3 us
    all_to_all x1, starting transfers between devices, exchange(): return lax.all_to_all(value, axes, 0, 0, tiled=True)  7.98 us
  transfers between devices with their start and end apart: 8, of which 3 were waited for; matrix products, arithmetic and copies ran while one was open for 0% of the time, Pallas kernels for 4%

profile of v5, /device:TPU:1, one launch (start us, length us, event | category | flops | bytes accessed | tf_op | source)
XLA Modules:
  0.0 215.0 jit_solution(1818591128380431927)
XLA Ops:
  0.6 2.8 %pack.1 = f32[64,32,128]{2,1,0:T(8,128)} custom-call(f32[16,128,128]{2,1,0:T(8,128)} %bitcast.23), custom_call_target="tpu_custom_call" | custom-call | flops 1048576 | bytes 2097152 | tf_op jit(solution)/shard_map/pack/pack/pallas_call | solution.py:360
  3.5 19.3 %all-to-all-start = ((f32[64,32,128]{2,1,0:T(8,128)}), f32[64,32,128]{2,1,0:T(8,128)S(1)}, u32[]{:S(2)}, u32[]{:S(2)}) async-start(f32[64,32,128]{2,1,0:T(8,128)} %pack.1), calls=%async_computation | async-start | bytes 2097152 | tf_op jit(solution)/shard_map/transpose/all_to_all | solution.py:375
  22.8 0.9 constants.1
  23.7 49.3 %all-to-all-done = f32[64,32,128]{2,1,0:T(8,128)S(1)} async-done(((f32[64,32,128]{2,1,0:T(8,128)}), f32[64,32,128]{2,1,0:T(8,128)S(1)}, u32[]{:S(2)}, u32[]{:S(2)}) %all-to-all-start) | async-done | bytes 1048608 | tf_op jit(solution)/shard_map/transpose/all_to_all | solution.py:375
  73.0 1.4 spread_y.1
  74.5 1.3 collective-permute-start
  75.8 5.6 %collective-permute-start.1 = (f32[28,64,128]{2,1,0:T(8,128)}, f32[28,64,128]{2,1,0:T(8,128)S(1)}, u32[]{:S(2)}, u32[]{:S(2)}) collective-permute-start(f32[28,64,128]{2,1,0:T(8,128)} %get-tuple-element.26), channel_id=1, source_target_pairs={{0,8},{8,16},{16,24},{24,32},{32,40},{40,48},{48,56},{56,64},{64,7... | collective-permute-start | bytes 2752520 | tf_op jit(solution)/shard_map/halo/ppermute | solution.py:353
  81.4 1.8 spread.1
  83.2 1.3 collective-permute-start.4
  84.5 5.4 %collective-permute-start.2 = (f32[16,64,128]{2,1,0:T(8,128)}, f32[16,64,128]{2,1,0:T(8,128)S(1)}, u32[]{:S(2)}, u32[]{:S(2)}) collective-permute-start(f32[16,64,128]{2,1,0:T(8,128)} %get-tuple-element.27), channel_id=1, source_target_pairs={{1,0},{2,1},{3,2},{4,3},{5,4},{6,5},{7,6},{9,8},{10,9},{11,10},{12... | collective-permute-start | bytes 1572872 | tf_op jit(solution)/shard_map/halo/ppermute | solution.py:353
  89.9 3.1 %collective-permute-start.3 = (f32[16,64,128]{2,1,0:T(8,128)}, f32[16,64,128]{2,1,0:T(8,128)S(1)}, u32[]{:S(2)}, u32[]{:S(2)}) collective-permute-start(f32[16,64,128]{2,1,0:T(8,128)} %get-tuple-element.28), channel_id=1, source_target_pairs={{0,1},{1,2},{2,3},{3,4},{4,5},{5,6},{6,7},{8,9},{9,10},{10,11},{11... | collective-permute-start | bytes 1572872 | tf_op jit(solution)/shard_map/halo/ppermute | solution.py:353
  93.0 4.3 %collective-permute-start.5 = (f32[8,64,128]{2,1,0:T(8,128)}, f32[8,64,128]{2,1,0:T(8,128)S(1)}, u32[]{:S(2)}, u32[]{:S(2)}) collective-permute-start(f32[8,64,128]{2,1,0:T(8,128)} %get-tuple-element.30), channel_id=1, source_target_pairs={{0,128},{128,256},{256,384},{1,129},{129,257},{257,385},{2,130},{1... | collective-permute-start | bytes 786440 | tf_op jit(solution)/shard_map/halo/ppermute | solution.py:353
  97.4 4.3 %inner.1 = (f32[32,64,128]{2,1,0:T(8,128)S(1)}, f32[64,64]{1,0:T(8,128)S(1)}) custom-call(f32[32,64,128]{2,1,0:T(8,128)S(1)} %get-tuple-element.21.phi, f32[32,128]{1,0:T(8,128)S(1)} %get-tuple-element.22.diagonal, f32[5,128,128]{2,1,0:T(8,128)S(1)} %copy-done.4), custom_call_target="tpu_custom_call" | custom-call | flops 4294967296 | bytes 2097152 | tf_op jit(solution)/shard_map/inner/inner/pallas_call | solution.py:426
  101.6 0.6 collective-permute-done.5.refs_5_
  102.2 2.9 %edge.1 = (f32[32,64,128]{2,1,0:T(8,128)S(1)}, f32[272,128]{1,0:T(8,128)S(1)}) custom-call(f32[32,64,128]{2,1,0:T(8,128)S(1)} %get-tuple-element.21.phi, f32[32,64,128]{2,1,0:T(8,128)S(1)} %get-tuple-element.23.inner, f32[64,64]{1,0:T(8,128)S(1)} %get-tuple-element.24.sums, bf16[512,512]{1,0:T(8,128)(2,1)S(1)} %copy-done.3, bf16[512,512]{1,0:T(8,128)(2,1)S(1)} %copy-done.2, ...), custom_call_target="tpu_custom_call" | custom-call | flops 2147483648 | bytes 6291456 | tf_op jit(solution)/shard_map/edge/edge/pallas_call | solution.py:430
  105.1 19.1 %all_to_all.25 = f32[16,17,1,128]{3,2,1,0:T(1,128)S(1)} all-to-all(f32[16,17,1,128]{3,2,1,0:T(1,128)S(1)} %bitcast.22), channel_id=1, replica_groups=mesh['x'=4,'z'=16,'y'=4,'core'=2] {'z'}, dimensions={0} | all-to-all | bytes 278528 | tf_op jit(solution)/shard_map/correlation_sum/all_to_all | solution.py:343
  124.3 18.8 %all_to_all.26 = f32[32,17,1,128]{3,2,1,0:T(1,128)S(1)} all-to-all(f32[32,17,1,128]{3,2,1,0:T(1,128)S(1)} %bitcast.19), channel_id=1, replica_groups=mesh['x'=4,'z'=16,'y'=4,'core'=2] {'core','x','y'}, dimensions={0} | all-to-all | bytes 557056 | tf_op jit(solution)/shard_map/correlation_sum/all_to_all | solution.py:343
  143.1 1.5 update.1
  144.5 56.8 %all_to_all.27 = f32[64,33,1,128]{3,2,1,0:T(1,128)S(1)} all-to-all(f32[64,33,1,128]{3,2,1,0:T(1,128)S(1)} %bitcast.18), channel_id=1, replica_groups=mesh['x'=4,'z'=16,'y'=4,'core'=2] {'x','z'}, dimensions={0} | all-to-all | bytes 2162688 | tf_op jit(solution)/shard_map/transpose_back/all_to_all | solution.py:343
  201.3 0.6 squares.1
  201.9 8.0 %all-to-all-start.4 = ((f32[8,1,128]{2,1,0:T(1,128)}), f32[8,1,128]{2,1,0:T(1,128)S(1)}, u32[]{:S(2)}, u32[]{:S(2)}) async-start(f32[8,1,128]{2,1,0:T(1,128)} %bitcast.12), calls=%async_computation.4 | async-start | bytes 8192 | tf_op jit(solution)/shard_map/rms/all_to_all | solution.py:343
  209.9 1.8 unpack.1
  211.7 2.7 %all-to-all-done.4 = f32[8,1,128]{2,1,0:T(1,128)S(1)} async-done(((f32[8,1,128]{2,1,0:T(1,128)}), f32[8,1,128]{2,1,0:T(1,128)S(1)}, u32[]{:S(2)}, u32[]{:S(2)}) %all-to-all-start.4) | async-done | bytes 4128 | tf_op jit(solution)/shard_map/rms/all_to_all | solution.py:343
  214.5 0.5 multiply_sqrt_fusion
  (18 shorter events, 0.2 us)
Async XLA Ops:
  3.4 19.4 %copy-start = (f32[16,128,128]{2,1,0:T(8,128)S(1)}, f32[16,128,128]{2,1,0:T(8,128)}, u32[]{:S(2)}) copy-start(f32[16,128,128]{2,1,0:T(8,128)} %potential.1) | copy-start | bytes 3145732
  3.5 19.4 %copy-start.1 = (s32[2,16,128]{2,1,0:T(8,128)S(1)}, s32[2,16,128]{2,1,0:T(8,128)}, u32[]{:S(2)}) copy-start(s32[2,16,128]{2,1,0:T(8,128)} %segments.1) | copy-start | bytes 49156
  3.5 69.6 %all-to-all-start = ((f32[64,32,128]{2,1,0:T(8,128)}), f32[64,32,128]{2,1,0:T(8,128)S(1)}, u32[]{:S(2)}, u32[]{:S(2)}) async-start(f32[64,32,128]{2,1,0:T(8,128)} %pack.1), calls=%async_computation | async-start | bytes 2097152 | tf_op jit(solution)/shard_map/transpose/all_to_all | solution.py:375
  23.7 73.6 %copy-start.4 = (f32[5,128,128]{2,1,0:T(8,128)S(1)}, f32[5,128,128]{2,1,0:T(8,128)}, u32[]{:S(2)}) copy-start(f32[5,128,128]{2,1,0:T(8,128)} %constant.22.clone.blocks) | copy-start | bytes 983044
  74.5 27.7 %collective-permute-start = (f32[28,64,128]{2,1,0:T(8,128)}, f32[28,64,128]{2,1,0:T(8,128)S(1)}, u32[]{:S(2)}, u32[]{:S(2)}) collective-permute-start(f32[28,64,128]{2,1,0:T(8,128)} %get-tuple-element.25), channel_id=1, source_target_pairs={{8,0},{16,8},{24,16},{32,24},{40,32},{48,40},{56,48},{64,56},{72,6... | collective-permute-start | bytes 2752520 | tf_op jit(solution)/shard_map/halo/ppermute | solution.py:353
  75.8 26.4 %collective-permute-start.1 = (f32[28,64,128]{2,1,0:T(8,128)}, f32[28,64,128]{2,1,0:T(8,128)S(1)}, u32[]{:S(2)}, u32[]{:S(2)}) collective-permute-start(f32[28,64,128]{2,1,0:T(8,128)} %get-tuple-element.26), channel_id=1, source_target_pairs={{0,8},{8,16},{16,24},{24,32},{32,40},{40,48},{48,56},{56,64},{64,7... | collective-permute-start | bytes 2752520 | tf_op jit(solution)/shard_map/halo/ppermute | solution.py:353
  83.2 9.8 %collective-permute-start.4 = (f32[8,64,128]{2,1,0:T(8,128)}, f32[8,64,128]{2,1,0:T(8,128)S(1)}, u32[]{:S(2)}, u32[]{:S(2)}) collective-permute-start(f32[8,64,128]{2,1,0:T(8,128)} %get-tuple-element.29), channel_id=1, source_target_pairs={{128,0},{256,128},{384,256},{129,1},{257,129},{385,257},{130,2},{2... | collective-permute-start | bytes 786440 | tf_op jit(solution)/shard_map/halo/ppermute | solution.py:353
  84.5 17.7 %collective-permute-start.2 = (f32[16,64,128]{2,1,0:T(8,128)}, f32[16,64,128]{2,1,0:T(8,128)S(1)}, u32[]{:S(2)}, u32[]{:S(2)}) collective-permute-start(f32[16,64,128]{2,1,0:T(8,128)} %get-tuple-element.27), channel_id=1, source_target_pairs={{1,0},{2,1},{3,2},{4,3},{5,4},{6,5},{7,6},{9,8},{10,9},{11,10},{12... | collective-permute-start | bytes 1572872 | tf_op jit(solution)/shard_map/halo/ppermute | solution.py:353
  89.9 12.3 %collective-permute-start.3 = (f32[16,64,128]{2,1,0:T(8,128)}, f32[16,64,128]{2,1,0:T(8,128)S(1)}, u32[]{:S(2)}, u32[]{:S(2)}) collective-permute-start(f32[16,64,128]{2,1,0:T(8,128)} %get-tuple-element.28), channel_id=1, source_target_pairs={{0,1},{1,2},{2,3},{3,4},{4,5},{5,6},{6,7},{8,9},{9,10},{10,11},{11... | collective-permute-start | bytes 1572872 | tf_op jit(solution)/shard_map/halo/ppermute | solution.py:353
  93.0 9.2 %collective-permute-start.5 = (f32[8,64,128]{2,1,0:T(8,128)}, f32[8,64,128]{2,1,0:T(8,128)S(1)}, u32[]{:S(2)}, u32[]{:S(2)}) collective-permute-start(f32[8,64,128]{2,1,0:T(8,128)} %get-tuple-element.30), channel_id=1, source_target_pairs={{0,128},{128,256},{256,384},{1,129},{129,257},{257,385},{2,130},{1... | collective-permute-start | bytes 786440 | tf_op jit(solution)/shard_map/halo/ppermute | solution.py:353
  97.3 4.9 %copy-start.2 = (bf16[512,512]{1,0:T(8,128)(2,1)S(1)}, bf16[512,512]{1,0:T(8,128)(2,1)}, u32[]{:S(2)}) copy-start(bf16[512,512]{1,0:T(8,128)(2,1)} %constant.24.clone.low) | copy-start | bytes 1572868
  97.3 4.9 %copy-start.3 = (bf16[512,512]{1,0:T(8,128)(2,1)S(1)}, bf16[512,512]{1,0:T(8,128)(2,1)}, u32[]{:S(2)}) copy-start(bf16[512,512]{1,0:T(8,128)(2,1)} %constant.23.clone.high) | copy-start | bytes 1572868
  201.9 12.6 %all-to-all-start.4 = ((f32[8,1,128]{2,1,0:T(1,128)}), f32[8,1,128]{2,1,0:T(1,128)S(1)}, u32[]{:S(2)}, u32[]{:S(2)}) async-start(f32[8,1,128]{2,1,0:T(1,128)} %bitcast.12), calls=%async_computation.4 | async-start | bytes 8192 | tf_op jit(solution)/shard_map/rms/all_to_all | solution.py:343

commit v6 on v5

v6 whole, which is shorter than its diff:
```python
import functools
import math

import jax
import jax.numpy as jnp
import numpy as np
from jax import lax
from jax.experimental import pallas as pl
from jax.experimental.pallas import tpu as pltpu
from jax.sharding import Mesh
from jax.sharding import PartitionSpec as P

spacing = 0.4
descent = 0.02
NX, NY, NZ, NORB = 128, 128, 128, 64
CELLS = NX * NY * NZ
KINETIC = -0.5 / spacing**2
REACH = 7
XG, YB, XL, ZB = 4, 8, 4, 32
ROWS, LANES = XG * YB, XL * ZB
FOLD = 17
HIGH = lax.Precision.HIGHEST
PARAMS = pltpu.CompilerParams(vmem_limit_bytes=12 * 1024 * 1024)
ORB, COMP = ("x", "z"), ("y", "core")


def second_coefs_list():
    terms = []
    for k in range(1, REACH + 1):
        terms.append(
            2.0
            * (-1) ** (k + 1)
            * math.factorial(REACH) ** 2
            / (k * k * math.factorial(REACH - k) * math.factorial(REACH + k))
        )
    return [-2.0 * sum(terms)] + terms


COEFS = [KINETIC * c for c in second_coefs_list()]


def coef(k):
    return COEFS[k] if 1 <= k <= REACH else 0.0


def inner_blocks():
    steps = np.arange(XL)[:, None] - np.arange(XL)[None, :]
    line_z = np.array([[coef(abs(i - j)) for j in range(ZB)] for i in range(ZB)])
    blocks = []
    for shift_by in range(-2, 3):
        line_x = np.array([[coef(abs(int(s) - shift_by * XL)) for s in row] for row in steps])
        blocks.append(np.kron(line_x, np.eye(ZB)) + (np.kron(np.eye(XL), line_z) if shift_by == 0 else 0.0))
    return np.stack(blocks).astype(np.float32)


def edge_matrix():
    table = np.zeros((3 * LANES, XG * LANES))
    for x in range(16):
        for z in range(ZB):
            out = x * ZB + z
            for layer in range(8):
                table[layer * ZB + z, out] += coef(16 + layer - x)
            for t in range(8):
                table[2 * LANES + (x % XL) * ZB + (x // XL) * 8 + t, out] += coef(ZB + t - z)
    return table


def line_matrix():
    return np.array([[coef(abs(i - j)) for j in range(NZ)] for i in range(NZ)], np.float32)


def split(value):
    high = value.astype(jnp.bfloat16)
    return high, (value - high.astype(jnp.float32)).astype(jnp.bfloat16)


def three_products(left, right, dims=(((1,), (0,)), ((), ()))):
    def product(a, b):
        return lax.dot_general(a, b, dims, preferred_element_type=jnp.float32)

    return product(left[0], right[0]) + (product(left[1], right[0]) + product(left[0], right[1]))


def pack_kernel(slab, dst, src, out, sems):
    group = lax.broadcasted_iota(jnp.int32, (32, LANES), 1) // ZB
    comes, goes = [], []
    for xg in range(XG):
        layers, rows = pl.ds(xg * XL, XL), pl.ds(xg * YB, YB)
        comes.append(pltpu.make_async_copy(slab.at[layers], src.at[layers], sems.at[0, xg]))
        goes.append(pltpu.make_async_copy(out.at[:, rows], dst.at[:, rows], sems.at[1, xg]))
        comes[xg].start()
    for xg in range(XG):
        comes[xg].wait()
        for part in range(4):
            rows = slice(part * 32, part * 32 + 32)
            layers = [src[xg * XL + x, rows, :] for x in range(XL)]
            for q in range(4):
                piece = layers[q]
                for x in range(XL):
                    if x != q:
                        moved = pltpu.roll(layers[x], ((x - q) * ZB) % LANES, 1)
                        piece = jnp.where(group == x, moved, piece)
                first = q * 16 + part * 4
                out[first : first + 4, xg * YB : (xg + 1) * YB, :] = piece.reshape(4, YB, LANES)
        goes[xg].start()
    for move in goes:
        move.wait()


def finish_kernel(src, slab, images, inside, dst, squares, own, sems):
    group = lax.broadcasted_iota(jnp.int32, (YB, LANES), 1) // ZB
    total = jnp.zeros((YB, LANES), jnp.float32)
    moves = []
    for xg in range(XG):
        layers = pl.ds(xg * XL, XL)
        moves.append(pltpu.make_async_copy(images.at[layers], own.at[layers], sems.at[xg]))
        moves[xg].start()
    for xg in range(XG):
        moves[xg].wait()
        for yb in range(16):
            rows = slice(yb * YB, (yb + 1) * YB)
            pieces = [src[pl.ds((q * 16 + yb) * (ROWS + 1) + xg * YB, YB), :] for q in range(4)]
            for x in range(XL):
                mixed = pieces[x]
                for q in range(4):
                    if q != x:
                        moved = pltpu.roll(pieces[q], ((q - x) * ZB) % LANES, 1)
                        mixed = jnp.where(group == q, moved, mixed)
                layer = xg * XL + x
                gradient = own[layer, rows, :] - mixed
                total = total + gradient * gradient
                moved = slab[layer, rows, :] - descent * gradient
                dst[layer, rows, :] = jnp.where(inside[layer, rows, :] > 0.0, moved, 0.0)
    squares[...] = jnp.broadcast_to(jnp.sum(total, keepdims=True), squares.shape)


def owner_kernel(slab, below, above, potential, line, own, squares):
    total = jnp.zeros((NY, NZ), jnp.float32)
    for layer in range(16):
        here = slab[layer]
        value = (potential[layer] + jnp.float32(3.0 * COEFS[0])) * here
        value = value + jnp.dot(line[...], here, precision=HIGH, preferred_element_type=jnp.float32)
        value = value + jnp.dot(here, line[...], precision=HIGH, preferred_element_type=jnp.float32)
        for k in range(1, REACH + 1):
            up, down = layer + k, layer - k
            pair = (slab[up] if up < 16 else above[up - 16]) + (slab[down] if down >= 0 else below[down + REACH])
            value = value + COEFS[k] * pair
        own[layer] = value
        total = total + value * value
    squares[...] = jnp.broadcast_to(jnp.sum(total, keepdims=True), squares.shape)


def spread_y_kernel(src, ready, *refs):
    sent, kept, sems = refs[:2], refs[2:4], refs[4]
    ready[...] = jnp.zeros(ready.shape, jnp.float32)
    moves = [pltpu.make_async_copy(kept[side], sent[side], sems.at[side]) for side in range(2)]
    for xg in range(XG):
        for i in range(REACH):
            y = i if xg < 2 else i + 1
            kept[xg // 2][(xg % 2) * REACH + i] = src[pl.ds(xg * YB + y, NORB, stride=ROWS), :]
        if xg % 2:
            moves[xg // 2].start()
    for move in moves:
        move.wait()


def spread_kernel(src, ready, phi, *refs):
    sent, kept, sems = refs[:2], refs[2:4], refs[4]
    x_up, z_up = kept
    moves = [pltpu.make_async_copy(kept[i], sent[i], sems.at[i]) for i in range(2)]
    lane = lax.broadcasted_iota(jnp.int32, (NORB, LANES), 1)
    slot = (lane % ZB) // 8
    for xg in range(XG):
        for y in range(YB):
            r = xg * YB + y
            row = src[pl.ds(r, NORB, stride=ROWS), :]
            phi[r] = row
            if xg == 0:
                x_up[r] = row
            up = pltpu.roll(row, xg * 8, 1) if xg else row
            z_up[y] = jnp.where(slot == xg, up, z_up[y]) if xg else up
        if xg == 1:
            for y in range(6):
                moved = pltpu.roll(phi[YB + 6 + y // 3], (XL - 1 - y % 3) * ZB, 1)
                x_up[YB + y] = jnp.where(lane >= (XL - 1) * ZB, moved, phi[YB + y])
            moves[0].start()
    moves[1].start()
    for move in moves:
        move.wait()


def constants_kernel(place, potential, diagonal):
    x_pos, z_pos = place[0], place[1]
    lane = lax.broadcasted_iota(jnp.int32, (YB, LANES), 1)
    first_row = pl.multiple_of(z_pos * YB, YB)
    for xg in range(XG):
        block = jnp.zeros((YB, LANES), jnp.float32)
        for x in range(XL):
            rows = potential[xg * XL + x, pl.ds(first_row, YB), :]
            moved = pltpu.roll(rows, lax.rem(x * ZB + LANES - x_pos * ZB, LANES), 1)
            block = jnp.where(lane // ZB == x, moved, block)
        diagonal[xg * YB : (xg + 1) * YB, :] = block + jnp.float32(3.0 * COEFS[0])


def tall(ref, xg):
    return ref[xg * YB : (xg + 1) * YB].reshape(YB * NORB, LANES)


def inner_kernel(phi, diagonal, blocks, sums):
    total = jnp.zeros((NORB, NORB), jnp.float32)
    nothing = jnp.zeros((LANES, LANES), jnp.float32)
    for pair in range(2):
        matrix = jnp.concatenate(
            [
                jnp.concatenate([blocks[to - xg + 2] if abs(to - xg) <= 2 else nothing for xg in range(XG)], axis=0)
                for to in (2 * pair, 2 * pair + 1)
            ],
            axis=1,
        )
        cells = jnp.concatenate([tall(phi, xg) for xg in range(XG)], axis=1)
        both = jnp.dot(cells, matrix, precision=HIGH, preferred_element_type=jnp.float32)
        for xg in (2 * pair, 2 * pair + 1):
            own = slice((xg % 2) * LANES, (xg % 2 + 1) * LANES)
            rows = [phi[xg * YB + y] for y in range(YB)]
            values = []
            for y in range(YB):
                r = xg * YB + y
                value = both[y * NORB : (y + 1) * NORB, own] + diagonal[r : r + 1, :] * rows[y]
                for other in range(YB):
                    if other != y:
                        value = value + COEFS[abs(other - y)] * rows[other]
                values.append(value)
            total = total + lax.dot_general(
                jnp.concatenate(rows, axis=1),
                jnp.concatenate(values, axis=1),
                (((1,), (1,)), ((), ())),
                precision=HIGH,
                preferred_element_type=jnp.float32,
            )
    sums[...] = total


def fold(table):
    n = NORB // 2
    above = lax.broadcasted_iota(jnp.int32, (n, n), 0) - lax.broadcasted_iota(jnp.int32, (n, n), 1)
    last = table[n:, n:]
    corner = table[:n, n:]
    mixed = jnp.where(above <= 0, table[:n, :n], last)
    diagonal = jnp.sum(jnp.where(above == 0, last, 0.0), axis=0, keepdims=True)
    top = jnp.concatenate([corner[: n // 2], corner[n // 2 :], mixed[: n // 2], mixed[n // 2 :]], axis=1)
    bottom = jnp.concatenate([diagonal, jnp.zeros((1, LANES - n), jnp.float32)], axis=1)
    return top, bottom


def unfold(top, bottom):
    n = NORB // 2
    above = lax.broadcasted_iota(jnp.int32, (n, n), 0) - lax.broadcasted_iota(jnp.int32, (n, n), 1)
    corner = jnp.concatenate([top[:, :n], top[:, n : 2 * n]], axis=0)
    mixed = jnp.concatenate([top[:, 2 * n : 3 * n], top[:, 3 * n :]], axis=0)
    turned = mixed.T
    first = jnp.where(above <= 0, mixed, turned)
    last = jnp.where(above > 0, mixed, jnp.where(above == 0, bottom[:, :n], turned))
    left = jnp.concatenate([first, corner.T], axis=0)
    right = jnp.concatenate([corner, last], axis=0)
    return jnp.concatenate([left, right], axis=1)


def edge_kernel(phi, sums, high, low, y_a, y_b, x_up, z_up, partial):
    total = sums[...]
    z_halo = z_up[...].reshape(YB * NORB, LANES)
    place = lax.broadcasted_iota(jnp.int32, (NORB, LANES), 1) // ZB
    next_rows = [x_up[YB + y] for y in range(6)]
    for y in (0, 3):
        parts = [pltpu.roll(next_rows[y + i], (i + 1) * ZB, 1) for i in range(3)]
        next_rows.append(jnp.where(place == 0, parts[0], jnp.where(place == 1, parts[1], parts[2])))
    next_group = jnp.stack(next_rows).reshape(YB * NORB, LANES)
    for pair in range(2):
        parts = [tall(x_up, 0), next_group, z_halo] if pair else [z_halo]
        halo = split(jnp.concatenate(parts, axis=1))
        used = slice(0 if pair else 2 * LANES, 3 * LANES), slice(pair * 2 * LANES, (pair + 1) * 2 * LANES)
        both = three_products(halo, (high[used], low[used]))
        y_halo = y_b if pair else y_a
        for xg in (2 * pair, 2 * pair + 1):
            own = slice((xg % 2) * LANES, (xg % 2 + 1) * LANES)
            rows = [y_halo[(xg % 2) * REACH + i] for i in range(REACH)]
            values = []
            for y in range(YB):
                value = both[y * NORB : (y + 1) * NORB, own]
                for i in range(REACH):
                    k = y + REACH - i if pair else YB + i - y
                    if 1 <= k <= REACH:
                        value = value + COEFS[k] * rows[i]
                values.append(value)
            left = split(jnp.concatenate([phi[xg * YB + y] for y in range(YB)], axis=1))
            right = split(jnp.concatenate(values, axis=1))
            total = total + 2.0 * three_products(left, right, (((1,), (1,)), ((), ())))
    top, bottom = fold(total + total.T)
    store_copies(partial, top, bottom)


def store_copies(sent, top, bottom):
    for i in range(sent.shape[0] // FOLD):
        sent[i * FOLD : i * FOLD + FOLD - 1, :] = top
        sent[i * FOLD + FOLD - 1 : (i + 1) * FOLD, :] = bottom


def added(came, count):
    size = came.shape[0] // count
    top = came[0 : FOLD - 1, :]
    bottom = came[FOLD - 1 : FOLD, :]
    for i in range(1, count):
        top = top + came[i * size : i * size + FOLD - 1, :]
        bottom = bottom + came[i * size + FOLD - 1 : i * size + FOLD, :]
    return top, bottom


def sum_kernel(count, came, sent):
    store_copies(sent, *added(came, count))


def mix_kernel(phi, sums, place, own_squares, out, cross):
    lag = unfold(*added(sums, 32)) * jnp.float32(0.5 / CELLS)
    squares = jnp.zeros((NORB, LANES), jnp.float32)
    for xg in range(XG):
        rows = [phi[xg * YB + y] for y in range(YB)]
        mixed = jnp.dot(lag, jnp.concatenate(rows, axis=1), precision=HIGH, preferred_element_type=jnp.float32)
        for y in range(YB):
            value = mixed[:, y * LANES : (y + 1) * LANES]
            squares = squares + value * value
            out[pl.ds(xg * YB + y, NORB, stride=ROWS + 1), :] = value
    across = (((1,), (1,)), ((), ()))
    ones = jnp.ones((8, LANES), jnp.float32)
    sums_row = lax.dot_general(ones, squares, across, precision=HIGH, preferred_element_type=jnp.float32)
    products = lax.dot_general(ones[:, :NORB], lag * lag, across, precision=HIGH, preferred_element_type=jnp.float32)
    lane = lax.broadcasted_iota(jnp.int32, (8, NORB), 1)
    images = jnp.where(lane == place[0] * 16 + place[1], own_squares[:, :NORB], 0.0)
    row = jnp.concatenate([sums_row, images], axis=1)
    out[pl.ds(ROWS, NORB, stride=ROWS + 1), :] = jnp.broadcast_to(row[0:1, :], (NORB, LANES))
    cross[...] = jnp.concatenate([products * jnp.float32(CELLS), jnp.zeros((8, LANES - NORB), jnp.float32)], axis=1)


def squares_kernel(src, sent):
    rows = src[pl.ds(ROWS, NORB, stride=ROWS + 1), :]
    sent[...] = jnp.broadcast_to(jnp.sum(rows, axis=0, keepdims=True), sent.shape)


def f32(*shape):
    return jax.ShapeDtypeStruct(shape, jnp.float32)


def call(kernel, out_shape, name, flops, nbytes, **more):
    return pl.pallas_call(
        kernel,
        out_shape=out_shape,
        compiler_params=PARAMS,
        name=name,
        cost_estimate=pl.CostEstimate(flops=flops, bytes_accessed=nbytes, transcendentals=0),
        **more,
    )


def exchange(value, axes):
    return lax.all_to_all(value, axes, 0, 0, tiled=True)


def exchange_folded(value, axes):
    shape = value.shape
    return exchange(value.reshape(shape[0] // FOLD, FOLD, 1, LANES), axes).reshape(shape)


def shift(value, axes, count, up):
    pairs = [(i + 1, i) if up else (i, i + 1) for i in range(count - 1)]
    return lax.ppermute(value, axes, pairs)


def on_device(orbitals, potential, segments):
    mib = 1 << 20
    far, vmem = pl.BlockSpec(memory_space=pltpu.HBM), pl.BlockSpec(memory_space=pltpu.VMEM)
    with jax.named_scope("pack"):
        pieces = call(
            pack_kernel,
            pltpu.HBM((NORB, ROWS, LANES), jnp.float32),
            "pack",
            1 << 20,
            2 * mib,
            in_specs=[far],
            out_specs=far,
            scratch_shapes=[
                pltpu.VMEM((16, NY, NZ), jnp.float32),
                pltpu.VMEM((NORB, ROWS, LANES), jnp.float32),
                pltpu.SemaphoreType.DMA((2, XG)),
            ],
        )(pltpu.with_memory_space_constraint(orbitals[0], pltpu.HBM))
    with jax.named_scope("transpose"):
        arrived = exchange(pieces, ORB).reshape(NORB * ROWS, LANES)
    with jax.named_scope("owner"):
        slab = orbitals[0]
        below = shift(slab[16 - REACH :], COMP, 8, False)
        above = shift(slab[:REACH], COMP, 8, True)
        own, own_squares = call(owner_kernel, [f32(16, NY, NZ), f32(8, LANES)], "owner", 1 << 30, 4 * mib)(
            slab, below, above, potential, jnp.asarray(line_matrix())
        )
        depth = lax.broadcasted_iota(jnp.int32, (16, NY, NZ), 2)
        inside = ((depth >= segments[0][..., None]) & (depth < segments[1][..., None])).astype(jnp.float32)
    with jax.named_scope("block_constants"):
        place = jnp.stack([lax.axis_index("x"), lax.axis_index("z")]).astype(jnp.int32)
        smem = pl.BlockSpec(memory_space=pltpu.SMEM)
        diagonal = call(
            constants_kernel, f32(ROWS, LANES), "constants", 1 << 20, mib, in_specs=[smem, vmem]
        )(place, potential)
    arrived, diagonal, own, own_squares, inside = lax.optimization_barrier(
        (arrived, diagonal, own, own_squares, inside)
    )
    edge = edge_matrix()
    edge_high = edge.astype(jnp.bfloat16)
    edge_low = (edge - edge_high.astype(np.float64)).astype(jnp.bfloat16)

    whole = f32(ROWS, NORB, LANES)
    y_side, x_side, z_side = (f32(n, NORB, LANES) for n in (2 * REACH, 2 * REACH, YB))

    def send(kernel, kept_out, sides, name, *inputs):
        return call(
            kernel,
            kept_out + [pltpu.HBM(side.shape, jnp.float32) for side in sides],
            name,
            1 << 20,
            4 * mib,
            out_specs=[vmem] * len(kept_out) + [far] * len(sides),
            scratch_shapes=[pltpu.VMEM(side.shape, jnp.float32) for side in sides]
            + [pltpu.SemaphoreType.DMA((len(sides),))],
        )(*inputs)

    with jax.named_scope("spread"):
        ready, y_up_a, y_down_b = send(spread_y_kernel, [f32(8, LANES)], [y_side, y_side], "spread_y", arrived)
        phi, x_up, z_up = send(spread_kernel, [whole], [x_side, z_side], "spread", arrived, ready)
    with jax.named_scope("halo"):
        y_up_a = shift(y_up_a, "z", 16, True)
        y_down_b = shift(y_down_b, "z", 16, False)
        x_up = shift(x_up, COMP, 8, True)
        z_up = shift(z_up, "x", 4, True)
    with jax.named_scope("inner"):
        sums = call(inner_kernel, f32(NORB, NORB), "inner", 1 << 32, 2 * mib)(
            phi, diagonal, jnp.asarray(inner_blocks())
        )
    with jax.named_scope("edge"):
        partial = call(edge_kernel, f32(16 * FOLD, LANES), "edge", 1 << 31, 4 * mib)(
            phi, sums, jnp.asarray(edge_high), jnp.asarray(edge_low), y_up_a, y_down_b, x_up, z_up
        )
    with jax.named_scope("correlation_sum"):
        partial = exchange_folded(partial, ("z",))
        partial = call(functools.partial(sum_kernel, 16), f32(32 * FOLD, LANES), "sum_column", 1 << 16, mib)(partial)
        partial = exchange_folded(partial, ("core", "x", "y"))
    with jax.named_scope("mix"):
        sent, cross = call(
            mix_kernel,
            [f32(NORB * (ROWS + 1), LANES), f32(8, LANES)],
            "mix",
            1 << 28,
            3 * mib,
            in_specs=[vmem, vmem, smem, vmem],
        )(phi, partial, place, own_squares)
    with jax.named_scope("transpose_back"):
        back = exchange(sent.reshape(NORB, ROWS + 1, 1, LANES), ORB).reshape(NORB * (ROWS + 1), LANES)
    with jax.named_scope("rms"):
        sent = call(squares_kernel, f32(8, LANES), "squares", 1 << 14, 1 << 15)(back)
        terms = jnp.sum(exchange(sent.reshape(8, 1, LANES), COMP), axis=(0, 1))
        of_images = terms[NORB:]
        squares = of_images - 2.0 * cross[0, :NORB] + terms[:NORB]
    with jax.named_scope("finish"):
        new, direct = call(
            finish_kernel,
            [f32(16, NY, NZ), f32(8, LANES)],
            "finish",
            1 << 22,
            5 * mib,
            in_specs=[vmem, vmem, far, vmem],
            scratch_shapes=[pltpu.VMEM((16, NY, NZ), jnp.float32), pltpu.SemaphoreType.DMA((XG,))],
        )(back, slab, pltpu.with_memory_space_constraint(own, pltpu.HBM), inside)
    with jax.named_scope("rms"):

        def summed_directly():
            mine = jnp.broadcast_to(direct[0:1, :NORB], (NORB, NORB))
            lane = lax.broadcasted_iota(jnp.int32, (NORB, NORB), 1)
            mine = jnp.where(lane == place[0] * 16 + place[1], mine, 0.0)
            slabs = jnp.sum(exchange(mine, ORB), axis=0)
            return jnp.sum(exchange(jnp.broadcast_to(slabs, (8, NORB)), COMP), axis=0)

        cancels = jnp.logical_not(jnp.all(squares >= 0.03 * of_images))
        squares = lax.cond(cancels, summed_directly, lambda: squares)
        grad_rms = jnp.sqrt(squares / CELLS)
    return new[None], grad_rms


def solution(mesh):
    fine = Mesh(mesh.devices.reshape(4, 16, 4, 2), ("x", "z", "y", "core"))
    return jax.shard_map(
        on_device,
        mesh=fine,
        in_specs=(P(ORB, COMP, None, None), P(COMP, None, None), P(None, COMP, None)),
        out_specs=(P(ORB, COMP, None, None), P()),
        check_vma=False,
    )
```

time: 216 us -> 210 us (0.972)
  waiting for transfers between devices: 52.7 us -> 42.6 us
  Pallas kernels: 18 us -> 22.5 us
  blocking collectives: 94.7 us -> 92.1 us
    all_to_all x1 -> x0, waiting for transfers between devices: 49.3 us -> none  [on_device(): lax.all_to_all(pieces, ORB, 0, 0, tiled=True).reshape(NORB * ROWS, LANES)]
    all_to_all x1 -> x2, waiting for transfers between devices: 2.74 us -> 34.3 us  [exchange(): return lax.all_to_all(value, axes, 0, 0, tiled=True)]
    all_to_all x1 -> x2, starting transfers between devices: 7.98 us -> 27.3 us  [exchange(): return lax.all_to_all(value, axes, 0, 0, tiled=True)]
    all_to_all x1 -> x0, starting transfers between devices: 19.3 us -> none  [on_device(): lax.all_to_all(pieces, ORB, 0, 0, tiled=True).reshape(NORB * ROWS, LANES)]
    ppermute x6, waiting for transfers between devices: 0.59 us -> 8.34 us  [shift(): return lax.ppermute(value, axes, pairs)]
    pallas_call x7 -> x8, Pallas kernels: 14.6 us -> 19 us  [the longest x1 4.63 us: on_device(): call(inner_kernel, f32(NORB, NORB), 'inner', 1 << 32, 2 * mib)]
    all_to_all x3, blocking collectives: 94.7 us -> 92.1 us  [exchange(): return lax.all_to_all(value, axes, 0, 0, tiled=True)]
  transfers between devices with their start and end apart: 8 -> 8, of which waited for: 3 -> 5; matrix products, arithmetic and copies ran while one was open for 0% -> 1% of each run, Pallas kernels for 4% -> 7%
where the time goes in v6:
time: 210 us; the launch traced here: 209 us
  blocking collectives  92.1 us (44%)
  starting transfers between devices  47 us (22%)
  waiting for transfers between devices  42.6 us (20%)
  Pallas kernels  22.5 us (11%)
    all_to_all x3, blocking collectives, exchange(): return lax.all_to_all(value, axes, 0, 0, tiled=True)  92.1 us
    all_to_all x2, waiting for transfers between devices, exchange(): return lax.all_to_all(value, axes, 0, 0, tiled=True)  34.3 us
    all_to_all x2, starting transfers between devices, exchange(): return lax.all_to_all(value, axes, 0, 0, tiled=True)  27.3 us
    ppermute x6, starting transfers between devices, shift(): return lax.ppermute(value, axes, pairs)  19.7 us
    ppermute x6, waiting for transfers between devices, shift(): return lax.ppermute(value, axes, pairs)  8.34 us
    pallas_call x1, Pallas kernels, on_device(): call(inner_kernel, f32(NORB, NORB), 'inner', 1 << 32, 2 * mib)  4.63 us
  transfers between devices with their start and end apart: 8, of which 5 were waited for; matrix products, arithmetic and copies ran while one was open for 1% of the time, Pallas kernels for 7%

profile of v6, /device:TPU:1, one launch (start us, length us, event | category | flops | bytes accessed | tf_op | source)
XLA Modules:
  0.0 209.5 jit_solution(13774905180905745196)
XLA Ops:
  0.6 2.8 %pack.1 = f32[64,32,128]{2,1,0:T(8,128)} custom-call(f32[16,128,128]{2,1,0:T(8,128)} %bitcast.35), custom_call_target="tpu_custom_call" | custom-call | flops 1048576 | bytes 2097152 | tf_op jit(solution)/shard_map/pack/pack/pallas_call | solution.py:380
  3.5 19.3 %all-to-all-start.2 = ((f32[64,32,128]{2,1,0:T(8,128)}), f32[64,32,128]{2,1,0:T(8,128)S(1)}, u32[]{:S(2)}, u32[]{:S(2)}) async-start(f32[64,32,128]{2,1,0:T(8,128)} %pack.1), calls=%async_computation.2 | async-start | bytes 2097152 | tf_op jit(solution)/shard_map/transpose/all_to_all | solution.py:363
  22.8 1.0 slice_bitcast_fusion.1
  23.7 2.9 %collective-permute-start.1 = (f32[7,128,128]{2,1,0:T(8,128)}, f32[7,128,128]{2,1,0:T(8,128)}, u32[]{:S(2)}, u32[]{:S(2)}) collective-permute-start(f32[7,128,128]{2,1,0:T(8,128)} %get-tuple-element.51), channel_id=1, source_target_pairs={{1,0},{2,1},{3,2},{4,3},{5,4},{6,5},{7,6},{9,8},{10,9},{11,10},{12... | collective-permute-start | bytes 1376264 | tf_op jit(solution)/shard_map/owner/ppermute | solution.py:373
  26.6 3.1 %collective-permute-start = (f32[7,128,128]{2,1,0:T(8,128)}, f32[7,128,128]{2,1,0:T(8,128)}, u32[]{:S(2)}, u32[]{:S(2)}) collective-permute-start(f32[7,128,128]{2,1,0:T(8,128)} %get-tuple-element.52), channel_id=1, source_target_pairs={{0,1},{1,2},{2,3},{3,4},{4,5},{5,6},{6,7},{8,9},{9,10},{10,11},{11... | collective-permute-start | bytes 1376264 | tf_op jit(solution)/shard_map/owner/ppermute | solution.py:373
  31.1 3.4 %collective-permute-done.1.above = f32[7,128,128]{2,1,0:T(8,128)} collective-permute-done((f32[7,128,128]{2,1,0:T(8,128)}, f32[7,128,128]{2,1,0:T(8,128)}, u32[]{:S(2)}, u32[]{:S(2)}) %collective-permute-start.1) | collective-permute-done | bytes 458784 | tf_op jit(solution)/shard_map/owner/ppermute | solution.py:373
  35.4 3.9 %owner.1 = (f32[16,128,128]{2,1,0:T(8,128)S(1)}, f32[8,128]{1,0:T(8,128)S(1)}) custom-call(f32[16,128,128]{2,1,0:T(8,128)S(1)} %bitcast.36, f32[7,128,128]{2,1,0:T(8,128)} %collective-permute-done.below, f32[7,128,128]{2,1,0:T(8,128)} %collective-permute-done.1.above, f32[16,128,128]{2,1,0:T(8,128)S(1)} %copy-done.2, f32[128,128]{1,0:T(8,128)S(1)} %copy-done.7), custom_call_target="tpu_custom_call" | custom-call | flops 1073741824 | bytes 4194304 | tf_op jit(solution)/shard_map/owner/owner/pallas_call | solution.py:400
  40.3 32.7 %all-to-all-done.2 = f32[64,32,128]{2,1,0:T(8,128)S(1)} async-done(((f32[64,32,128]{2,1,0:T(8,128)}), f32[64,32,128]{2,1,0:T(8,128)S(1)}, u32[]{:S(2)}, u32[]{:S(2)}) %all-to-all-start.2) | async-done | bytes 1048608 | tf_op jit(solution)/shard_map/transpose/all_to_all | solution.py:363
  73.0 1.4 spread_y.1
  74.4 1.3 collective-permute-start.2
  75.7 5.6 %collective-permute-start.3 = (f32[14,64,128]{2,1,0:T(8,128)}, f32[14,64,128]{2,1,0:T(8,128)S(1)}, u32[]{:S(2)}, u32[]{:S(2)}) collective-permute-start(f32[14,64,128]{2,1,0:T(8,128)} %get-tuple-element.39), channel_id=1, source_target_pairs={{0,8},{8,16},{16,24},{24,32},{32,40},{40,48},{48,56},{56,64},{64,7... | collective-permute-start | bytes 1376264 | tf_op jit(solution)/shard_map/halo/ppermute | solution.py:373
  81.3 1.5 spread.1
  82.8 5.4 %collective-permute-start.4 = (f32[14,64,128]{2,1,0:T(8,128)}, f32[14,64,128]{2,1,0:T(8,128)S(1)}, u32[]{:S(2)}, u32[]{:S(2)}) collective-permute-start(f32[14,64,128]{2,1,0:T(8,128)} %get-tuple-element.40), channel_id=1, source_target_pairs={{1,0},{2,1},{3,2},{4,3},{5,4},{6,5},{7,6},{9,8},{10,9},{11,10},{12... | collective-permute-start | bytes 1376264 | tf_op jit(solution)/shard_map/halo/ppermute | solution.py:373
  88.2 1.5 collective-permute-start.5
  89.7 4.6 %inner.1.sums = f32[64,64]{1,0:T(8,128)S(1)} custom-call(f32[32,64,128]{2,1,0:T(8,128)S(1)} %get-tuple-element.36.phi, f32[32,128]{1,0:T(8,128)S(1)} %constants.1.diagonal, f32[5,128,128]{2,1,0:T(8,128)S(1)} %copy-done.6), custom_call_target="tpu_custom_call" | custom-call | flops 4294967296 | bytes 2097152 | tf_op jit(solution)/shard_map/inner/inner/pallas_call | solution.py:442
  94.3 4.0 %collective-permute-done.5.z_up = f32[8,64,128]{2,1,0:T(8,128)S(1)} collective-permute-done((f32[8,64,128]{2,1,0:T(8,128)}, f32[8,64,128]{2,1,0:T(8,128)S(1)}, u32[]{:S(2)}, u32[]{:S(2)}) %collective-permute-start.5) | collective-permute-done | bytes 262176 | tf_op jit(solution)/shard_map/halo/ppermute | solution.py:373
  98.3 2.0 edge.1
  100.3 18.0 %all_to_all.37 = f32[16,17,1,128]{3,2,1,0:T(1,128)S(1)} all-to-all(f32[16,17,1,128]{3,2,1,0:T(1,128)S(1)} %bitcast.42), channel_id=1, replica_groups=mesh['x'=4,'z'=16,'y'=4,'core'=2] {'z'}, dimensions={0} | all-to-all | bytes 278528 | tf_op jit(solution)/shard_map/correlation_sum/all_to_all | solution.py:363
  118.3 17.5 %all_to_all.38 = f32[32,17,1,128]{3,2,1,0:T(1,128)S(1)} all-to-all(f32[32,17,1,128]{3,2,1,0:T(1,128)S(1)} %bitcast.39), channel_id=1, replica_groups=mesh['x'=4,'z'=16,'y'=4,'core'=2] {'core','x','y'}, dimensions={0} | all-to-all | bytes 557056 | tf_op jit(solution)/shard_map/correlation_sum/all_to_all | solution.py:363
  135.8 2.0 mix.1
  137.8 56.6 %all_to_all.39 = f32[64,33,1,128]{3,2,1,0:T(1,128)S(1)} all-to-all(f32[64,33,1,128]{3,2,1,0:T(1,128)S(1)} %bitcast.40), channel_id=1, replica_groups=mesh['x'=4,'z'=16,'y'=4,'core'=2] {'x','z'}, dimensions={0} | all-to-all | bytes 2162688 | tf_op jit(solution)/shard_map/transpose_back/all_to_all | solution.py:363
  195.0 8.1 %all-to-all-start.6 = ((f32[8,1,128]{2,1,0:T(1,128)}), f32[8,1,128]{2,1,0:T(1,128)S(1)}, u32[]{:S(2)}, u32[]{:S(2)}) async-start(f32[8,1,128]{2,1,0:T(1,128)} %bitcast.19), calls=%async_computation.6 | async-start | bytes 8192 | tf_op jit(solution)/shard_map/rms/all_to_all | solution.py:363
  203.1 3.1 %finish.1 = (f32[16,128,128]{2,1,0:T(8,128)}, f32[8,128]{1,0:T(8,128)S(1)}) custom-call(f32[2112,128]{1,0:T(8,128)S(1)} %bitcast.32, f32[16,128,128]{2,1,0:T(8,128)S(1)} %bitcast.37, f32[16,128,128]{2,1,0:T(8,128)} %copy-done.3, f32[16,128,128]{2,1,0:T(8,128)S(1)} %fusion.1.inside), custom_call_target="tpu_custom_call" | custom-call | flops 4194304 | bytes 5242880 | tf_op jit(solution)/shard_map/finish/finish/pallas_call | solution.py:470
  206.2 1.5 all-to-all-done.6
  (32 shorter events, 5.2 us)
Async XLA Ops:
  3.4 19.3 %copy-start = (f32[1,16,128,128]{3,2,1,0:T(8,128)S(1)}, f32[1,16,128,128]{3,2,1,0:T(8,128)}, u32[]{:S(2)}) copy-start(f32[1,16,128,128]{3,2,1,0:T(8,128)} %param.9) | copy-start | bytes 3145732
  3.5 69.6 %all-to-all-start.2 = ((f32[64,32,128]{2,1,0:T(8,128)}), f32[64,32,128]{2,1,0:T(8,128)S(1)}, u32[]{:S(2)}, u32[]{:S(2)}) async-start(f32[64,32,128]{2,1,0:T(8,128)} %pack.1), calls=%async_computation.2 | async-start | bytes 2097152 | tf_op jit(solution)/shard_map/transpose/all_to_all | solution.py:363
  22.7 7.1 %copy-start.1 = (f32[16,128,128]{2,1,0:T(8,128)S(1)}, f32[16,128,128]{2,1,0:T(8,128)}, u32[]{:S(2)}) copy-start(f32[16,128,128]{2,1,0:T(8,128)} %potential.3) | copy-start | bytes 3145732
  22.7 7.7 %copy-start.8 = (s32[2,16,128]{2,1,0:T(8,128)S(1)}, s32[2,16,128]{2,1,0:T(8,128)}, u32[]{:S(2)}) copy-start(s32[2,16,128]{2,1,0:T(8,128)} %param.11) | copy-start | bytes 49156
  23.7 10.7 %collective-permute-start.1 = (f32[7,128,128]{2,1,0:T(8,128)}, f32[7,128,128]{2,1,0:T(8,128)}, u32[]{:S(2)}, u32[]{:S(2)}) collective-permute-start(f32[7,128,128]{2,1,0:T(8,128)} %get-tuple-element.51), channel_id=1, source_target_pairs={{1,0},{2,1},{3,2},{4,3},{5,4},{6,5},{7,6},{9,8},{10,9},{11,10},{12... | collective-permute-start | bytes 1376264 | tf_op jit(solution)/shard_map/owner/ppermute | solution.py:373
  26.6 8.8 %collective-permute-start = (f32[7,128,128]{2,1,0:T(8,128)}, f32[7,128,128]{2,1,0:T(8,128)}, u32[]{:S(2)}, u32[]{:S(2)}) collective-permute-start(f32[7,128,128]{2,1,0:T(8,128)} %get-tuple-element.52), channel_id=1, source_target_pairs={{0,1},{1,2},{2,3},{3,4},{4,5},{5,6},{6,7},{8,9},{9,10},{10,11},{11... | collective-permute-start | bytes 1376264 | tf_op jit(solution)/shard_map/owner/ppermute | solution.py:373
  29.8 5.6 %copy-start.2 = (f32[16,128,128]{2,1,0:T(8,128)S(1)}, f32[16,128,128]{2,1,0:T(8,128)}, u32[]{:S(2)}) copy-start(f32[16,128,128]{2,1,0:T(8,128)} %potential.3) | copy-start | bytes 3145732
  29.8 5.6 %copy-start.7 = (f32[128,128]{1,0:T(8,128)S(1)}, f32[128,128]{1,0:T(8,128)}, u32[]{:S(2)}) copy-start(f32[128,128]{1,0:T(8,128)} %constant.34.clone.line) | copy-start | bytes 196612
  39.3 1.0 copy-start.3
  40.3 49.4 %copy-start.6 = (f32[5,128,128]{2,1,0:T(8,128)S(1)}, f32[5,128,128]{2,1,0:T(8,128)}, u32[]{:S(2)}) copy-start(f32[5,128,128]{2,1,0:T(8,128)} %constant.35.clone.blocks) | copy-start | bytes 983044
  74.4 23.9 %collective-permute-start.2 = (f32[14,64,128]{2,1,0:T(8,128)}, f32[14,64,128]{2,1,0:T(8,128)S(1)}, u32[]{:S(2)}, u32[]{:S(2)}) collective-permute-start(f32[14,64,128]{2,1,0:T(8,128)} %get-tuple-element.38), channel_id=1, source_target_pairs={{8,0},{16,8},{24,16},{32,24},{40,32},{48,40},{56,48},{64,56},{72,6... | collective-permute-start | bytes 1376264 | tf_op jit(solution)/shard_map/halo/ppermute | solution.py:373
  75.7 22.6 %collective-permute-start.3 = (f32[14,64,128]{2,1,0:T(8,128)}, f32[14,64,128]{2,1,0:T(8,128)S(1)}, u32[]{:S(2)}, u32[]{:S(2)}) collective-permute-start(f32[14,64,128]{2,1,0:T(8,128)} %get-tuple-element.39), channel_id=1, source_target_pairs={{0,8},{8,16},{16,24},{24,32},{32,40},{40,48},{48,56},{56,64},{64,7... | collective-permute-start | bytes 1376264 | tf_op jit(solution)/shard_map/halo/ppermute | solution.py:373
  82.8 15.5 %collective-permute-start.4 = (f32[14,64,128]{2,1,0:T(8,128)}, f32[14,64,128]{2,1,0:T(8,128)S(1)}, u32[]{:S(2)}, u32[]{:S(2)}) collective-permute-start(f32[14,64,128]{2,1,0:T(8,128)} %get-tuple-element.40), channel_id=1, source_target_pairs={{1,0},{2,1},{3,2},{4,3},{5,4},{6,5},{7,6},{9,8},{10,9},{11,10},{12... | collective-permute-start | bytes 1376264 | tf_op jit(solution)/shard_map/halo/ppermute | solution.py:373
  88.2 10.1 %collective-permute-start.5 = (f32[8,64,128]{2,1,0:T(8,128)}, f32[8,64,128]{2,1,0:T(8,128)S(1)}, u32[]{:S(2)}, u32[]{:S(2)}) collective-permute-start(f32[8,64,128]{2,1,0:T(8,128)} %get-tuple-element.41), channel_id=1, source_target_pairs={{128,0},{256,128},{384,256},{129,1},{257,129},{385,257},{130,2},{2... | collective-permute-start | bytes 786440 | tf_op jit(solution)/shard_map/halo/ppermute | solution.py:373
  89.7 8.6 %copy-start.4 = (bf16[384,512]{1,0:T(8,128)(2,1)S(1)}, bf16[384,512]{1,0:T(8,128)(2,1)}, u32[]{:S(2)}) copy-start(bf16[384,512]{1,0:T(8,128)(2,1)} %constant.37.clone.low) | copy-start | bytes 1179652
  89.7 8.6 %copy-start.5 = (bf16[384,512]{1,0:T(8,128)(2,1)S(1)}, bf16[384,512]{1,0:T(8,128)(2,1)}, u32[]{:S(2)}) copy-start(bf16[384,512]{1,0:T(8,128)(2,1)} %constant.36.clone.high) | copy-start | bytes 1179652
  195.0 12.7 %all-to-all-start.6 = ((f32[8,1,128]{2,1,0:T(1,128)}), f32[8,1,128]{2,1,0:T(1,128)S(1)}, u32[]{:S(2)}, u32[]{:S(2)}) async-start(f32[8,1,128]{2,1,0:T(1,128)} %bitcast.19), calls=%async_computation.6 | async-start | bytes 8192 | tf_op jit(solution)/shard_map/rms/all_to_all | solution.py:363

commit v7 on v6

--- a/solution.py
+++ b/solution.py
@@ -168,6 +168,7 @@
     sent, kept, sems = refs[:2], refs[2:4], refs[4]
     x_up, z_up = kept
     moves = [pltpu.make_async_copy(kept[i], sent[i], sems.at[i]) for i in range(2)]
+    z_rows = [None] * YB
     lane = lax.broadcasted_iota(jnp.int32, (NORB, LANES), 1)
     slot = (lane % ZB) // 8
     for xg in range(XG):
@@ -178,12 +179,15 @@
             if xg == 0:
                 x_up[r] = row
             up = pltpu.roll(row, xg * 8, 1) if xg else row
-            z_up[y] = jnp.where(slot == xg, up, z_up[y]) if xg else up
+            z_rows[y] = jnp.where(slot == xg, up, z_rows[y]) if xg else up
         if xg == 1:
             for y in range(6):
                 moved = pltpu.roll(phi[YB + 6 + y // 3], (XL - 1 - y % 3) * ZB, 1)
                 x_up[YB + y] = jnp.where(lane >= (XL - 1) * ZB, moved, phi[YB + y])
             moves[0].start()
+    for y in range(REACH):
+        moved = pltpu.roll(z_rows[REACH], REACH - y, 1)
+        z_up[y] = jnp.where(lane % 8 == REACH, moved, z_rows[y])
     moves[1].start()
     for move in moves:
         move.wait()
@@ -267,7 +271,12 @@
 
 def edge_kernel(phi, sums, high, low, y_a, y_b, x_up, z_up, partial):
     total = sums[...]
-    z_halo = z_up[...].reshape(YB * NORB, LANES)
+    lane = lax.broadcasted_iota(jnp.int32, (NORB, LANES), 1)
+    z_rows = [z_up[y] for y in range(REACH)]
+    z_rows.append(z_rows[0])
+    for y in range(REACH):
+        z_rows[REACH] = jnp.where(lane % 8 == y, pltpu.roll(z_rows[y], LANES - (REACH - y), 1), z_rows[REACH])
+    z_halo = jnp.stack(z_rows).reshape(YB * NORB, LANES)
     place = lax.broadcasted_iota(jnp.int32, (NORB, LANES), 1) // ZB
     next_rows = [x_up[YB + y] for y in range(6)]
     for y in (0, 3):
@@ -416,7 +425,7 @@
     edge_low = (edge - edge_high.astype(np.float64)).astype(jnp.bfloat16)
 
     whole = f32(ROWS, NORB, LANES)
-    y_side, x_side, z_side = (f32(n, NORB, LANES) for n in (2 * REACH, 2 * REACH, YB))
+    y_side, x_side, z_side = (f32(n, NORB, LANES) for n in (2 * REACH, 2 * REACH, REACH))
 
     def send(kernel, kept_out, sides, name, *inputs):
         return call(
@@ -483,11 +492,12 @@
             lane = lax.broadcasted_iota(jnp.int32, (NORB, NORB), 1)
             mine = jnp.where(lane == place[0] * 16 + place[1], mine, 0.0)
             slabs = jnp.sum(exchange(mine, ORB), axis=0)
-            return jnp.sum(exchange(jnp.broadcast_to(slabs, (8, NORB)), COMP), axis=0)
-
-        cancels = jnp.logical_not(jnp.all(squares >= 0.03 * of_images))
-        squares = lax.cond(cancels, summed_directly, lambda: squares)
-        grad_rms = jnp.sqrt(squares / CELLS)
+            whole_sums = jnp.sum(exchange(jnp.broadcast_to(slabs, (8, NORB)), COMP), axis=0)
+            return jnp.sqrt(whole_sums / CELLS)
+
+        cancels = jnp.logical_not(jnp.all(squares >= 0.1 * of_images))
+        from_terms = jnp.sqrt(squares / CELLS)
+        grad_rms = lax.cond(cancels, summed_directly, lambda: from_terms)
     return new[None], grad_rms
 
 

time: 210 us -> 209 us (level)
  no operation moved by 1% of the time
where the time goes in v7:
time: 209 us
  blocking collectives  92 us (44%)
  starting transfers between devices  47 us (22%)
  waiting for transfers between devices  41.9 us (20%)
  Pallas kernels  22.6 us (11%)
    all_to_all x3, blocking collectives, exchange(): return lax.all_to_all(value, axes, 0, 0, tiled=True)  92 us
    all_to_all x2, waiting for transfers between devices, exchange(): return lax.all_to_all(value, axes, 0, 0, tiled=True)  34.3 us
    all_to_all x2, starting transfers between devices, exchange(): return lax.all_to_all(value, axes, 0, 0, tiled=True)  27.3 us
    ppermute x6, starting transfers between devices, shift(): return lax.ppermute(value, axes, pairs)  19.7 us
    ppermute x6, waiting for transfers between devices, shift(): return lax.ppermute(value, axes, pairs)  7.64 us
    pallas_call x1, Pallas kernels, on_device(): call(inner_kernel, f32(NORB, NORB), 'inner', 1 << 32, 2 * mib)  4.63 us
  transfers between devices with their start and end apart: 8, of which 5 were waited for; matrix products, arithmetic and copies ran while one was open for 1% of the time, Pallas kernels for 7%

profile of v7, /device:TPU:1, one launch (start us, length us, event | category | flops | bytes accessed | tf_op | source)
XLA Modules:
  0.0 208.9 jit_solution(17006880986081953647)
XLA Ops:
  0.6 2.8 %pack.1 = f32[64,32,128]{2,1,0:T(8,128)} custom-call(f32[16,128,128]{2,1,0:T(8,128)} %bitcast.35), custom_call_target="tpu_custom_call" | custom-call | flops 1048576 | bytes 2097152 | tf_op jit(solution)/shard_map/pack/pack/pallas_call | solution.py:389
  3.5 19.3 %all-to-all-start.2 = ((f32[64,32,128]{2,1,0:T(8,128)}), f32[64,32,128]{2,1,0:T(8,128)S(1)}, u32[]{:S(2)}, u32[]{:S(2)}) async-start(f32[64,32,128]{2,1,0:T(8,128)} %pack.1), calls=%async_computation.2 | async-start | bytes 2097152 | tf_op jit(solution)/shard_map/transpose/all_to_all | solution.py:372
  22.8 1.0 slice_bitcast_fusion.1
  23.7 2.9 %collective-permute-start.1 = (f32[7,128,128]{2,1,0:T(8,128)}, f32[7,128,128]{2,1,0:T(8,128)}, u32[]{:S(2)}, u32[]{:S(2)}) collective-permute-start(f32[7,128,128]{2,1,0:T(8,128)} %get-tuple-element.57), channel_id=1, source_target_pairs={{1,0},{2,1},{3,2},{4,3},{5,4},{6,5},{7,6},{9,8},{10,9},{11,10},{12... | collective-permute-start | bytes 1376264 | tf_op jit(solution)/shard_map/owner/ppermute | solution.py:382
  26.6 3.1 %collective-permute-start = (f32[7,128,128]{2,1,0:T(8,128)}, f32[7,128,128]{2,1,0:T(8,128)}, u32[]{:S(2)}, u32[]{:S(2)}) collective-permute-start(f32[7,128,128]{2,1,0:T(8,128)} %get-tuple-element.58), channel_id=1, source_target_pairs={{0,1},{1,2},{2,3},{3,4},{4,5},{5,6},{6,7},{8,9},{9,10},{10,11},{11... | collective-permute-start | bytes 1376264 | tf_op jit(solution)/shard_map/owner/ppermute | solution.py:382
  31.1 3.4 %collective-permute-done.1.above = f32[7,128,128]{2,1,0:T(8,128)} collective-permute-done((f32[7,128,128]{2,1,0:T(8,128)}, f32[7,128,128]{2,1,0:T(8,128)}, u32[]{:S(2)}, u32[]{:S(2)}) %collective-permute-start.1) | collective-permute-done | bytes 458784 | tf_op jit(solution)/shard_map/owner/ppermute | solution.py:382
  35.4 3.9 %owner.1 = (f32[16,128,128]{2,1,0:T(8,128)S(1)}, f32[8,128]{1,0:T(8,128)S(1)}) custom-call(f32[16,128,128]{2,1,0:T(8,128)S(1)} %bitcast.36, f32[7,128,128]{2,1,0:T(8,128)} %collective-permute-done.below, f32[7,128,128]{2,1,0:T(8,128)} %collective-permute-done.1.above, f32[16,128,128]{2,1,0:T(8,128)S(1)} %copy-done.2, f32[128,128]{1,0:T(8,128)S(1)} %copy-done.7), custom_call_target="tpu_custom_call" | custom-call | flops 1073741824 | bytes 4194304 | tf_op jit(solution)/shard_map/owner/owner/pallas_call | solution.py:409
  40.3 32.7 %all-to-all-done.2 = f32[64,32,128]{2,1,0:T(8,128)S(1)} async-done(((f32[64,32,128]{2,1,0:T(8,128)}), f32[64,32,128]{2,1,0:T(8,128)S(1)}, u32[]{:S(2)}, u32[]{:S(2)}) %all-to-all-start.2) | async-done | bytes 1048608 | tf_op jit(solution)/shard_map/transpose/all_to_all | solution.py:372
  73.0 1.4 spread_y.1
  74.4 1.3 collective-permute-start.2
  75.7 5.6 %collective-permute-start.3 = (f32[14,64,128]{2,1,0:T(8,128)}, f32[14,64,128]{2,1,0:T(8,128)S(1)}, u32[]{:S(2)}, u32[]{:S(2)}) collective-permute-start(f32[14,64,128]{2,1,0:T(8,128)} %get-tuple-element.45), channel_id=1, source_target_pairs={{0,8},{8,16},{16,24},{24,32},{32,40},{40,48},{48,56},{56,64},{64,7... | collective-permute-start | bytes 1376264 | tf_op jit(solution)/shard_map/halo/ppermute | solution.py:382
  81.3 1.6 spread.1
  82.9 5.4 %collective-permute-start.4 = (f32[14,64,128]{2,1,0:T(8,128)}, f32[14,64,128]{2,1,0:T(8,128)S(1)}, u32[]{:S(2)}, u32[]{:S(2)}) collective-permute-start(f32[14,64,128]{2,1,0:T(8,128)} %get-tuple-element.46), channel_id=1, source_target_pairs={{1,0},{2,1},{3,2},{4,3},{5,4},{6,5},{7,6},{9,8},{10,9},{11,10},{12... | collective-permute-start | bytes 1376264 | tf_op jit(solution)/shard_map/halo/ppermute | solution.py:382
  88.3 1.5 collective-permute-start.5
  89.8 4.6 %inner.1.sums = f32[64,64]{1,0:T(8,128)S(1)} custom-call(f32[32,64,128]{2,1,0:T(8,128)S(1)} %get-tuple-element.42.phi, f32[32,128]{1,0:T(8,128)S(1)} %constants.1.diagonal, f32[5,128,128]{2,1,0:T(8,128)S(1)} %copy-done.6), custom_call_target="tpu_custom_call" | custom-call | flops 4294967296 | bytes 2097152 | tf_op jit(solution)/shard_map/inner/inner/pallas_call | solution.py:451
  94.5 3.3 %collective-permute-done.5.z_up = f32[7,64,128]{2,1,0:T(8,128)S(1)} collective-permute-done((f32[7,64,128]{2,1,0:T(8,128)}, f32[7,64,128]{2,1,0:T(8,128)S(1)}, u32[]{:S(2)}, u32[]{:S(2)}) %collective-permute-start.5) | collective-permute-done | bytes 229408 | tf_op jit(solution)/shard_map/halo/ppermute | solution.py:382
  97.8 2.0 edge.1
  99.8 18.0 %all_to_all.37 = f32[16,17,1,128]{3,2,1,0:T(1,128)S(1)} all-to-all(f32[16,17,1,128]{3,2,1,0:T(1,128)S(1)} %bitcast.42), channel_id=1, replica_groups=mesh['x'=4,'z'=16,'y'=4,'core'=2] {'z'}, dimensions={0} | all-to-all | bytes 278528 | tf_op jit(solution)/shard_map/correlation_sum/all_to_all | solution.py:372
  117.8 17.5 %all_to_all.38 = f32[32,17,1,128]{3,2,1,0:T(1,128)S(1)} all-to-all(f32[32,17,1,128]{3,2,1,0:T(1,128)S(1)} %bitcast.39), channel_id=1, replica_groups=mesh['x'=4,'z'=16,'y'=4,'core'=2] {'core','x','y'}, dimensions={0} | all-to-all | bytes 557056 | tf_op jit(solution)/shard_map/correlation_sum/all_to_all | solution.py:372
  135.3 2.0 mix.1
  137.3 56.6 %all_to_all.39 = f32[64,33,1,128]{3,2,1,0:T(1,128)S(1)} all-to-all(f32[64,33,1,128]{3,2,1,0:T(1,128)S(1)} %bitcast.40), channel_id=1, replica_groups=mesh['x'=4,'z'=16,'y'=4,'core'=2] {'x','z'}, dimensions={0} | all-to-all | bytes 2162688 | tf_op jit(solution)/shard_map/transpose_back/all_to_all | solution.py:372
  194.5 8.1 %all-to-all-start.6 = ((f32[8,1,128]{2,1,0:T(1,128)}), f32[8,1,128]{2,1,0:T(1,128)S(1)}, u32[]{:S(2)}, u32[]{:S(2)}) async-start(f32[8,1,128]{2,1,0:T(1,128)} %bitcast.19), calls=%async_computation.6 | async-start | bytes 8192 | tf_op jit(solution)/shard_map/rms/all_to_all | solution.py:372
  202.5 3.1 %finish.1 = (f32[16,128,128]{2,1,0:T(8,128)}, f32[8,128]{1,0:T(8,128)S(1)}) custom-call(f32[2112,128]{1,0:T(8,128)S(1)} %bitcast.32, f32[16,128,128]{2,1,0:T(8,128)S(1)} %bitcast.37, f32[16,128,128]{2,1,0:T(8,128)} %copy-done.3, f32[16,128,128]{2,1,0:T(8,128)S(1)} %fusion.1.inside), custom_call_target="tpu_custom_call" | custom-call | flops 4194304 | bytes 5242880 | tf_op jit(solution)/shard_map/finish/finish/pallas_call | solution.py:479
  205.6 1.5 all-to-all-done.6
  (32 shorter events, 5.2 us)
Async XLA Ops:
  3.4 19.3 %copy-start = (f32[1,16,128,128]{3,2,1,0:T(8,128)S(1)}, f32[1,16,128,128]{3,2,1,0:T(8,128)}, u32[]{:S(2)}) copy-start(f32[1,16,128,128]{3,2,1,0:T(8,128)} %param.9) | copy-start | bytes 3145732
  3.5 69.6 %all-to-all-start.2 = ((f32[64,32,128]{2,1,0:T(8,128)}), f32[64,32,128]{2,1,0:T(8,128)S(1)}, u32[]{:S(2)}, u32[]{:S(2)}) async-start(f32[64,32,128]{2,1,0:T(8,128)} %pack.1), calls=%async_computation.2 | async-start | bytes 2097152 | tf_op jit(solution)/shard_map/transpose/all_to_all | solution.py:372
  22.7 7.1 %copy-start.1 = (f32[16,128,128]{2,1,0:T(8,128)S(1)}, f32[16,128,128]{2,1,0:T(8,128)}, u32[]{:S(2)}) copy-start(f32[16,128,128]{2,1,0:T(8,128)} %potential.3) | copy-start | bytes 3145732
  22.7 7.7 %copy-start.8 = (s32[2,16,128]{2,1,0:T(8,128)S(1)}, s32[2,16,128]{2,1,0:T(8,128)}, u32[]{:S(2)}) copy-start(s32[2,16,128]{2,1,0:T(8,128)} %param.11) | copy-start | bytes 49156
  23.7 10.7 %collective-permute-start.1 = (f32[7,128,128]{2,1,0:T(8,128)}, f32[7,128,128]{2,1,0:T(8,128)}, u32[]{:S(2)}, u32[]{:S(2)}) collective-permute-start(f32[7,128,128]{2,1,0:T(8,128)} %get-tuple-element.57), channel_id=1, source_target_pairs={{1,0},{2,1},{3,2},{4,3},{5,4},{6,5},{7,6},{9,8},{10,9},{11,10},{12... | collective-permute-start | bytes 1376264 | tf_op jit(solution)/shard_map/owner/ppermute | solution.py:382
  26.6 8.8 %collective-permute-start = (f32[7,128,128]{2,1,0:T(8,128)}, f32[7,128,128]{2,1,0:T(8,128)}, u32[]{:S(2)}, u32[]{:S(2)}) collective-permute-start(f32[7,128,128]{2,1,0:T(8,128)} %get-tuple-element.58), channel_id=1, source_target_pairs={{0,1},{1,2},{2,3},{3,4},{4,5},{5,6},{6,7},{8,9},{9,10},{10,11},{11... | collective-permute-start | bytes 1376264 | tf_op jit(solution)/shard_map/owner/ppermute | solution.py:382
  29.8 5.6 %copy-start.2 = (f32[16,128,128]{2,1,0:T(8,128)S(1)}, f32[16,128,128]{2,1,0:T(8,128)}, u32[]{:S(2)}) copy-start(f32[16,128,128]{2,1,0:T(8,128)} %potential.3) | copy-start | bytes 3145732
  29.8 5.6 %copy-start.7 = (f32[128,128]{1,0:T(8,128)S(1)}, f32[128,128]{1,0:T(8,128)}, u32[]{:S(2)}) copy-start(f32[128,128]{1,0:T(8,128)} %constant.38.clone.line) | copy-start | bytes 196612
  39.3 1.0 copy-start.3
  40.3 49.5 %copy-start.6 = (f32[5,128,128]{2,1,0:T(8,128)S(1)}, f32[5,128,128]{2,1,0:T(8,128)}, u32[]{:S(2)}) copy-start(f32[5,128,128]{2,1,0:T(8,128)} %constant.39.clone.blocks) | copy-start | bytes 983044
  74.4 23.4 %collective-permute-start.2 = (f32[14,64,128]{2,1,0:T(8,128)}, f32[14,64,128]{2,1,0:T(8,128)S(1)}, u32[]{:S(2)}, u32[]{:S(2)}) collective-permute-start(f32[14,64,128]{2,1,0:T(8,128)} %get-tuple-element.44), channel_id=1, source_target_pairs={{8,0},{16,8},{24,16},{32,24},{40,32},{48,40},{56,48},{64,56},{72,6... | collective-permute-start | bytes 1376264 | tf_op jit(solution)/shard_map/halo/ppermute | solution.py:382
  75.7 22.1 %collective-permute-start.3 = (f32[14,64,128]{2,1,0:T(8,128)}, f32[14,64,128]{2,1,0:T(8,128)S(1)}, u32[]{:S(2)}, u32[]{:S(2)}) collective-permute-start(f32[14,64,128]{2,1,0:T(8,128)} %get-tuple-element.45), channel_id=1, source_target_pairs={{0,8},{8,16},{16,24},{24,32},{32,40},{40,48},{48,56},{56,64},{64,7... | collective-permute-start | bytes 1376264 | tf_op jit(solution)/shard_map/halo/ppermute | solution.py:382
  82.9 14.8 %collective-permute-start.4 = (f32[14,64,128]{2,1,0:T(8,128)}, f32[14,64,128]{2,1,0:T(8,128)S(1)}, u32[]{:S(2)}, u32[]{:S(2)}) collective-permute-start(f32[14,64,128]{2,1,0:T(8,128)} %get-tuple-element.46), channel_id=1, source_target_pairs={{1,0},{2,1},{3,2},{4,3},{5,4},{6,5},{7,6},{9,8},{10,9},{11,10},{12... | collective-permute-start | bytes 1376264 | tf_op jit(solution)/shard_map/halo/ppermute | solution.py:382
  88.3 9.4 %collective-permute-start.5 = (f32[7,64,128]{2,1,0:T(8,128)}, f32[7,64,128]{2,1,0:T(8,128)S(1)}, u32[]{:S(2)}, u32[]{:S(2)}) collective-permute-start(f32[7,64,128]{2,1,0:T(8,128)} %get-tuple-element.47), channel_id=1, source_target_pairs={{128,0},{256,128},{384,256},{129,1},{257,129},{385,257},{130,2},{2... | collective-permute-start | bytes 688136 | tf_op jit(solution)/shard_map/halo/ppermute | solution.py:382
  89.8 7.9 %copy-start.4 = (bf16[384,512]{1,0:T(8,128)(2,1)S(1)}, bf16[384,512]{1,0:T(8,128)(2,1)}, u32[]{:S(2)}) copy-start(bf16[384,512]{1,0:T(8,128)(2,1)} %constant.41.clone.low) | copy-start | bytes 1179652
  89.8 7.9 %copy-start.5 = (bf16[384,512]{1,0:T(8,128)(2,1)S(1)}, bf16[384,512]{1,0:T(8,128)(2,1)}, u32[]{:S(2)}) copy-start(bf16[384,512]{1,0:T(8,128)(2,1)} %constant.40.clone.high) | copy-start | bytes 1179652
  194.5 12.7 %all-to-all-start.6 = ((f32[8,1,128]{2,1,0:T(1,128)}), f32[8,1,128]{2,1,0:T(1,128)S(1)}, u32[]{:S(2)}, u32[]{:S(2)}) async-start(f32[8,1,128]{2,1,0:T(1,128)} %bitcast.19), calls=%async_computation.6 | async-start | bytes 8192 | tf_op jit(solution)/shard_map/rms/all_to_all | solution.py:372

commit v8 on v7

--- a/solution.py
+++ b/solution.py
@@ -351,6 +351,15 @@
 def squares_kernel(src, sent):
     rows = src[pl.ds(ROWS, NORB, stride=ROWS + 1), :]
     sent[...] = jnp.broadcast_to(jnp.sum(rows, axis=0, keepdims=True), sent.shape)
+
+
+def verdict_kernel(came, cross, rms, cancels):
+    terms = jnp.sum(came[...], axis=0, keepdims=True)
+    of_images = terms[:, NORB:]
+    squares = of_images - 2.0 * cross[0:1, :NORB] + terms[:, :NORB]
+    rms[...] = jnp.sqrt(jnp.maximum(squares, 0.0) * jnp.float32(1.0 / CELLS))
+    kept = jnp.where(squares >= 0.1 * of_images, 0.0, 1.0)
+    cancels[0, 0] = (jnp.sum(kept) > 0.0).astype(jnp.int32)
 
 
 def f32(*shape):
@@ -472,9 +481,15 @@
         back = exchange(sent.reshape(NORB, ROWS + 1, 1, LANES), ORB).reshape(NORB * (ROWS + 1), LANES)
     with jax.named_scope("rms"):
         sent = call(squares_kernel, f32(8, LANES), "squares", 1 << 14, 1 << 15)(back)
-        terms = jnp.sum(exchange(sent.reshape(8, 1, LANES), COMP), axis=(0, 1))
-        of_images = terms[NORB:]
-        squares = of_images - 2.0 * cross[0, :NORB] + terms[:NORB]
+        came = exchange(sent.reshape(8, 1, LANES), COMP).reshape(8, LANES)
+        from_terms, cancels = call(
+            verdict_kernel,
+            [f32(1, NORB), jax.ShapeDtypeStruct((1, 1), jnp.int32)],
+            "verdict",
+            1 << 12,
+            1 << 13,
+            out_specs=[vmem, smem],
+        )(came, cross)
     with jax.named_scope("finish"):
         new, direct = call(
             finish_kernel,
@@ -495,9 +510,7 @@
             whole_sums = jnp.sum(exchange(jnp.broadcast_to(slabs, (8, NORB)), COMP), axis=0)
             return jnp.sqrt(whole_sums / CELLS)
 
-        cancels = jnp.logical_not(jnp.all(squares >= 0.1 * of_images))
-        from_terms = jnp.sqrt(squares / CELLS)
-        grad_rms = lax.cond(cancels, summed_directly, lambda: from_terms)
+        grad_rms = lax.cond(cancels[0, 0] > 0, summed_directly, lambda: from_terms[0])
     return new[None], grad_rms
 
 

time: 209 us -> 210 us (level)
  no operation moved by 1% of the time
where the time goes in v8:
time: 210 us; the launch traced here: 209 us
  blocking collectives  92 us (44%)
  starting transfers between devices  47 us (22%)
  waiting for transfers between devices  41.9 us (20%)
  Pallas kernels  23.4 us (11%)
  local copies, waits for them, and re-layouts  2.55 us (1%)
    all_to_all x3, blocking collectives, exchange(): return lax.all_to_all(value, axes, 0, 0, tiled=True)  92 us
    all_to_all x2, waiting for transfers between devices, exchange(): return lax.all_to_all(value, axes, 0, 0, tiled=True)  34.3 us
    all_to_all x2, starting transfers between devices, exchange(): return lax.all_to_all(value, axes, 0, 0, tiled=True)  27.3 us
    ppermute x6, starting transfers between devices, shift(): return lax.ppermute(value, axes, pairs)  19.7 us
    ppermute x6, waiting for transfers between devices, shift(): return lax.ppermute(value, axes, pairs)  7.64 us
    pallas_call x1, Pallas kernels, on_device(): call(inner_kernel, f32(NORB, NORB), 'inner', 1 << 32, 2 * mib)  4.63 us
  transfers between devices with their start and end apart: 8, of which 5 were waited for; matrix products, arithmetic and copies ran while one was open for 1% of the time, Pallas kernels for 7%

profile of v8, /device:TPU:1, one launch (start us, length us, event | category | flops | bytes accessed | tf_op | source)
XLA Modules:
  0.0 209.1 jit_solution(7846625145737067586)
XLA Ops:
  0.6 2.8 %pack.1 = f32[64,32,128]{2,1,0:T(8,128)} custom-call(f32[16,128,128]{2,1,0:T(8,128)} %bitcast.33), custom_call_target="tpu_custom_call" | custom-call | flops 1048576 | bytes 2097152 | tf_op jit(solution)/shard_map/pack/pack/pallas_call | solution.py:398
  3.5 19.3 %all-to-all-start.2 = ((f32[64,32,128]{2,1,0:T(8,128)}), f32[64,32,128]{2,1,0:T(8,128)S(1)}, u32[]{:S(2)}, u32[]{:S(2)}) async-start(f32[64,32,128]{2,1,0:T(8,128)} %pack.1), calls=%async_computation.2 | async-start | bytes 2097152 | tf_op jit(solution)/shard_map/transpose/all_to_all | solution.py:381
  22.8 1.0 slice_bitcast_fusion.1
  23.8 2.9 %collective-permute-start.1 = (f32[7,128,128]{2,1,0:T(8,128)}, f32[7,128,128]{2,1,0:T(8,128)}, u32[]{:S(2)}, u32[]{:S(2)}) collective-permute-start(f32[7,128,128]{2,1,0:T(8,128)} %get-tuple-element.53), channel_id=1, source_target_pairs={{1,0},{2,1},{3,2},{4,3},{5,4},{6,5},{7,6},{9,8},{10,9},{11,10},{12... | collective-permute-start | bytes 1376264 | tf_op jit(solution)/shard_map/owner/ppermute | solution.py:391
  26.6 3.1 %collective-permute-start = (f32[7,128,128]{2,1,0:T(8,128)}, f32[7,128,128]{2,1,0:T(8,128)}, u32[]{:S(2)}, u32[]{:S(2)}) collective-permute-start(f32[7,128,128]{2,1,0:T(8,128)} %get-tuple-element.54), channel_id=1, source_target_pairs={{0,1},{1,2},{2,3},{3,4},{4,5},{5,6},{6,7},{8,9},{9,10},{10,11},{11... | collective-permute-start | bytes 1376264 | tf_op jit(solution)/shard_map/owner/ppermute | solution.py:391
  31.1 3.4 %collective-permute-done.1.above = f32[7,128,128]{2,1,0:T(8,128)} collective-permute-done((f32[7,128,128]{2,1,0:T(8,128)}, f32[7,128,128]{2,1,0:T(8,128)}, u32[]{:S(2)}, u32[]{:S(2)}) %collective-permute-start.1) | collective-permute-done | bytes 458784 | tf_op jit(solution)/shard_map/owner/ppermute | solution.py:391
  35.5 3.9 %owner.1 = (f32[16,128,128]{2,1,0:T(8,128)S(1)}, f32[8,128]{1,0:T(8,128)S(1)}) custom-call(f32[16,128,128]{2,1,0:T(8,128)S(1)} %bitcast.34, f32[7,128,128]{2,1,0:T(8,128)} %collective-permute-done.below, f32[7,128,128]{2,1,0:T(8,128)} %collective-permute-done.1.above, f32[16,128,128]{2,1,0:T(8,128)S(1)} %copy-done.2, f32[128,128]{1,0:T(8,128)S(1)} %copy-done.7), custom_call_target="tpu_custom_call" | custom-call | flops 1073741824 | bytes 4194304 | tf_op jit(solution)/shard_map/owner/owner/pallas_call | solution.py:418
  40.3 32.7 %all-to-all-done.2 = f32[64,32,128]{2,1,0:T(8,128)S(1)} async-done(((f32[64,32,128]{2,1,0:T(8,128)}), f32[64,32,128]{2,1,0:T(8,128)S(1)}, u32[]{:S(2)}, u32[]{:S(2)}) %all-to-all-start.2) | async-done | bytes 1048608 | tf_op jit(solution)/shard_map/transpose/all_to_all | solution.py:381
  73.0 1.3 spread_y.1
  74.4 1.3 collective-permute-start.2
  75.7 5.6 %collective-permute-start.3 = (f32[14,64,128]{2,1,0:T(8,128)}, f32[14,64,128]{2,1,0:T(8,128)S(1)}, u32[]{:S(2)}, u32[]{:S(2)}) collective-permute-start(f32[14,64,128]{2,1,0:T(8,128)} %get-tuple-element.41), channel_id=1, source_target_pairs={{0,8},{8,16},{16,24},{24,32},{32,40},{40,48},{48,56},{56,64},{64,7... | collective-permute-start | bytes 1376264 | tf_op jit(solution)/shard_map/halo/ppermute | solution.py:391
  81.2 1.7 spread.1
  82.9 5.4 %collective-permute-start.4 = (f32[14,64,128]{2,1,0:T(8,128)}, f32[14,64,128]{2,1,0:T(8,128)S(1)}, u32[]{:S(2)}, u32[]{:S(2)}) collective-permute-start(f32[14,64,128]{2,1,0:T(8,128)} %get-tuple-element.42), channel_id=1, source_target_pairs={{1,0},{2,1},{3,2},{4,3},{5,4},{6,5},{7,6},{9,8},{10,9},{11,10},{12... | collective-permute-start | bytes 1376264 | tf_op jit(solution)/shard_map/halo/ppermute | solution.py:391
  88.3 1.5 collective-permute-start.5
  89.8 4.6 %inner.1.sums = f32[64,64]{1,0:T(8,128)S(1)} custom-call(f32[32,64,128]{2,1,0:T(8,128)S(1)} %get-tuple-element.38.phi, f32[32,128]{1,0:T(8,128)S(1)} %constants.1.diagonal, f32[5,128,128]{2,1,0:T(8,128)S(1)} %copy-done.6), custom_call_target="tpu_custom_call" | custom-call | flops 4294967296 | bytes 2097152 | tf_op jit(solution)/shard_map/inner/inner/pallas_call | solution.py:460
  94.5 3.3 %collective-permute-done.5.z_up = f32[7,64,128]{2,1,0:T(8,128)S(1)} collective-permute-done((f32[7,64,128]{2,1,0:T(8,128)}, f32[7,64,128]{2,1,0:T(8,128)S(1)}, u32[]{:S(2)}, u32[]{:S(2)}) %collective-permute-start.5) | collective-permute-done | bytes 229408 | tf_op jit(solution)/shard_map/halo/ppermute | solution.py:391
  97.8 2.0 edge.1
  99.8 18.0 %all_to_all.37 = f32[16,17,1,128]{3,2,1,0:T(1,128)S(1)} all-to-all(f32[16,17,1,128]{3,2,1,0:T(1,128)S(1)} %bitcast.40), channel_id=1, replica_groups=mesh['x'=4,'z'=16,'y'=4,'core'=2] {'z'}, dimensions={0} | all-to-all | bytes 278528 | tf_op jit(solution)/shard_map/correlation_sum/all_to_all | solution.py:381
  117.8 17.5 %all_to_all.38 = f32[32,17,1,128]{3,2,1,0:T(1,128)S(1)} all-to-all(f32[32,17,1,128]{3,2,1,0:T(1,128)S(1)} %bitcast.37), channel_id=1, replica_groups=mesh['x'=4,'z'=16,'y'=4,'core'=2] {'core','x','y'}, dimensions={0} | all-to-all | bytes 557056 | tf_op jit(solution)/shard_map/correlation_sum/all_to_all | solution.py:381
  135.2 2.0 mix.1
  137.3 56.6 %all_to_all.39 = f32[64,33,1,128]{3,2,1,0:T(1,128)S(1)} all-to-all(f32[64,33,1,128]{3,2,1,0:T(1,128)S(1)} %bitcast.38), channel_id=1, replica_groups=mesh['x'=4,'z'=16,'y'=4,'core'=2] {'x','z'}, dimensions={0} | all-to-all | bytes 2162688 | tf_op jit(solution)/shard_map/transpose_back/all_to_all | solution.py:381
  194.5 8.1 %all-to-all-start.6 = ((f32[8,1,128]{2,1,0:T(1,128)}), f32[8,1,128]{2,1,0:T(1,128)S(1)}, u32[]{:S(2)}, u32[]{:S(2)}) async-start(f32[8,1,128]{2,1,0:T(1,128)} %bitcast.20), calls=%async_computation.6 | async-start | bytes 8192 | tf_op jit(solution)/shard_map/rms/all_to_all | solution.py:381
  202.5 3.1 %finish.1 = (f32[16,128,128]{2,1,0:T(8,128)}, f32[8,128]{1,0:T(8,128)S(1)}) custom-call(f32[2112,128]{1,0:T(8,128)S(1)} %bitcast.30, f32[16,128,128]{2,1,0:T(8,128)S(1)} %bitcast.35, f32[16,128,128]{2,1,0:T(8,128)} %copy-done.3, f32[16,128,128]{2,1,0:T(8,128)S(1)} %fusion.1.inside), custom_call_target="tpu_custom_call" | custom-call | flops 4194304 | bytes 5242880 | tf_op jit(solution)/shard_map/finish/finish/pallas_call | solution.py:494
  205.6 1.5 all-to-all-done.6
  (32 shorter events, 5.3 us)
Async XLA Ops:
  3.4 19.3 %copy-start = (f32[1,16,128,128]{3,2,1,0:T(8,128)S(1)}, f32[1,16,128,128]{3,2,1,0:T(8,128)}, u32[]{:S(2)}) copy-start(f32[1,16,128,128]{3,2,1,0:T(8,128)} %param.9) | copy-start | bytes 3145732
  3.5 69.6 %all-to-all-start.2 = ((f32[64,32,128]{2,1,0:T(8,128)}), f32[64,32,128]{2,1,0:T(8,128)S(1)}, u32[]{:S(2)}, u32[]{:S(2)}) async-start(f32[64,32,128]{2,1,0:T(8,128)} %pack.1), calls=%async_computation.2 | async-start | bytes 2097152 | tf_op jit(solution)/shard_map/transpose/all_to_all | solution.py:381
  22.7 7.1 %copy-start.1 = (f32[16,128,128]{2,1,0:T(8,128)S(1)}, f32[16,128,128]{2,1,0:T(8,128)}, u32[]{:S(2)}) copy-start(f32[16,128,128]{2,1,0:T(8,128)} %potential.3) | copy-start | bytes 3145732
  22.7 7.7 %copy-start.8 = (s32[2,16,128]{2,1,0:T(8,128)S(1)}, s32[2,16,128]{2,1,0:T(8,128)}, u32[]{:S(2)}) copy-start(s32[2,16,128]{2,1,0:T(8,128)} %param.11) | copy-start | bytes 49156
  23.8 10.7 %collective-permute-start.1 = (f32[7,128,128]{2,1,0:T(8,128)}, f32[7,128,128]{2,1,0:T(8,128)}, u32[]{:S(2)}, u32[]{:S(2)}) collective-permute-start(f32[7,128,128]{2,1,0:T(8,128)} %get-tuple-element.53), channel_id=1, source_target_pairs={{1,0},{2,1},{3,2},{4,3},{5,4},{6,5},{7,6},{9,8},{10,9},{11,10},{12... | collective-permute-start | bytes 1376264 | tf_op jit(solution)/shard_map/owner/ppermute | solution.py:391
  26.6 8.8 %collective-permute-start = (f32[7,128,128]{2,1,0:T(8,128)}, f32[7,128,128]{2,1,0:T(8,128)}, u32[]{:S(2)}, u32[]{:S(2)}) collective-permute-start(f32[7,128,128]{2,1,0:T(8,128)} %get-tuple-element.54), channel_id=1, source_target_pairs={{0,1},{1,2},{2,3},{3,4},{4,5},{5,6},{6,7},{8,9},{9,10},{10,11},{11... | collective-permute-start | bytes 1376264 | tf_op jit(solution)/shard_map/owner/ppermute | solution.py:391
  29.8 5.6 %copy-start.2 = (f32[16,128,128]{2,1,0:T(8,128)S(1)}, f32[16,128,128]{2,1,0:T(8,128)}, u32[]{:S(2)}) copy-start(f32[16,128,128]{2,1,0:T(8,128)} %potential.3) | copy-start | bytes 3145732
  29.8 5.6 %copy-start.7 = (f32[128,128]{1,0:T(8,128)S(1)}, f32[128,128]{1,0:T(8,128)}, u32[]{:S(2)}) copy-start(f32[128,128]{1,0:T(8,128)} %constant.29.clone.line) | copy-start | bytes 196612
  39.3 1.0 copy-start.3
  40.3 49.5 %copy-start.6 = (f32[5,128,128]{2,1,0:T(8,128)S(1)}, f32[5,128,128]{2,1,0:T(8,128)}, u32[]{:S(2)}) copy-start(f32[5,128,128]{2,1,0:T(8,128)} %constant.30.clone.blocks) | copy-start | bytes 983044
  74.4 23.4 %collective-permute-start.2 = (f32[14,64,128]{2,1,0:T(8,128)}, f32[14,64,128]{2,1,0:T(8,128)S(1)}, u32[]{:S(2)}, u32[]{:S(2)}) collective-permute-start(f32[14,64,128]{2,1,0:T(8,128)} %get-tuple-element.40), channel_id=1, source_target_pairs={{8,0},{16,8},{24,16},{32,24},{40,32},{48,40},{56,48},{64,56},{72,6... | collective-permute-start | bytes 1376264 | tf_op jit(solution)/shard_map/halo/ppermute | solution.py:391
  75.7 22.1 %collective-permute-start.3 = (f32[14,64,128]{2,1,0:T(8,128)}, f32[14,64,128]{2,1,0:T(8,128)S(1)}, u32[]{:S(2)}, u32[]{:S(2)}) collective-permute-start(f32[14,64,128]{2,1,0:T(8,128)} %get-tuple-element.41), channel_id=1, source_target_pairs={{0,8},{8,16},{16,24},{24,32},{32,40},{40,48},{48,56},{56,64},{64,7... | collective-permute-start | bytes 1376264 | tf_op jit(solution)/shard_map/halo/ppermute | solution.py:391
  82.9 14.8 %collective-permute-start.4 = (f32[14,64,128]{2,1,0:T(8,128)}, f32[14,64,128]{2,1,0:T(8,128)S(1)}, u32[]{:S(2)}, u32[]{:S(2)}) collective-permute-start(f32[14,64,128]{2,1,0:T(8,128)} %get-tuple-element.42), channel_id=1, source_target_pairs={{1,0},{2,1},{3,2},{4,3},{5,4},{6,5},{7,6},{9,8},{10,9},{11,10},{12... | collective-permute-start | bytes 1376264 | tf_op jit(solution)/shard_map/halo/ppermute | solution.py:391
  88.3 9.4 %collective-permute-start.5 = (f32[7,64,128]{2,1,0:T(8,128)}, f32[7,64,128]{2,1,0:T(8,128)S(1)}, u32[]{:S(2)}, u32[]{:S(2)}) collective-permute-start(f32[7,64,128]{2,1,0:T(8,128)} %get-tuple-element.43), channel_id=1, source_target_pairs={{128,0},{256,128},{384,256},{129,1},{257,129},{385,257},{130,2},{2... | collective-permute-start | bytes 688136 | tf_op jit(solution)/shard_map/halo/ppermute | solution.py:391
  89.8 7.9 %copy-start.4 = (bf16[384,512]{1,0:T(8,128)(2,1)S(1)}, bf16[384,512]{1,0:T(8,128)(2,1)}, u32[]{:S(2)}) copy-start(bf16[384,512]{1,0:T(8,128)(2,1)} %constant.32.clone.low) | copy-start | bytes 1179652
  89.8 7.9 %copy-start.5 = (bf16[384,512]{1,0:T(8,128)(2,1)S(1)}, bf16[384,512]{1,0:T(8,128)(2,1)}, u32[]{:S(2)}) copy-start(bf16[384,512]{1,0:T(8,128)(2,1)} %constant.31.clone.high) | copy-start | bytes 1179652
  194.5 12.7 %all-to-all-start.6 = ((f32[8,1,128]{2,1,0:T(1,128)}), f32[8,1,128]{2,1,0:T(1,128)S(1)}, u32[]{:S(2)}, u32[]{:S(2)}) async-start(f32[8,1,128]{2,1,0:T(1,128)} %bitcast.20), calls=%async_computation.6 | async-start | bytes 8192 | tf_op jit(solution)/shard_map/rms/all_to_all | solution.py:381
  208.6 0.5 copy-start.9
